TPU v7x, 32 devices: a whole 2x2x4 slice. The times are simulated.
32 devices in a mesh: groups: 2 (over y), slab: 4 (over z), angle: 4 (over x, core).
Axes of the slice: x: 2, y: 2, z: 4, core: 2. Of those that a mesh axis runs over, the one named last changes fastest.
Arguments:
- activity: bfloat16 [12288, 128], P(('groups', 'slab')), parts along dimension 0, may hold values from 0.19921875 to 5
- sensitivity: float32 [12288], P(('groups', 'slab')), parts along dimension 0, may hold values from 8 to 64
- system_tiles: bfloat16 [8, 4, 86, 128, 128], P(('groups', 'slab'), 'angle'), parts along dimension 0, may hold values from 1.5616417e-05 to 0.0078125
- tile_voxel: int32 [8, 4, 86], P(('groups', 'slab'), 'angle'), parts along dimension 0, may hold values from 0 to 11, as said below
- tile_line: int32 [8, 4, 86], P(('groups', 'slab'), 'angle'), parts along dimension 0, may hold values from 0 to 8, as said below
- oblique_rows: int32 [8, 4, 2], P(('groups', 'slab'), 'angle'), parts along dimension 0, may hold values from 0 to 3, as said below
- counts: int32 [8, 4, 512, 128], P(('groups', 'slab'), 'angle'), parts along dimension 0, may hold values from 0 to 11
- background: bfloat16 [8, 4, 512, 128], P(('groups', 'slab'), 'angle'), parts along dimension 0, may hold values from 0.5 to 4
Outputs:
- updated: bfloat16 [12288, 128], P(('groups', 'slab')), parts along dimension 0
There are 2 independent parts, one for each index of `groups`. A program takes and returns all parts, laid end to end along the dimension named above; each array names one. Nothing has to cross between parts.
Inputs may be any that keep to these rules, and one draw needn't show every extreme that they name: On each slab and angle the used slots come first; an unused slot has tile_line 8 and tile_voxel 0. Used slots of one slab and angle name distinct pairs of voxel block and local LOR block, sorted by voxel block then LOR block. Every draw has a slab and angle with all 86 slots used. `tile_line`: see tile_voxel; the value 8 marks an unused slot. `oblique_rows`: the 2 entries of one slab and angle are distinct.
All inputs are finite; a program needn't handle non-finite values.
Results may differ from a plain program's by a relative error of at most 0.0022.
Values may be sent and summed in bfloat16 or wider, within the bound.
No kernel may reach another device: no remote copies, remote signals or barrier semaphores. Data moves between devices by JAX's collectives and lax.ppermute only.
A program may use at most 64 MiB of HBM per device.

v0:
```python
import jax
import jax.numpy as jnp
from jax import lax
from jax.sharding import PartitionSpec as P


def with_halo(block, sides, width):
    for axis, dim in sides:
        count = lax.axis_size(axis)
        forward = [(i, i + 1) for i in range(count - 1)]
        backward = [(target, source) for source, target in forward]
        low = lax.ppermute(
            lax.slice_in_dim(block, block.shape[dim] - width, None, axis=dim), axis, forward
        )
        high = lax.ppermute(lax.slice_in_dim(block, 0, width, axis=dim), axis, backward)
        block = jnp.concatenate([low, block, high], axis=dim)
    return block


def body(
    activity, sensitivity, system_tiles, tile_voxel, tile_line, oblique_rows, counts, background
):
    highest = lax.Precision.HIGHEST
    block_size = system_tiles.shape[-1]
    frames = activity.shape[1]
    voxel_blocks = activity.shape[0] // block_size
    own_blocks = counts.shape[2] // block_size
    oblique_count = oblique_rows.shape[-1]
    local_blocks = own_blocks + 2 * oblique_count
    tiles_here = system_tiles[0, 0]
    voxel_index = tile_voxel[0, 0]
    line_index = tile_line[0, 0]
    oblique_table = oblique_rows[0, 0]
    blocks = activity.reshape(voxel_blocks, block_size, frames)
    gathered = jnp.take(blocks, voxel_index, axis=0)
    per_tile = lax.dot_general(
        tiles_here, gathered, (((1,), (1,)), ((0,), (0,))), preferred_element_type=jnp.float32
    )
    partial_value = (
        jnp.zeros((local_blocks + 1, block_size, frames), jnp.float32)
        .at[line_index]
        .add(per_tile)[:local_blocks]
    )
    own_part = partial_value[:own_blocks]
    edge_parts = partial_value[own_blocks:]
    padded = with_halo(edge_parts.astype(jnp.bfloat16), (("slab", 0),), oblique_count).astype(
        edge_parts.dtype
    )
    from_left = padded[:oblique_count]
    from_right = padded[3 * oblique_count :]
    oblique_select = (
        oblique_table[:, None] == jnp.arange(own_blocks, dtype=jnp.int32)[None, :]
    ).astype(jnp.float32)
    projection = own_part + jnp.einsum(
        "jo,jlf->olf", oblique_select, from_left + from_right, precision=highest
    )
    measured = counts[0, 0].reshape(own_blocks, block_size, frames).astype(jnp.float32)
    additive = background[0, 0].reshape(own_blocks, block_size, frames).astype(jnp.float32)
    ratios = (measured / (projection + additive)).astype(jnp.bfloat16)
    oblique_ratio = jnp.take(ratios, oblique_table, axis=0)
    beside_all = with_halo(oblique_ratio, (("slab", 0),), oblique_count)
    local_ratio = jnp.concatenate(
        [ratios, beside_all[:oblique_count], beside_all[2 * oblique_count :]], axis=0
    )
    clamped = jnp.minimum(line_index, local_blocks - 1)
    picked = jnp.take(local_ratio, clamped, axis=0)
    live_slot = line_index < local_blocks
    picked = jnp.where(live_slot[:, None, None], picked, jnp.zeros_like(picked))
    per_voxel = lax.dot_general(
        tiles_here, picked, (((2,), (1,)), ((0,), (0,))), preferred_element_type=jnp.float32
    )
    back_local = (
        jnp.zeros((voxel_blocks, block_size, frames), jnp.float32).at[voxel_index].add(per_voxel)
    )
    back_local = back_local.reshape(voxel_blocks * block_size, frames)
    back_share = lax.psum_scatter(back_local, "angle", scatter_dimension=0, tiled=True)
    row_count = back_share.shape[0]
    row_start = lax.axis_index("angle") * row_count
    image_rows = lax.dynamic_slice_in_dim(activity, row_start, row_count, 0)
    sens_rows = lax.dynamic_slice_in_dim(sensitivity, row_start, row_count, 0)
    new_rows = (image_rows.astype(jnp.float32) * back_share / sens_rows[:, None]).astype(
        jnp.bfloat16
    )
    updated = lax.all_gather(new_rows, "angle", axis=0, tiled=True)
    return updated


def solution(mesh):
    placed = (
        P(("groups", "slab"), None),
        P(("groups", "slab")),
        P(("groups", "slab"), "angle", None, None, None),
        P(("groups", "slab"), "angle", None),
        P(("groups", "slab"), "angle", None),
        P(("groups", "slab"), "angle", None),
        P(("groups", "slab"), "angle", None, None),
        P(("groups", "slab"), "angle", None, None),
    )
    return jax.shard_map(
        body, mesh=mesh, in_specs=placed, out_specs=P(("groups", "slab"), None), check_vma=False
    )
```

profile of v0, /device:TPU:0, one launch (start us, length us, event | category | flops | bytes accessed | tf_op | source)
XLA Modules:
  0.0 133.2 jit_solution(13367799499831912926)
XLA Ops:
  6.5 0.8 fusion.31
  7.3 0.7 compare_and_fusion.1
  8.1 3.6 %gather_fusion = bf16[86,128,128]{2,1,0:T(8,128)(2,1)} fusion(bf16[12,128,128]{2,1,0:T(8,128)(2,1)} %bitcast.47, s32[1024]{0:T(1024)S(1)} %pad_clamp_fusion.2), kind=kCustom, calls=%fused_computation | custom fusion | bytes 5636440 | tf_op jit(solution)/shard_map/jit(_take)/gather | solution.py:35
  11.7 5.4 %fusion.10 = f32[86,128,128]{1,2,0:T(8,128)} fusion(bf16[1,1,86,128,128]{4,3,2,1,0:T(8,128)(2,1)S(1)} %copy-done, bf16[86,128,128]{2,1,0:T(8,128)(2,1)} %gather_fusion, pred[86]{0:T(512)(128)(4,1)S(1)} %compare_and_fusion.1), kind=kOutput, calls=%fused_computation.15 | convolution fusion | flops 362119168 | bytes 11272278 | tf_op jit(solution)/shard_map/dot_general | solution.py:36
  17.1 6.3 %copy.27 = f32[86,128,128]{2,1,0:T(8,128)} copy(f32[86,128,128]{1,2,0:T(8,128)} %fusion.10) | data formatting | bytes 11272192 | tf_op jit(solution)/shard_map/dot_general | solution.py:36
  23.4 0.5 fusion.34
  24.0 0.0 copy-start.2
  24.0 12.7 %scatter_fusion = f32[9,128,128]{2,1,0:T(8,128)S(1)} fusion(f32[9,128,128]{2,1,0:T(8,128)S(1)} %broadcast_in_dim.53, s32[86]{0:T(128)S(1)} %get-tuple-element.8, f32[86,128,128]{2,1,0:T(8,128)} %copy.27), kind=kCustom, calls=%fused_computation.3 | custom fusion | flops 1409024 | bytes 16908632 | tf_op jit(solution)/shard_map/scatter-add | solution.py:42
  36.7 4.9 %collective-permute-start = (bf16[2,128,128]{2,1,0:T(8,128)(2,1)S(1)}, bf16[2,128,128]{2,1,0:T(8,128)(2,1)S(1)}, u32[]{:S(2)}, u32[]{:S(2)}) collective-permute-start(bf16[2,128,128]{2,1,0:T(8,128)(2,1)S(1)} %get-tuple-element.5), channel_id=1, source_target_pairs={{0,4},{4,8},{8,12},{1,5},{5,9},{9,13},{2,6},{6,10},{10,14},{3,7},{... | collective-permute-start | bytes 196616 | tf_op jit(solution)/shard_map/ppermute | solution.py:12
  41.7 1.3 collective-permute-start.1
  43.0 0.5 compare_and_fusion
  43.6 1.0 convert_element_type.27
  44.5 3.3 %collective-permute-done.1 = bf16[2,128,128]{2,1,0:T(8,128)(2,1)S(1)} collective-permute-done((bf16[2,128,128]{2,1,0:T(8,128)(2,1)S(1)}, bf16[2,128,128]{2,1,0:T(8,128)(2,1)S(1)}, u32[]{:S(2)}, u32[]{:S(2)}) %collective-permute-start.1) | collective-permute-done | bytes 65568 | tf_op jit(solution)/shard_map/ppermute | solution.py:15
  47.9 0.5 fusion.26
  48.4 0.1 fusion.25
  48.5 0.6 gather_fusion.1
  49.0 0.7 broadcast_select_fusion
  49.7 3.5 %collective-permute-start.2 = (bf16[2,128,128]{2,1,0:T(8,128)(2,1)S(1)}, bf16[2,128,128]{2,1,0:T(8,128)(2,1)S(1)}, u32[]{:S(2)}, u32[]{:S(2)}) collective-permute-start(bf16[2,128,128]{2,1,0:T(8,128)(2,1)S(1)} %broadcast_select_fusion), channel_id=1, source_target_pairs={{0,4},{4,8},{8,12},{1,5},{5,9},{9,13},{2,6},{6,10},{10,14},{3,7},{... | collective-permute-start | bytes 196616 | tf_op jit(solution)/shard_map/ppermute | solution.py:12
  53.2 1.3 collective-permute-start.3
  54.5 0.7 pad_clamp_fusion
  55.2 4.2 %collective-permute-done.3 = bf16[2,128,128]{2,1,0:T(8,128)(2,1)S(1)} collective-permute-done((bf16[2,128,128]{2,1,0:T(8,128)(2,1)S(1)}, bf16[2,128,128]{2,1,0:T(8,128)(2,1)S(1)}, u32[]{:S(2)}, u32[]{:S(2)}) %collective-permute-start.3) | collective-permute-done | bytes 65568 | tf_op jit(solution)/shard_map/ppermute | solution.py:15
  59.4 2.6 %gather_fusion.2 = bf16[86,128,128]{2,1,0:T(8,128)(2,1)} fusion(bf16[8,128,128]{2,1,0:T(8,128)(2,1)S(1)} %pad_maximum_fusion, s32[1024]{0:T(1024)S(1)} %pad_clamp_fusion), kind=kCustom, calls=%fused_computation.2 | custom fusion | bytes 5636440 | tf_op jit(solution)/shard_map/jit(_take)/gather | solution.py:66
  62.0 6.5 %fusion.15 = f32[86,128,128]{1,2,0:T(8,128)} fusion(bf16[1,1,86,128,128]{4,3,2,1,0:T(8,128)(2,1)S(1)} %copy-done, bf16[86,128,128]{2,1,0:T(8,128)(2,1)} %gather_fusion.2, pred[86]{0:T(512)(128)(4,1)S(1)} %compare_and_fusion.2, pred[86]{0:T(512)(128)(4,1)S(1)} %compare_bitcast_fusion), kind=kOutput, calls=%fused_computation.16 | convolution fusion | flops 363528192 | bytes 11272364 | tf_op jit(solution)/shard_map/dot_general | solution.py:69
  68.5 6.2 %copy.31 = f32[86,128,128]{2,1,0:T(8,128)} copy(f32[86,128,128]{1,2,0:T(8,128)} %fusion.15) | data formatting | bytes 11272192 | tf_op jit(solution)/shard_map/dot_general | solution.py:69
  74.7 1.0 broadcast_in_dim.50
  75.7 20.3 %scatter_fusion.1 = f32[12,128,128]{2,1,0:T(8,128)} fusion(f32[12,128,128]{2,1,0:T(8,128)} %broadcast_in_dim.50, s32[86]{0:T(128)S(1)} %fusion.31, f32[86,128,128]{2,1,0:T(8,128)} %copy.31), kind=kCustom, calls=%fused_computation.4 | custom fusion | flops 1409024 | bytes 16908632 | tf_op jit(solution)/shard_map/scatter-add | solution.py:73
  96.0 0.0 reduce-scatter.2.cloned.1.call-update
  96.0 0.8 dynamic_slice.7
  96.8 21.6 %reduce-scatter.2.cloned.1.call-done = f32[384,128]{1,0:T(8,128)} async-done(((f32[1536,128]{1,0:T(8,128)}), f32[384,128]{1,0:T(8,128)}) %reduce-scatter.2.cloned.1.call-update) | async-done | bytes 196624 | tf_op jit(solution)/shard_map/reduce_scatter | solution.py:76
  118.4 1.1 divide_convert_fusion
  119.5 6.1 %all_gather.3 = bf16[1536,128]{1,0:T(8,128)(2,1)S(1)} all-gather(bf16[384,128]{1,0:T(8,128)(2,1)S(1)} %divide_convert_fusion), channel_id=1, replica_groups=mesh['groups'=2,'slab'=4,'angle'=4] {'angle'}, dimensions={0}, use_global_device_ids=true | all-gather | bytes 491520 | tf_op jit(solution)/shard_map/all_gather | solution.py:84
  125.6 0.7 copy.42
  (21 shorter events, 0.2 us)
Async XLA Ops:
  6.5 5.1 %copy-start = (bf16[1,1,86,128,128]{4,3,2,1,0:T(8,128)(2,1)S(1)}, bf16[1,1,86,128,128]{4,3,2,1,0:T(8,128)(2,1)}, u32[]{:S(2)}) copy-start(bf16[1,1,86,128,128]{4,3,2,1,0:T(8,128)(2,1)} %param.10) | copy-start | bytes 8454148
  6.5 111.8 %reduce-scatter.2.cloned.1.call-start = ((), (), s32[]{:S(2)}) async-start(), calls=%async_computation.1 | async-start | bytes 983040 | tf_op jit(solution)/shard_map/reduce_scatter | solution.py:76
  17.1 6.3 %copy-start.3 = (s32[1,1,86]{2,1,0:T(1,128)S(1)}, s32[1,1,86]{2,1,0:T(1,128)}, u32[]{:S(2)}) copy-start(s32[1,1,86]{2,1,0:T(1,128)} %param.12) | copy-start | bytes 1036
  24.0 19.0 %copy-start.2 = (s32[1,1,2]{2,1,0:T(1,128)S(1)}, s32[1,1,2]{2,1,0:T(1,128)}, u32[]{:S(2)}) copy-start(s32[1,1,2]{2,1,0:T(1,128)} %param.13) | copy-start | bytes 28
  36.6 11.7 %copy-start.1 = (bf16[1,1,512,128]{3,2,1,0:T(8,128)(2,1)S(1)}, bf16[1,1,512,128]{3,2,1,0:T(8,128)(2,1)}, u32[]{:S(2)}) copy-start(bf16[1,1,512,128]{3,2,1,0:T(8,128)(2,1)} %param.15) | copy-start | bytes 393220
  36.7 7.8 %collective-permute-start = (bf16[2,128,128]{2,1,0:T(8,128)(2,1)S(1)}, bf16[2,128,128]{2,1,0:T(8,128)(2,1)S(1)}, u32[]{:S(2)}, u32[]{:S(2)}) collective-permute-start(bf16[2,128,128]{2,1,0:T(8,128)(2,1)S(1)} %get-tuple-element.5), channel_id=1, source_target_pairs={{0,4},{4,8},{8,12},{1,5},{5,9},{9,13},{2,6},{6,10},{10,14},{3,7},{... | collective-permute-start | bytes 196616 | tf_op jit(solution)/shard_map/ppermute | solution.py:12
  41.7 6.2 %collective-permute-start.1 = (bf16[2,128,128]{2,1,0:T(8,128)(2,1)S(1)}, bf16[2,128,128]{2,1,0:T(8,128)(2,1)S(1)}, u32[]{:S(2)}, u32[]{:S(2)}) collective-permute-start(bf16[2,128,128]{2,1,0:T(8,128)(2,1)S(1)} %get-tuple-element.6), channel_id=1, source_target_pairs={{4,0},{8,4},{12,8},{5,1},{9,5},{13,9},{6,2},{10,6},{14,10},{7,3},{... | collective-permute-start | bytes 196616 | tf_op jit(solution)/shard_map/ppermute | solution.py:15
  49.7 5.4 %collective-permute-start.2 = (bf16[2,128,128]{2,1,0:T(8,128)(2,1)S(1)}, bf16[2,128,128]{2,1,0:T(8,128)(2,1)S(1)}, u32[]{:S(2)}, u32[]{:S(2)}) collective-permute-start(bf16[2,128,128]{2,1,0:T(8,128)(2,1)S(1)} %broadcast_select_fusion), channel_id=1, source_target_pairs={{0,4},{4,8},{8,12},{1,5},{5,9},{9,13},{2,6},{6,10},{10,14},{3,7},{... | collective-permute-start | bytes 196616 | tf_op jit(solution)/shard_map/ppermute | solution.py:12
  53.2 6.2 %collective-permute-start.3 = (bf16[2,128,128]{2,1,0:T(8,128)(2,1)S(1)}, bf16[2,128,128]{2,1,0:T(8,128)(2,1)S(1)}, u32[]{:S(2)}, u32[]{:S(2)}) collective-permute-start(bf16[2,128,128]{2,1,0:T(8,128)(2,1)S(1)} %broadcast_select_fusion), channel_id=1, source_target_pairs={{4,0},{8,4},{12,8},{5,1},{9,5},{13,9},{6,2},{10,6},{14,10},{7,3},{... | collective-permute-start | bytes 196616 | tf_op jit(solution)/shard_map/ppermute | solution.py:15
Sparse Core Ops, SparseCore 0:
  96.1 22.2 reduce-scatter.1
where the time goes:
time: 134 us; the launch traced here: 133 us
  other arithmetic  39.1 us (29%)
  waiting for transfers between devices  29.1 us (22%)
  local copies, waits for them, and re-layouts  21.8 us (16%)
  between operations  13.6 us (10%)
  matrix products  12.5 us (9%)
  starting transfers between devices  11 us (8%)
  blocking collectives  6.15 us (5%)
    reduce_scatter x1, waiting for transfers between devices, body(): lax.psum_scatter(back_local, 'angle', scatter_dimension=0, tiled=True)  21.6 us
    scatter-add x1, other arithmetic, body(): jnp.zeros((voxel_blocks, block_size, frames), jnp.float32).at[voxel_index]  20.3 us
    scatter-add x1, other arithmetic, body(): partial_value = jnp.zeros((local_blocks + 1, block_size, frames), jnp.flo...  12.7 us
    ppermute x2, starting transfers between devices, with_halo(): lax.ppermute(lax.slice_in_dim(block, block.shape[dim] - width, None, axis...  8.41 us
    ppermute x2, waiting for transfers between devices, with_halo(): lax.ppermute(lax.slice_in_dim(block, 0, width, axis=dim), axis, backward)  7.47 us
    dot_general x1, matrix products, body(): lax.dot_general(tiles_here, picked, (((2,), (1,)), ((0,), (0,))), preferr...  6.5 us
    dot_general x1, local copies, waits for them, and re-layouts, body(): lax.dot_general(tiles_here, gathered, (((1,), (1,)), ((0,), (0,))), prefe...  6.26 us
    dot_general x1, local copies, waits for them, and re-layouts, body(): lax.dot_general(tiles_here, picked, (((2,), (1,)), ((0,), (0,))), preferr...  6.24 us
  transfers between devices with their start and end apart: 5, of which 3 were waited for; matrix products, arithmetic and copies ran while one was open for 2% of the time, Pallas kernels for 0%

commit v1 on v0

v1 whole, which is shorter than its diff:
```python
import functools

import jax
import jax.numpy as jnp
from jax import lax
from jax.experimental import pallas as pl
from jax.experimental.pallas import tpu as pltpu
from jax.sharding import PartitionSpec as P

VMEM = pl.BlockSpec(memory_space=pltpu.VMEM)
SMEM = pl.BlockSpec(memory_space=pltpu.SMEM)
PART_SCALE = 256.0
CHIP_SCALE = 128.0


def params(**more):
    return pltpu.CompilerParams(vmem_limit_bytes=16 * 1024 * 1024, **more)


def index_tiles(voxel_ref, line_ref, slot_ref, blocks, lines):
    stride = lines + 1
    for n in range(blocks * stride):
        slot_ref[n] = -1
    for k in range(voxel_ref.shape[-1]):
        slot_ref[voxel_ref[k] * stride + line_ref[k]] = k


def tile_of(tiles_ref, slot_ref, voxel, line, lines):
    slot = slot_ref[voxel * (lines + 1) + line]
    tile = tiles_ref[jnp.maximum(slot, 0)]
    return jnp.where(slot >= 0, tile, jnp.zeros_like(tile))


def project(image_ref, tiles_ref, slot_ref, first, count, blocks, lines):
    weights = jnp.concatenate(
        [
            jnp.concatenate(
                [tile_of(tiles_ref, slot_ref, v, first + c, lines) for c in range(count)], axis=1
            )
            for v in range(blocks)
        ],
        axis=0,
    )
    return jnp.dot(image_ref[...], weights, preferred_element_type=jnp.float32)


def edge_kernel(
    blocks, own, lines, place_ref, voxel_ref, line_ref, activity_ref, tiles_ref,
    forth_ref, back_ref, image_ref, slot_ref,
):
    size = tiles_ref.shape[-1]
    width = (lines - own) // 2
    index_tiles(voxel_ref, line_ref, slot_ref, blocks, lines)
    for v in range(blocks):
        image_ref[:, v * size : (v + 1) * size] = activity_ref[v * size : (v + 1) * size, :].T
    odd = place_ref[0]
    for out_ref, first in (
        (forth_ref, own + width * (1 - odd)),
        (back_ref, own + width * odd),
    ):
        sums = project(image_ref, tiles_ref, slot_ref, first, width, blocks, lines)
        for c in range(width):
            out_ref[c] = sums[:, c * size : (c + 1) * size].astype(out_ref.dtype)


def own_kernel(
    blocks, own, lines, voxel_ref, line_ref, image_ref, tiles_ref, counts_ref, background_ref,
    base_ref, ratio_ref, slot_ref,
):
    size = tiles_ref.shape[-1]
    index_tiles(voxel_ref, line_ref, slot_ref, blocks, lines)
    for first in range(0, own, 2):
        sums = project(image_ref, tiles_ref, slot_ref, first, 2, blocks, lines)
        for c in range(2):
            o = first + c
            base = sums[:, c * size : (c + 1) * size].T + background_ref[o].astype(jnp.float32)
            base_ref[o] = base
            ratio_ref[o] = (counts_ref[o].astype(jnp.float32) / base).astype(ratio_ref.dtype)


def oblique_kernel(
    place_ref, rows_ref, forth_ref, back_ref, base_ref, counts_ref, out_ref,
):
    has_forth = place_ref[1] > 0
    has_back = place_ref[2] > 0
    for j in range(out_ref.shape[0]):
        row = rows_ref[j]
        forth = forth_ref[j].astype(jnp.float32)
        back = back_ref[j].astype(jnp.float32)
        extra = jnp.where(has_forth, forth, 0.0) + jnp.where(has_back, back, 0.0)
        total = base_ref[row] + extra.T
        out_ref[j] = (counts_ref[row].astype(jnp.float32) / total).astype(out_ref.dtype)


def back_project(ratios, tiles_ref, slot_ref, voxels, firsts, lines):
    rows = jnp.concatenate(
        [
            jnp.concatenate(
                [tile_of(tiles_ref, slot_ref, v, c, lines) for c in firsts], axis=1
            )
            for v in voxels
        ],
        axis=0,
    )
    return jnp.dot(rows, ratios, preferred_element_type=jnp.float32)


def own_back_kernel(
    blocks, own, lines, rows_ref, voxel_ref, line_ref, tiles_ref, ratio_ref, oblique_ref,
    out_ref, slot_ref, mixed_ref,
):
    size = tiles_ref.shape[-1]
    index_tiles(voxel_ref, line_ref, slot_ref, blocks, lines)
    mixed_ref[...] = ratio_ref[...]
    for j in range(oblique_ref.shape[0]):
        mixed_ref[rows_ref[j]] = oblique_ref[j]
    ratios = mixed_ref[...].reshape(own * size, -1)
    out_ref[...] = back_project(
        ratios, tiles_ref, slot_ref, range(blocks), range(own), lines
    ).reshape(out_ref.shape)


def edge_back_kernel(
    blocks, own, lines, other, scale, place_ref, voxel_ref, line_ref, tiles_ref, forth_ref,
    back_ref, own_ref, out_ref, slot_ref,
):
    size = tiles_ref.shape[-1]
    width = (lines - own) // 2
    half = blocks // 2
    index_tiles(voxel_ref, line_ref, slot_ref, blocks, lines)
    odd = place_ref[0]
    forth = jnp.where(place_ref[1] > 0, forth_ref[...], jnp.zeros_like(forth_ref))
    back = jnp.where(place_ref[2] > 0, back_ref[...], jnp.zeros_like(back_ref))
    ratios = jnp.concatenate([forth, back], axis=0).reshape(2 * width * size, -1)
    firsts = [own + width * odd + c for c in range(width)]
    firsts += [own + width * (1 - odd) + c for c in range(width)]
    start = (1 - odd if other else odd) * half
    sums = back_project(
        ratios, tiles_ref, slot_ref, [start + n for n in range(half)], firsts, lines
    ).reshape(half, size, -1)
    total = (sums + own_ref[pl.ds(start, half)]) * scale
    out_ref[...] = total.astype(out_ref.dtype)


def body(
    slabs, angles, activity, sensitivity, system_tiles, tile_voxel, tile_line, oblique_rows,
    counts, background,
):
    size = system_tiles.shape[-1]
    frames = activity.shape[1]
    blocks = activity.shape[0] // size
    own = counts.shape[2] // size
    width = oblique_rows.shape[-1]
    lines = own + 2 * width
    half = blocks // 2
    tiles = system_tiles[0, 0]
    voxel = tile_voxel[0, 0]
    line = tile_line[0, 0]
    rows = oblique_rows[0, 0]
    measured = counts[0, 0].reshape(own, size, frames)
    additive = background[0, 0].reshape(own, size, frames)

    slab = lax.axis_index("slab")
    odd = lax.axis_index("angle") % 2
    left = slab > 0
    right = slab < slabs - 1
    place = jnp.stack(
        [
            odd,
            jnp.where(odd == 0, left, right).astype(jnp.int32),
            jnp.where(odd == 0, right, left).astype(jnp.int32),
        ]
    ).astype(jnp.int32)

    forth = []
    for s in range(slabs):
        for a in range(angles):
            t = s + 1 if a % 2 == 0 else s - 1
            here = s * angles + a
            there = t * angles + a if 0 <= t < slabs else s * angles + (a ^ 1)
            forth.append((here, there))
    back = [(there, here) for here, there in forth]
    both = ("slab", "angle")
    slots = pltpu.SMEM((blocks * (lines + 1),), jnp.int32)

    def block_out(count, dtype, first=size, second=frames):
        return jax.ShapeDtypeStruct((count, first, second), dtype)

    edge_forth, edge_back, image = pl.pallas_call(
        functools.partial(edge_kernel, blocks, own, lines),
        out_shape=(
            block_out(width, jnp.bfloat16, frames, size),
            block_out(width, jnp.bfloat16, frames, size),
            jax.ShapeDtypeStruct((frames, blocks * size), jnp.bfloat16),
        ),
        in_specs=[SMEM, SMEM, SMEM, VMEM, VMEM],
        out_specs=(VMEM, VMEM, VMEM),
        scratch_shapes=[slots],
        compiler_params=params(),
        name="edge_partials",
    )(place, voxel, line, activity, tiles)
    got_forth = lax.ppermute(edge_forth, both, forth)
    got_back = lax.ppermute(edge_back, both, back)
    base, ratio = pl.pallas_call(
        functools.partial(own_kernel, blocks, own, lines),
        out_shape=(block_out(own, jnp.float32), block_out(own, jnp.bfloat16)),
        in_specs=[SMEM, SMEM, VMEM, VMEM, VMEM, VMEM],
        out_specs=(VMEM, VMEM),
        scratch_shapes=[slots],
        compiler_params=params(),
        name="own_partials",
    )(voxel, line, image, tiles, measured, additive)
    oblique = pl.pallas_call(
        oblique_kernel,
        out_shape=block_out(width, jnp.bfloat16),
        in_specs=[SMEM, SMEM, VMEM, VMEM, VMEM, VMEM],
        out_specs=VMEM,
        compiler_params=params(),
        name="oblique_ratios",
    )(place, rows, got_forth, got_back, base, measured)
    beside_forth = lax.ppermute(oblique, both, forth)
    beside_back = lax.ppermute(oblique, both, back)
    own_back = pl.pallas_call(
        functools.partial(own_back_kernel, blocks, own, lines),
        out_shape=block_out(blocks, jnp.float32),
        in_specs=[SMEM, SMEM, SMEM, VMEM, VMEM, VMEM],
        out_specs=VMEM,
        scratch_shapes=[slots, pltpu.VMEM((own, size, frames), jnp.bfloat16)],
        compiler_params=params(),
        name="own_back",
    )(rows, voxel, line, tiles, ratio, oblique)

    def edge_half(other, scale, dtype, name):
        return pl.pallas_call(
            functools.partial(edge_back_kernel, blocks, own, lines, other, scale),
            out_shape=block_out(half, dtype),
            in_specs=[SMEM, SMEM, SMEM, VMEM, VMEM, VMEM, VMEM],
            out_specs=VMEM,
            scratch_shapes=[slots],
            compiler_params=params(),
            name=name,
        )(place, voxel, line, tiles, beside_forth, beside_back, own_back)

    half_rows = half * size
    mine = odd * half_rows
    image_rows = lax.dynamic_slice_in_dim(activity, mine, half_rows, 0).astype(jnp.float32)
    sens_rows = lax.dynamic_slice_in_dim(sensitivity, mine, half_rows, 0)
    pairs = [(a, a ^ 1) for a in range(angles)]
    sent = edge_half(True, PART_SCALE, jnp.float32, "edge_back_sent").astype(jnp.float16)
    got = lax.ppermute(sent, "angle", pairs)
    kept = edge_half(False, 1.0, jnp.float32, "edge_back_kept")
    chip = kept + got.astype(jnp.float32) * (1.0 / PART_SCALE)
    if angles == 4:
        chip = (chip * CHIP_SCALE).astype(jnp.float16)
        beside = lax.ppermute(chip, "angle", [(a, a ^ 2) for a in range(angles)])
        total = (chip.astype(jnp.float32) + beside.astype(jnp.float32)) * (1.0 / CHIP_SCALE)
    else:
        groups = [list(range(odd_one, angles, 2)) for odd_one in range(2)]
        total = lax.psum(chip, "angle", axis_index_groups=groups)
    total = total.reshape(half_rows, frames)
    new_rows = (image_rows * total / sens_rows[:, None]).astype(jnp.bfloat16)
    other_rows = lax.ppermute(new_rows, "angle", pairs)
    low = jnp.where(odd == 0, new_rows, other_rows)
    high = jnp.where(odd == 0, other_rows, new_rows)
    return jnp.concatenate([low, high], axis=0)


def solution(mesh):
    placed = (
        P(("groups", "slab"), None),
        P(("groups", "slab")),
        P(("groups", "slab"), "angle", None, None, None),
        P(("groups", "slab"), "angle", None),
        P(("groups", "slab"), "angle", None),
        P(("groups", "slab"), "angle", None),
        P(("groups", "slab"), "angle", None, None),
        P(("groups", "slab"), "angle", None, None),
    )
    return jax.shard_map(
        functools.partial(body, mesh.shape["slab"], mesh.shape["angle"]),
        mesh=mesh,
        in_specs=placed,
        out_specs=P(("groups", "slab"), None),
        check_vma=False,
    )
```

time: 134 us -> 31.9 us (0.24)
  other arithmetic: 39.1 us -> 1.23 us
  local copies, waits for them, and re-layouts: 21.8 us -> 4.21 us
  waiting for transfers between devices: 29.1 us -> 13 us
  between operations: 13.6 us -> 0.15 us
  matrix products: 12.5 us -> 0 us
  Pallas kernels: 0 us -> 6.77 us
  blocking collectives: 6.15 us -> 0 us
  starting transfers between devices: 11 us -> 6.34 us
    scatter-add x2 -> x0, other arithmetic: 32.9 us -> none  [the longest x1 20.3 us: body(): jnp.zeros((voxel_blocks, block_size, frames), jnp.float32).at[voxel_index]]
    reduce_scatter x1 -> x0, waiting for transfers between devices: 21.6 us -> none  [body(): lax.psum_scatter(back_local, 'angle', scatter_dimension=0, tiled=True)]
    dot_general x2 -> x0, local copies, waits for them, and re-layouts: 12.5 us -> none  [the longest x1 6.26 us: body(): lax.dot_general(tiles_here, gathered, (((1,), (1,)), ((0,), (0,))), prefe...]
    dot_general x3 -> x0, matrix products: 12.5 us -> none  [the longest x1 6.5 us: body(): lax.dot_general(tiles_here, picked, (((2,), (1,)), ((0,), (0,))), preferr...]
    pallas_call x0 -> x6, Pallas kernels: none -> 6.77 us  [the longest x2 2.22 us: edge_half(): pl.pallas_call(functools.partial(edge_back_kernel, blocks, own, lines, ot...]
    gather x3 -> x0, local copies, waits for them, and re-layouts: 6.77 us -> none  [the longest x1 3.61 us: body(): gathered = jnp.take(blocks, voxel_index, axis=0)]
    all_gather x1 -> x0, blocking collectives: 6.15 us -> none  [body(): updated = lax.all_gather(new_rows, 'angle', axis=0, tiled=True)]
    ppermute x4 -> x7, waiting for transfers between devices: 7.48 us -> 13 us  [the longest x1 5.43 us: body(): beside = lax.ppermute(chip, 'angle', [(a, a ^ 2) for a in range(angles)])]
  transfers between devices with their start and end apart: 5 -> 7, of which waited for: 3 -> 7; matrix products, arithmetic and copies ran while one was open for 2% -> 0% of each run, Pallas kernels for 0% -> 12%
where the time goes in v1:
time: 31.9 us; the launch traced here: 31.7 us
  waiting for transfers between devices  13 us (41%)
  Pallas kernels  6.77 us (21%)
  starting transfers between devices  6.34 us (20%)
  local copies, waits for them, and re-layouts  4.21 us (13%)
  other arithmetic  1.23 us (4%)
    ppermute x1, waiting for transfers between devices, body(): beside = lax.ppermute(chip, 'angle', [(a, a ^ 2) for a in range(angles)])  5.43 us
    unnamed x22, local copies, waits for them, and re-layouts  4.13 us
    ppermute x1, starting transfers between devices, body(): got_forth = lax.ppermute(edge_forth, both, forth)  3.04 us
    ppermute x1, waiting for transfers between devices, body(): got_back = lax.ppermute(edge_back, both, back)  2.36 us
    ppermute x1, waiting for transfers between devices, body(): beside_back = lax.ppermute(oblique, both, back)  2.36 us
    pallas_call x2, Pallas kernels, edge_half(): pl.pallas_call(functools.partial(edge_back_kernel, blocks, own, lines, ot...  2.22 us
    ppermute x1, starting transfers between devices, body(): beside_forth = lax.ppermute(oblique, both, forth)  1.59 us
    ppermute x1, starting transfers between devices, body(): beside = lax.ppermute(chip, 'angle', [(a, a ^ 2) for a in range(angles)])  1.56 us
  transfers between devices with their start and end apart: 7, of which 7 were waited for; matrix products, arithmetic and copies ran while one was open for 0% of the time, Pallas kernels for 12%

profile of v1, /device:TPU:0, one launch (start us, length us, event | category | flops | bytes accessed | tf_op | source)
XLA Modules:
  0.0 31.7 jit_solution(16599205249452704050)
XLA Ops:
  0.0 0.1 pad_add_fusion.place_ref
  0.1 1.8 %copy-done = bf16[1,1,86,128,128]{4,3,2,1,0:T(8,128)(2,1)S(1)} copy-done((bf16[1,1,86,128,128]{4,3,2,1,0:T(8,128)(2,1)S(1)}, bf16[1,1,86,128,128]{4,3,2,1,0:T(8,128)(2,1)}, u32[]{:S(2)}) %copy-start) | copy-done | bytes 2818072
  1.9 1.0 %copy-done.3 = bf16[1536,128]{1,0:T(8,128)(2,1)S(1)} copy-done((bf16[1536,128]{1,0:T(8,128)(2,1)S(1)}, bf16[1536,128]{1,0:T(8,128)(2,1)}, u32[]{:S(2)}) %copy-start.3) | copy-done | bytes 393240
  2.9 0.7 %copy-done.6 = s32[1,1,86]{2,1,0:T(1,128)S(1)} copy-done((s32[1,1,86]{2,1,0:T(1,128)S(1)}, s32[1,1,86]{2,1,0:T(1,128)}, u32[]{:S(2)}) %copy-start.6) | copy-done | bytes 368
  3.5 0.7 %copy-done.8 = s32[1,1,86]{2,1,0:T(1,128)S(1)} copy-done((s32[1,1,86]{2,1,0:T(1,128)S(1)}, s32[1,1,86]{2,1,0:T(1,128)}, u32[]{:S(2)}) %copy-start.8) | copy-done | bytes 368
  4.2 1.3 %edge_partials.1 = (bf16[2,128,128]{2,1,0:T(8,128)(2,1)S(1)}, bf16[2,128,128]{2,1,0:T(8,128)(2,1)S(1)}, bf16[128,1536]{1,0:T(8,128)(2,1)S(1)}) custom-call(s32[3]{0:T(128)S(1)} %pad_add_fusion.place_ref, s32[86]{0:T(128)S(1)} %bitcast.23, s32[86]{0:T(128)S(1)} %bitcast.28, bf16[1536,128]{1,0:T(8,128)(2,1)S(1)} %copy-done.3, bf16[86,128,128]{2,1,0:T(8,128)(2,1)S(1)} %bitcast.15), custom_call_target="tpu_custom_call" | custom-call | tf_op jit(solution)/shard_map/edge_partials/pallas_call | solution.py:189
  5.5 3.0 %collective-permute-start = (bf16[2,128,128]{2,1,0:T(8,128)(2,1)S(1)}, bf16[2,128,128]{2,1,0:T(8,128)(2,1)S(1)}, u32[]{:S(2)}, u32[]{:S(2)}) collective-permute-start(bf16[2,128,128]{2,1,0:T(8,128)(2,1)S(1)} %get-tuple-element.10), channel_id=1, source_target_pairs={{0,4},{1,0},{2,6},{3,2},{4,8},{5,1},{6,10},{7,3},{8,12},{9,5},{10,... | collective-permute-start | bytes 196616 | tf_op jit(solution)/shard_map/ppermute | solution.py:202
  8.5 0.0 collective-permute-start.1
  8.6 1.3 %own_partials.1 = (f32[4,128,128]{2,1,0:T(8,128)S(1)}, bf16[4,128,128]{2,1,0:T(8,128)(2,1)S(1)}) custom-call(s32[86]{0:T(128)S(1)} %bitcast.24, s32[86]{0:T(128)S(1)} %bitcast.29, bf16[128,1536]{1,0:T(8,128)(2,1)S(1)} %get-tuple-element.12.image_ref, bf16[86,128,128]{2,1,0:T(8,128)(2,1)S(1)} %bitcast.16, s32[4,128,128]{2,1,0:T(8,128)S(1)} %bitcast.20, ...), custom_call_target="tpu_custom_call" | custom-call | tf_op jit(solution)/shard_map/own_partials/pallas_call | solution.py:204
  9.9 0.5 %collective-permute-done.forth_ref = bf16[2,128,128]{2,1,0:T(8,128)(2,1)S(1)} collective-permute-done((bf16[2,128,128]{2,1,0:T(8,128)(2,1)S(1)}, bf16[2,128,128]{2,1,0:T(8,128)(2,1)S(1)}, u32[]{:S(2)}, u32[]{:S(2)}) %collective-permute-start) | collective-permute-done | bytes 65568 | tf_op jit(solution)/shard_map/ppermute | solution.py:202
  10.4 2.4 %collective-permute-done.1.back_ref = bf16[2,128,128]{2,1,0:T(8,128)(2,1)S(1)} collective-permute-done((bf16[2,128,128]{2,1,0:T(8,128)(2,1)S(1)}, bf16[2,128,128]{2,1,0:T(8,128)(2,1)S(1)}, u32[]{:S(2)}, u32[]{:S(2)}) %collective-permute-start.1) | collective-permute-done | bytes 65568 | tf_op jit(solution)/shard_map/ppermute | solution.py:203
  12.8 0.7 %oblique_ratios.1.oblique_ref = bf16[2,128,128]{2,1,0:T(8,128)(2,1)S(1)} custom-call(s32[3]{0:T(128)S(1)} %pad_add_fusion.place_ref, s32[2]{0:T(128)S(1)} %bitcast.33, bf16[2,128,128]{2,1,0:T(8,128)(2,1)S(1)} %collective-permute-done.forth_ref, bf16[2,128,128]{2,1,0:T(8,128)(2,1)S(1)} %collective-permute-done.1.back_ref, ...), custom_call_target="tpu_custom_call" | custom-call | tf_op jit(solution)/shard_map/oblique_ratios/pallas_call | solution.py:213
  13.5 1.6 %collective-permute-start.2 = (bf16[2,128,128]{2,1,0:T(8,128)(2,1)S(1)}, bf16[2,128,128]{2,1,0:T(8,128)(2,1)S(1)}, u32[]{:S(2)}, u32[]{:S(2)}) collective-permute-start(bf16[2,128,128]{2,1,0:T(8,128)(2,1)S(1)} %oblique_ratios.1.oblique_ref), channel_id=1, source_target_pairs={{0,4},{1,0},{2,6},{3,2},{4,8},{5,1},{6,10},{7,3},{8,12},{9,5},{10,... | collective-permute-start | bytes 196616 | tf_op jit(solution)/shard_map/ppermute | solution.py:221
  15.0 0.0 collective-permute-start.3
  15.0 1.3 %own_back.1.own_ref = f32[12,128,128]{2,1,0:T(8,128)S(1)} custom-call(s32[2]{0:T(128)S(1)} %bitcast.34, s32[86]{0:T(128)S(1)} %bitcast.25, s32[86]{0:T(128)S(1)} %bitcast.30, bf16[86,128,128]{2,1,0:T(8,128)(2,1)S(1)} %bitcast.17, bf16[4,128,128]{2,1,0:T(8,128)(2,1)S(1)} %get-tuple-element.14.ratio_ref, bf16[2,128,128]{2,1,0:T(8,128)(2,1)S(1)} %oblique_ratios.1.oblique_ref), custom_call_target="tpu_custom_call" | custom-call | tf_op jit(solution)/shard_map/own_back/pallas_call | solution.py:223
  16.4 0.6 %collective-permute-done.2.forth_ref = bf16[2,128,128]{2,1,0:T(8,128)(2,1)S(1)} collective-permute-done((bf16[2,128,128]{2,1,0:T(8,128)(2,1)S(1)}, bf16[2,128,128]{2,1,0:T(8,128)(2,1)S(1)}, u32[]{:S(2)}, u32[]{:S(2)}) %collective-permute-start.2) | collective-permute-done | bytes 65568 | tf_op jit(solution)/shard_map/ppermute | solution.py:221
  17.0 2.4 %collective-permute-done.3.back_ref = bf16[2,128,128]{2,1,0:T(8,128)(2,1)S(1)} collective-permute-done((bf16[2,128,128]{2,1,0:T(8,128)(2,1)S(1)}, bf16[2,128,128]{2,1,0:T(8,128)(2,1)S(1)}, u32[]{:S(2)}, u32[]{:S(2)}) %collective-permute-start.3) | collective-permute-done | bytes 65568 | tf_op jit(solution)/shard_map/ppermute | solution.py:222
  19.3 1.1 %edge_back_sent.1 = f32[6,128,128]{2,1,0:T(8,128)S(1)} custom-call(s32[3]{0:T(128)S(1)} %pad_add_fusion.place_ref, s32[86]{0:T(128)S(1)} %bitcast.26, s32[86]{0:T(128)S(1)} %bitcast.31, bf16[86,128,128]{2,1,0:T(8,128)(2,1)S(1)} %bitcast.18, bf16[2,128,128]{2,1,0:T(8,128)(2,1)S(1)} %collective-permute-done.2.forth_ref, ...), custom_call_target="tpu_custom_call" | custom-call | tf_op jit(solution)/shard_map/edge_back_sent/pallas_call | solution.py:234
  20.4 0.0 copy-start.10
  20.5 0.0 copy-start.4
  20.5 0.1 collective-permute-start.4
  20.6 1.1 %edge_back_kept.1 = f32[6,128,128]{2,1,0:T(8,128)S(1)} custom-call(s32[3]{0:T(128)S(1)} %pad_add_fusion.place_ref, s32[86]{0:T(128)S(1)} %bitcast.27, s32[86]{0:T(128)S(1)} %bitcast.32, bf16[86,128,128]{2,1,0:T(8,128)(2,1)S(1)} %bitcast.19, bf16[2,128,128]{2,1,0:T(8,128)(2,1)S(1)} %collective-permute-done.2.forth_ref, ...), custom_call_target="tpu_custom_call" | custom-call | tf_op jit(solution)/shard_map/edge_back_kept/pallas_call | solution.py:234
  21.7 0.3 collective-permute-done.4
  22.0 0.1 multiply_convert_fusion
  22.1 1.6 %collective-permute-start.5 = (f16[6,128,128]{2,1,0:T(8,128)(2,1)S(1)}, f16[6,128,128]{2,1,0:T(8,128)(2,1)S(1)}, u32[]{:S(2)}, u32[]{:S(2)}) collective-permute-start(f16[6,128,128]{2,1,0:T(8,128)(2,1)S(1)} %multiply_convert_fusion), channel_id=1, source_target_pairs={{0,2},{1,3},{2,0},{3,1},{4,6},{5,7},{6,4},{7,5},{8,10},{9,11},{10,... | collective-permute-start | bytes 589832 | tf_op jit(solution)/shard_map/ppermute | solution.py:255
  23.6 0.1 dynamic_slice.7
  23.7 5.4 %collective-permute-done.5 = f16[6,128,128]{2,1,0:T(8,128)(2,1)S(1)} collective-permute-done((f16[6,128,128]{2,1,0:T(8,128)(2,1)S(1)}, f16[6,128,128]{2,1,0:T(8,128)(2,1)S(1)}, u32[]{:S(2)}, u32[]{:S(2)}) %collective-permute-start.5) | collective-permute-done | bytes 196640 | tf_op jit(solution)/shard_map/ppermute | solution.py:255
  29.2 0.1 add_multiply_fusion
  29.2 0.2 fusion.1
  29.4 0.1 collective-permute-start.6
  29.5 1.4 %collective-permute-done.6 = bf16[768,128]{1,0:T(8,128)(2,1)S(1)} collective-permute-done((bf16[768,128]{1,0:T(8,128)(2,1)S(1)}, bf16[768,128]{1,0:T(8,128)(2,1)S(1)}, u32[]{:S(2)}, u32[]{:S(2)}) %collective-permute-start.6) | collective-permute-done | bytes 196640 | tf_op jit(solution)/shard_map/ppermute | solution.py:262
  31.0 0.8 %pad_maximum_fusion = bf16[1536,128]{1,0:T(8,128)(2,1)} fusion(bf16[768,128]{1,0:T(8,128)(2,1)S(1)} %get-tuple-element.16, bf16[768,128]{1,0:T(8,128)(2,1)S(1)} %get-tuple-element.15), kind=kLoop, calls=%fused_computation | loop fusion | flops 786432 | bytes 786432 | tf_op jit(solution)/shard_map/concatenate | solution.py:265
  (18 shorter events, 0.1 us)
Async XLA Ops:
  0.0 8.5 %copy-start.7 = (s32[1,1,86]{2,1,0:T(1,128)S(1)}, s32[1,1,86]{2,1,0:T(1,128)}, u32[]{:S(2)}) copy-start(s32[1,1,86]{2,1,0:T(1,128)} %param.11) | copy-start | bytes 1036
  0.1 1.8 %copy-start = (bf16[1,1,86,128,128]{4,3,2,1,0:T(8,128)(2,1)S(1)}, bf16[1,1,86,128,128]{4,3,2,1,0:T(8,128)(2,1)}, u32[]{:S(2)}) copy-start(bf16[1,1,86,128,128]{4,3,2,1,0:T(8,128)(2,1)} %param.10) | copy-start | bytes 8454148
  1.9 1.0 %copy-start.3 = (bf16[1536,128]{1,0:T(8,128)(2,1)S(1)}, bf16[1536,128]{1,0:T(8,128)(2,1)}, u32[]{:S(2)}) copy-start(bf16[1536,128]{1,0:T(8,128)(2,1)} %activity_ref.1) | copy-start | bytes 1179652
  2.9 0.7 %copy-start.6 = (s32[1,1,86]{2,1,0:T(1,128)S(1)}, s32[1,1,86]{2,1,0:T(1,128)}, u32[]{:S(2)}) copy-start(s32[1,1,86]{2,1,0:T(1,128)} %param.11) | copy-start | bytes 1036
  3.5 0.7 %copy-start.8 = (s32[1,1,86]{2,1,0:T(1,128)S(1)}, s32[1,1,86]{2,1,0:T(1,128)}, u32[]{:S(2)}) copy-start(s32[1,1,86]{2,1,0:T(1,128)} %param.12) | copy-start | bytes 1036
  4.2 4.3 %copy-start.1 = (bf16[1,1,86,128,128]{4,3,2,1,0:T(8,128)(2,1)S(1)}, bf16[1,1,86,128,128]{4,3,2,1,0:T(8,128)(2,1)}, u32[]{:S(2)}) copy-start(bf16[1,1,86,128,128]{4,3,2,1,0:T(8,128)(2,1)} %param.10) | copy-start | bytes 8454148
  4.2 4.3 %copy-start.2 = (s32[1,1,512,128]{3,2,1,0:T(8,128)S(1)}, s32[1,1,512,128]{3,2,1,0:T(8,128)}, u32[]{:S(2)}) copy-start(s32[1,1,512,128]{3,2,1,0:T(8,128)} %param.14) | copy-start | bytes 786436
  4.2 4.4 %copy-start.5 = (bf16[1,1,512,128]{3,2,1,0:T(8,128)(2,1)S(1)}, bf16[1,1,512,128]{3,2,1,0:T(8,128)(2,1)}, u32[]{:S(2)}) copy-start(bf16[1,1,512,128]{3,2,1,0:T(8,128)(2,1)} %param.15) | copy-start | bytes 393220
  4.2 8.6 %copy-start.9 = (s32[1,1,2]{2,1,0:T(1,128)S(1)}, s32[1,1,2]{2,1,0:T(1,128)}, u32[]{:S(2)}) copy-start(s32[1,1,2]{2,1,0:T(1,128)} %param.13) | copy-start | bytes 28
  5.5 4.9 %collective-permute-start = (bf16[2,128,128]{2,1,0:T(8,128)(2,1)S(1)}, bf16[2,128,128]{2,1,0:T(8,128)(2,1)S(1)}, u32[]{:S(2)}, u32[]{:S(2)}) collective-permute-start(bf16[2,128,128]{2,1,0:T(8,128)(2,1)S(1)} %get-tuple-element.10), channel_id=1, source_target_pairs={{0,4},{1,0},{2,6},{3,2},{4,8},{5,1},{6,10},{7,3},{8,12},{9,5},{10,... | collective-permute-start | bytes 196616 | tf_op jit(solution)/shard_map/ppermute | solution.py:202
  8.5 4.3 %collective-permute-start.1 = (bf16[2,128,128]{2,1,0:T(8,128)(2,1)S(1)}, bf16[2,128,128]{2,1,0:T(8,128)(2,1)S(1)}, u32[]{:S(2)}, u32[]{:S(2)}) collective-permute-start(bf16[2,128,128]{2,1,0:T(8,128)(2,1)S(1)} %get-tuple-element.11), channel_id=1, source_target_pairs={{4,0},{0,1},{6,2},{2,3},{8,4},{1,5},{10,6},{3,7},{12,8},{5,9},{14,... | collective-permute-start | bytes 196616 | tf_op jit(solution)/shard_map/ppermute | solution.py:203
  13.5 3.5 %collective-permute-start.2 = (bf16[2,128,128]{2,1,0:T(8,128)(2,1)S(1)}, bf16[2,128,128]{2,1,0:T(8,128)(2,1)S(1)}, u32[]{:S(2)}, u32[]{:S(2)}) collective-permute-start(bf16[2,128,128]{2,1,0:T(8,128)(2,1)S(1)} %oblique_ratios.1.oblique_ref), channel_id=1, source_target_pairs={{0,4},{1,0},{2,6},{3,2},{4,8},{5,1},{6,10},{7,3},{8,12},{9,5},{10,... | collective-permute-start | bytes 196616 | tf_op jit(solution)/shard_map/ppermute | solution.py:221
  15.0 4.3 %collective-permute-start.3 = (bf16[2,128,128]{2,1,0:T(8,128)(2,1)S(1)}, bf16[2,128,128]{2,1,0:T(8,128)(2,1)S(1)}, u32[]{:S(2)}, u32[]{:S(2)}) collective-permute-start(bf16[2,128,128]{2,1,0:T(8,128)(2,1)S(1)} %oblique_ratios.1.oblique_ref), channel_id=1, source_target_pairs={{4,0},{0,1},{6,2},{2,3},{8,4},{1,5},{10,6},{3,7},{12,8},{5,9},{14,... | collective-permute-start | bytes 196616 | tf_op jit(solution)/shard_map/ppermute | solution.py:222
  20.4 3.2 %copy-start.10 = (f32[1536]{0:T(1024)S(1)}, f32[1536]{0:T(1024)}, u32[]{:S(2)}) copy-start(f32[1536]{0:T(1024)} %param.9) | copy-start | bytes 18436
  20.5 8.7 %copy-start.4 = (bf16[1536,128]{1,0:T(8,128)(2,1)S(1)}, bf16[1536,128]{1,0:T(8,128)(2,1)}, u32[]{:S(2)}) copy-start(bf16[1536,128]{1,0:T(8,128)(2,1)} %activity_ref.1) | copy-start | bytes 1179652
  20.5 1.5 %collective-permute-start.4 = (f16[6,128,128]{2,1,0:T(8,128)(2,1)S(1)}, f16[6,128,128]{2,1,0:T(8,128)(2,1)S(1)}, u32[]{:S(2)}, u32[]{:S(2)}) collective-permute-start(f16[6,128,128]{2,1,0:T(8,128)(2,1)S(1)} %convert_element_type.24), channel_id=1, source_target_pairs={{0,1},{1,0},{2,3},{3,2},{4,5},{5,4},{6,7},{7,6},{8,9},{9,8},{10,11... | collective-permute-start | bytes 589832 | tf_op jit(solution)/shard_map/ppermute | solution.py:250
  22.1 7.1 %collective-permute-start.5 = (f16[6,128,128]{2,1,0:T(8,128)(2,1)S(1)}, f16[6,128,128]{2,1,0:T(8,128)(2,1)S(1)}, u32[]{:S(2)}, u32[]{:S(2)}) collective-permute-start(f16[6,128,128]{2,1,0:T(8,128)(2,1)S(1)} %multiply_convert_fusion), channel_id=1, source_target_pairs={{0,2},{1,3},{2,0},{3,1},{4,6},{5,7},{6,4},{7,5},{8,10},{9,11},{10,... | collective-permute-start | bytes 589832 | tf_op jit(solution)/shard_map/ppermute | solution.py:255
  29.4 1.5 %collective-permute-start.6 = (bf16[768,128]{1,0:T(8,128)(2,1)S(1)}, bf16[768,128]{1,0:T(8,128)(2,1)S(1)}, u32[]{:S(2)}, u32[]{:S(2)}) collective-permute-start(bf16[768,128]{1,0:T(8,128)(2,1)S(1)} %fusion.1), channel_id=1, source_target_pairs={{0,1},{1,0},{2,3},{3,2},{4,5},{5,4},{6,7},{7,6},{8,9},{9,8},{10,11... | collective-permute-start | bytes 589832 | tf_op jit(solution)/shard_map/ppermute | solution.py:262

commit v2 on v1

v2 whole, which is shorter than its diff:
```python
import functools

import jax
import jax.numpy as jnp
from jax import lax
from jax.experimental import pallas as pl
from jax.experimental.pallas import tpu as pltpu
from jax.sharding import PartitionSpec as P

VMEM = pl.BlockSpec(memory_space=pltpu.VMEM)
SMEM = pl.BlockSpec(memory_space=pltpu.SMEM)
HBM = pl.BlockSpec(memory_space=pltpu.HBM)
PART_SCALE = 256.0
CHIP_SCALE = 128.0
GROUP = 4
PIECE = 8


def params(mebibytes=16):
    return pltpu.CompilerParams(vmem_limit_bytes=mebibytes * 1024 * 1024)


def place(slabs):
    slab = lax.axis_index("slab")
    odd = lax.axis_index("angle") % 2
    left = slab > 0
    right = slab < slabs - 1
    even = odd == 0
    forth = jnp.logical_or(jnp.logical_and(even, left), jnp.logical_and(~even, right))
    back = jnp.logical_or(jnp.logical_and(even, right), jnp.logical_and(~even, left))
    return odd, forth, back


def index_tiles(voxel_ref, line_ref, slot_ref, blocks, lines):
    stride = lines + 1
    for n in range(blocks * stride):
        slot_ref[n] = -1
    for k in range(voxel_ref.shape[-1]):
        slot_ref[voxel_ref[k] * stride + line_ref[k]] = k


def tile_of(tiles_ref, slot_ref, voxel, line, lines):
    slot = slot_ref[voxel * (lines + 1) + line]
    tile = tiles_ref[jnp.maximum(slot, 0)]
    return jnp.where(slot >= 0, tile, jnp.zeros_like(tile))


def project(image, tiles_ref, slot_ref, voxels, which, lines):
    weights = jnp.concatenate(
        [
            jnp.concatenate([tile_of(tiles_ref, slot_ref, v, c, lines) for c in which], axis=1)
            for v in voxels
        ],
        axis=0,
    )
    return jnp.dot(image, weights, preferred_element_type=jnp.float32)


def edge_kernel(
    blocks, own, lines, voxel_hbm, line_hbm, activity_hbm, tiles_hbm,
    forth_ref, back_ref, image_ref, tiles_ref,
    voxel_ref, line_ref, activity_ref, slot_ref, small_sem, tile_sem,
):
    size = tiles_ref.shape[-1]
    total = tiles_ref.shape[0]
    width = (lines - own) // 2
    first = [
        pltpu.make_async_copy(voxel_hbm, voxel_ref, small_sem.at[0]),
        pltpu.make_async_copy(line_hbm, line_ref, small_sem.at[1]),
        pltpu.make_async_copy(activity_hbm, activity_ref, small_sem.at[2]),
    ]
    pieces = []
    for n, start in enumerate(range(0, total, PIECE)):
        span = pl.ds(start, min(PIECE, total - start))
        pieces.append(
            pltpu.make_async_copy(tiles_hbm.at[span], tiles_ref.at[span], tile_sem.at[n])
        )
    for copy in first + pieces:
        copy.start()
    first[0].wait()
    first[1].wait()
    index_tiles(voxel_ref, line_ref, slot_ref, blocks, lines)
    first[2].wait()
    for v in range(blocks):
        image_ref[:, v * size : (v + 1) * size] = activity_ref[v * size : (v + 1) * size, :].T
    odd = lax.axis_index("angle") % 2
    outs = (
        (forth_ref, own + width * (1 - odd)),
        (back_ref, own + width * odd),
    )
    sums = [None, None]
    waited = 0
    for low in range(0, blocks, GROUP):
        high = min(low + GROUP, blocks)
        needed = len(pieces) if high == blocks else min(len(pieces), pl.cdiv(high * lines, PIECE))
        for copy in pieces[waited:needed]:
            copy.wait()
        waited = needed
        image = image_ref[:, low * size : high * size]
        for n, (_, start) in enumerate(outs):
            which = [start + c for c in range(width)]
            part = project(image, tiles_ref, slot_ref, range(low, high), which, lines)
            sums[n] = part if sums[n] is None else sums[n] + part
    for n, (out_ref, _) in enumerate(outs):
        for c in range(width):
            out_ref[c] = sums[n][:, c * size : (c + 1) * size].astype(out_ref.dtype)


def own_kernel(
    blocks, own, lines, voxel_ref, line_ref, rows_ref, image_ref, tiles_ref, counts_ref,
    background_ref, base_ref, measured_ref, ratio_ref, matrix_ref, slot_ref, order_ref,
):
    size = tiles_ref.shape[-1]
    width = (lines - own) // 2
    half = blocks // 2
    index_tiles(voxel_ref, line_ref, slot_ref, blocks, lines)
    for j in range(width):
        order_ref[j] = rows_ref[j]
    at = jnp.int32(width)
    for o in range(own):
        oblique = functools.reduce(jnp.logical_or, [rows_ref[j] == o for j in range(width)])
        order_ref[jnp.where(oblique, own, at)] = o
        at = at + jnp.where(oblique, 0, 1)
    image = image_ref[...]
    for start in range(0, own, width):
        which = [order_ref[start + c] for c in range(width)]
        sums = project(image, tiles_ref, slot_ref, range(blocks), which, lines)
        for c, row in enumerate(which):
            base = sums[:, c * size : (c + 1) * size].T + background_ref[row].astype(jnp.float32)
            measured = counts_ref[row].astype(jnp.float32)
            if start == 0:
                base_ref[c] = base
                measured_ref[c] = measured
            else:
                ratio_ref[start - width + c] = (measured / base).astype(ratio_ref.dtype)
    away = (1 - lax.axis_index("angle") % 2) * half
    for v in range(blocks):
        voxel = away + v if v < half else half - away + v - half
        for c in range(lines):
            line = order_ref[c] if c < own else c
            matrix_ref[v * size : (v + 1) * size, c * size : (c + 1) * size] = tile_of(
                tiles_ref, slot_ref, voxel, line, lines
            )


def oblique_kernel(slabs, forth_ref, back_ref, base_ref, measured_ref, out_ref):
    _, has_forth, has_back = place(slabs)
    for j in range(out_ref.shape[0]):
        forth = forth_ref[j].astype(jnp.float32)
        back = back_ref[j].astype(jnp.float32)
        extra = jnp.where(has_forth, forth, 0.0) + jnp.where(has_back, back, 0.0)
        out_ref[j] = (measured_ref[j] / (base_ref[j] + extra.T)).astype(out_ref.dtype)


def own_back_kernel(own, matrix_ref, oblique_ref, ratio_ref, out_ref):
    size = ratio_ref.shape[1]
    ratios = jnp.concatenate([oblique_ref[...], ratio_ref[...]], axis=0)
    ratios = ratios.reshape(own * size, -1)
    out_ref[...] = jnp.dot(
        matrix_ref[:, : own * size], ratios, preferred_element_type=jnp.float32
    )


def edge_back_kernel(slabs, own, start, scale, matrix_ref, forth_ref, back_ref, own_ref, out_ref):
    size = forth_ref.shape[1]
    rows = out_ref.shape[0]
    odd, has_forth, has_back = place(slabs)
    forth = jnp.where(has_forth, forth_ref[...], jnp.zeros_like(forth_ref))
    back = jnp.where(has_back, back_ref[...], jnp.zeros_like(back_ref))
    left = jnp.where(odd == 0, forth, back)
    right = jnp.where(odd == 0, back, forth)
    ratios = jnp.concatenate([left, right], axis=0)
    ratios = ratios.reshape(ratios.shape[0] * size, -1)
    sums = jnp.dot(
        matrix_ref[start : start + rows, own * size :], ratios, preferred_element_type=jnp.float32
    )
    out_ref[...] = (sums + own_ref[start : start + rows]) * scale


def body(
    slabs, angles, activity, sensitivity, system_tiles, tile_voxel, tile_line, oblique_rows,
    counts, background,
):
    size = system_tiles.shape[-1]
    frames = activity.shape[1]
    blocks = activity.shape[0] // size
    own = counts.shape[2] // size
    width = oblique_rows.shape[-1]
    lines = own + 2 * width
    half = blocks // 2
    tiles = system_tiles[0, 0]
    voxel = tile_voxel[0, 0]
    line = tile_line[0, 0]
    rows = oblique_rows[0, 0]
    measured = counts[0, 0].reshape(own, size, frames)
    additive = background[0, 0].reshape(own, size, frames)

    forth = []
    for s in range(slabs):
        for a in range(angles):
            t = s + 1 if a % 2 == 0 else s - 1
            here = s * angles + a
            there = t * angles + a if 0 <= t < slabs else s * angles + (a ^ 1)
            forth.append((here, there))
    back = [(there, here) for here, there in forth]
    both = ("slab", "angle")
    slots = pltpu.SMEM((blocks * (lines + 1),), jnp.int32)

    def array(dtype, *shape):
        return jax.ShapeDtypeStruct(shape, dtype)

    edge_forth, edge_back, image, held = pl.pallas_call(
        functools.partial(edge_kernel, blocks, own, lines),
        out_shape=(
            array(jnp.bfloat16, width, frames, size),
            array(jnp.bfloat16, width, frames, size),
            array(jnp.bfloat16, frames, blocks * size),
            array(jnp.bfloat16, *tiles.shape),
        ),
        in_specs=[HBM] * 4,
        out_specs=(VMEM,) * 4,
        scratch_shapes=[
            pltpu.SMEM(voxel.shape, jnp.int32),
            pltpu.SMEM(line.shape, jnp.int32),
            pltpu.VMEM(activity.shape, activity.dtype),
            slots,
            pltpu.SemaphoreType.DMA((3,)),
            pltpu.SemaphoreType.DMA((pl.cdiv(tiles.shape[0], PIECE),)),
        ],
        compiler_params=params(),
        name="edge_partials",
    )(*[pltpu.with_memory_space_constraint(a, pltpu.HBM) for a in (voxel, line, activity, tiles)])
    got_forth = lax.ppermute(edge_forth, both, forth)
    got_back = lax.ppermute(edge_back, both, back)
    base, taken, ratio, matrix = pl.pallas_call(
        functools.partial(own_kernel, blocks, own, lines),
        out_shape=(
            array(jnp.float32, width, size, frames),
            array(jnp.float32, width, size, frames),
            array(jnp.bfloat16, own - width, size, frames),
            array(jnp.bfloat16, blocks * size, lines * size),
        ),
        in_specs=[SMEM] * 3 + [VMEM] * 4,
        out_specs=(VMEM,) * 4,
        scratch_shapes=[slots, pltpu.SMEM((own + 1,), jnp.int32)],
        compiler_params=params(),
        name="own_partials",
    )(voxel, line, rows, image, held, measured, additive)
    oblique = pl.pallas_call(
        functools.partial(oblique_kernel, slabs),
        out_shape=array(jnp.bfloat16, width, size, frames),
        in_specs=[VMEM] * 4,
        out_specs=VMEM,
        compiler_params=params(),
        name="oblique_ratios",
    )(got_forth, got_back, base, taken)
    beside_forth = lax.ppermute(oblique, both, forth)
    beside_back = lax.ppermute(oblique, both, back)
    own_back = pl.pallas_call(
        functools.partial(own_back_kernel, own),
        out_shape=array(jnp.float32, blocks * size, frames),
        in_specs=[VMEM] * 3,
        out_specs=VMEM,
        compiler_params=params(),
        name="own_back",
    )(matrix, oblique, ratio)

    half_rows = half * size

    def edge_half(start, scale, name):
        return pl.pallas_call(
            functools.partial(edge_back_kernel, slabs, own, start, scale),
            out_shape=array(jnp.float32, half_rows, frames),
            in_specs=[VMEM] * 4,
            out_specs=VMEM,
            compiler_params=params(),
            name=name,
        )(matrix, beside_forth, beside_back, own_back)

    odd = lax.axis_index("angle") % 2
    mine = odd * half_rows
    image_rows = lax.dynamic_slice_in_dim(activity, mine, half_rows, 0).astype(jnp.float32)
    sens_rows = lax.dynamic_slice_in_dim(sensitivity, mine, half_rows, 0)
    pairs = [(a, a ^ 1) for a in range(angles)]
    sent = edge_half(0, PART_SCALE, "edge_back_sent").astype(jnp.float16)
    got = lax.ppermute(sent, "angle", pairs)
    kept = edge_half(half_rows, 1.0, "edge_back_kept")
    chip = kept + got.astype(jnp.float32) * (1.0 / PART_SCALE)
    if angles == 4:
        chip = (chip * CHIP_SCALE).astype(jnp.float16)
        beside = lax.ppermute(chip, "angle", [(a, a ^ 2) for a in range(angles)])
        total = (chip.astype(jnp.float32) + beside.astype(jnp.float32)) * (1.0 / CHIP_SCALE)
    else:
        groups = [list(range(odd_one, angles, 2)) for odd_one in range(2)]
        total = lax.psum(chip, "angle", axis_index_groups=groups)
    new_rows = (image_rows * total / sens_rows[:, None]).astype(jnp.bfloat16)
    other_rows = lax.ppermute(new_rows, "angle", pairs)
    low = jnp.where(odd == 0, new_rows, other_rows)
    high = jnp.where(odd == 0, other_rows, new_rows)
    return jnp.concatenate([low, high], axis=0)


def solution(mesh):
    placed = (
        P(("groups", "slab"), None),
        P(("groups", "slab")),
        P(("groups", "slab"), "angle", None, None, None),
        P(("groups", "slab"), "angle", None),
        P(("groups", "slab"), "angle", None),
        P(("groups", "slab"), "angle", None),
        P(("groups", "slab"), "angle", None, None),
        P(("groups", "slab"), "angle", None, None),
    )
    return jax.shard_map(
        functools.partial(body, mesh.shape["slab"], mesh.shape["angle"]),
        mesh=mesh,
        in_specs=placed,
        out_specs=P(("groups", "slab"), None),
        check_vma=False,
    )
```

time: 31.9 us -> 27.7 us (0.87)
  local copies, waits for them, and re-layouts: 4.21 us -> 0.11 us
  waiting for transfers between devices: 13 us -> 13.4 us
    unnamed x22 -> x14, local copies, waits for them, and re-layouts: 4.13 us -> 0.03 us
    pallas_call x4, Pallas kernels: 4.18 us -> 1.43 us  [the longest x2 0.75 us: edge_half(): pl.pallas_call(functools.partial(edge_back_kernel, slabs, own, start, sca...]
    pallas_call x1, Pallas kernels: 1.27 us -> 2.74 us  [body(): pl.pallas_call(functools.partial(edge_kernel, blocks, own, lines), out_sh...]
    pallas_call x1, Pallas kernels: 1.32 us -> 2.33 us  [body(): pl.pallas_call(functools.partial(own_kernel, blocks, own, lines), out_sha...]
    ppermute x1, waiting for transfers between devices: 0.59 us -> 1.33 us  [body(): beside_forth = lax.ppermute(oblique, both, forth)]
    ppermute x1, waiting for transfers between devices: 0.31 us -> 1.05 us  [body(): got = lax.ppermute(sent, 'angle', pairs)]
    ppermute x1, waiting for transfers between devices: 0.55 us -> 0.01 us  [body(): got_forth = lax.ppermute(edge_forth, both, forth)]
    ppermute x1, waiting for transfers between devices: 2.36 us -> 1.88 us  [body(): got_back = lax.ppermute(edge_back, both, back)]
  transfers between devices with their start and end apart: 7 -> 7, of which waited for: 7 -> 6; matrix products, arithmetic and copies ran while one was open for 0% -> 0% of each run, Pallas kernels for 12% -> 12%
where the time goes in v2:
time: 27.7 us; the launch traced here: 27.6 us
  waiting for transfers between devices  13.4 us (48%)
  Pallas kernels  6.5 us (23%)
  starting transfers between devices  6.35 us (23%)
  other arithmetic  1.09 us (4%)
    ppermute x1, waiting for transfers between devices, body(): beside = lax.ppermute(chip, 'angle', [(a, a ^ 2) for a in range(angles)])  5.37 us
    ppermute x1, starting transfers between devices, body(): got_forth = lax.ppermute(edge_forth, both, forth)  3.06 us
    pallas_call x1, Pallas kernels, body(): pl.pallas_call(functools.partial(edge_kernel, blocks, own, lines), out_sh...  2.74 us
    ppermute x1, waiting for transfers between devices, body(): beside_back = lax.ppermute(oblique, both, back)  2.36 us
    pallas_call x1, Pallas kernels, body(): pl.pallas_call(functools.partial(own_kernel, blocks, own, lines), out_sha...  2.33 us
    ppermute x1, waiting for transfers between devices, body(): got_back = lax.ppermute(edge_back, both, back)  1.88 us
    ppermute x1, starting transfers between devices, body(): beside_forth = lax.ppermute(oblique, both, forth)  1.59 us
    ppermute x1, starting transfers between devices, body(): beside = lax.ppermute(chip, 'angle', [(a, a ^ 2) for a in range(angles)])  1.56 us
  transfers between devices with their start and end apart: 7, of which 6 were waited for; matrix products, arithmetic and copies ran while one was open for 0% of the time, Pallas kernels for 12%

profile of v2, /device:TPU:0, one launch (start us, length us, event | category | flops | bytes accessed | tf_op | source)
XLA Modules:
  0.0 27.6 jit_solution(8323921138784426425)
XLA Ops:
  0.0 2.7 %edge_partials.1 = (bf16[2,128,128]{2,1,0:T(8,128)(2,1)S(1)}, bf16[2,128,128]{2,1,0:T(8,128)(2,1)S(1)}, bf16[128,1536]{1,0:T(8,128)(2,1)S(1)}, bf16[86,128,128]{2,1,0:T(8,128)(2,1)S(1)}) custom-call(s32[86]{0:T(128)} %bitcast.8, s32[86]{0:T(128)} %bitcast.10, bf16[1536,128]{1,0:T(8,128)(2,1)} %activity_hbm.1, bf16[86,128,128]{2,1,0:T(8,128)(2,1)} %bitcast.13), custom_call_target="tpu_custom_call" | custom-call | tf_op jit(solution)/shard_map/edge_partials/pallas_call | solution.py:212
  2.8 3.1 %collective-permute-start = (bf16[2,128,128]{2,1,0:T(8,128)(2,1)S(1)}, bf16[2,128,128]{2,1,0:T(8,128)(2,1)S(1)}, u32[]{:S(2)}, u32[]{:S(2)}) collective-permute-start(bf16[2,128,128]{2,1,0:T(8,128)(2,1)S(1)} %get-tuple-element.16), channel_id=1, source_target_pairs={{0,4},{1,0},{2,6},{3,2},{4,8},{5,1},{6,10},{7,3},{8,12},{9,5},{10,... | collective-permute-start | bytes 196616 | tf_op jit(solution)/shard_map/ppermute | solution.py:233
  5.8 0.0 collective-permute-start.1
  5.8 0.0 copy-done.2
  5.8 0.0 copy-done.3
  5.8 0.0 copy-done.4
  5.8 0.0 copy-done
  5.9 0.0 copy-done.1
  5.9 2.3 %own_partials.1 = (f32[2,128,128]{2,1,0:T(8,128)S(1)}, f32[2,128,128]{2,1,0:T(8,128)S(1)}, bf16[2,128,128]{2,1,0:T(8,128)(2,1)S(1)}, bf16[1536,1024]{1,0:T(8,128)(2,1)S(1)}) custom-call(s32[86]{0:T(128)S(1)} %bitcast.9, s32[86]{0:T(128)S(1)} %bitcast.11, s32[2]{0:T(128)S(1)} %bitcast.12, bf16[128,1536]{1,0:T(8,128)(2,1)S(1)} %get-tuple-element.13.image_ref, ...), custom_call_target="tpu_custom_call" | custom-call | tf_op jit(solution)/shard_map/own_partials/pallas_call | solution.py:235
  8.2 0.0 collective-permute-done.forth_ref
  8.2 1.9 %collective-permute-done.1.back_ref = bf16[2,128,128]{2,1,0:T(8,128)(2,1)S(1)} collective-permute-done((bf16[2,128,128]{2,1,0:T(8,128)(2,1)S(1)}, bf16[2,128,128]{2,1,0:T(8,128)(2,1)S(1)}, u32[]{:S(2)}, u32[]{:S(2)}) %collective-permute-start.1) | collective-permute-done | bytes 65568 | tf_op jit(solution)/shard_map/ppermute | solution.py:234
  10.1 0.1 oblique_ratios.1.oblique_ref
  10.2 1.6 %collective-permute-start.2 = (bf16[2,128,128]{2,1,0:T(8,128)(2,1)S(1)}, bf16[2,128,128]{2,1,0:T(8,128)(2,1)S(1)}, u32[]{:S(2)}, u32[]{:S(2)}) collective-permute-start(bf16[2,128,128]{2,1,0:T(8,128)(2,1)S(1)} %oblique_ratios.1.oblique_ref), channel_id=1, source_target_pairs={{0,4},{1,0},{2,6},{3,2},{4,8},{5,1},{6,10},{7,3},{8,12},{9,5},{10,... | collective-permute-start | bytes 196616 | tf_op jit(solution)/shard_map/ppermute | solution.py:257
  11.8 0.0 collective-permute-start.3
  11.8 0.6 %own_back.1.own_ref = f32[1536,128]{1,0:T(8,128)S(1)} custom-call(bf16[1536,1024]{1,0:T(8,128)(2,1)S(1)} %get-tuple-element.15.matrix_ref, bf16[2,128,128]{2,1,0:T(8,128)(2,1)S(1)} %oblique_ratios.1.oblique_ref, bf16[2,128,128]{2,1,0:T(8,128)(2,1)S(1)} %get-tuple-element.20.ratio_ref), custom_call_target="tpu_custom_call" | custom-call | tf_op jit(solution)/shard_map/own_back/pallas_call | solution.py:259
  12.4 1.3 %collective-permute-done.2.forth_ref = bf16[2,128,128]{2,1,0:T(8,128)(2,1)S(1)} collective-permute-done((bf16[2,128,128]{2,1,0:T(8,128)(2,1)S(1)}, bf16[2,128,128]{2,1,0:T(8,128)(2,1)S(1)}, u32[]{:S(2)}, u32[]{:S(2)}) %collective-permute-start.2) | collective-permute-done | bytes 65568 | tf_op jit(solution)/shard_map/ppermute | solution.py:257
  13.7 2.4 %collective-permute-done.3.back_ref = bf16[2,128,128]{2,1,0:T(8,128)(2,1)S(1)} collective-permute-done((bf16[2,128,128]{2,1,0:T(8,128)(2,1)S(1)}, bf16[2,128,128]{2,1,0:T(8,128)(2,1)S(1)}, u32[]{:S(2)}, u32[]{:S(2)}) %collective-permute-start.3) | collective-permute-done | bytes 65568 | tf_op jit(solution)/shard_map/ppermute | solution.py:258
  16.1 0.4 %edge_back_sent.1 = f32[768,128]{1,0:T(8,128)S(1)} custom-call(bf16[1536,1024]{1,0:T(8,128)(2,1)S(1)} %get-tuple-element.15.matrix_ref, bf16[2,128,128]{2,1,0:T(8,128)(2,1)S(1)} %collective-permute-done.2.forth_ref, bf16[2,128,128]{2,1,0:T(8,128)(2,1)S(1)} %collective-permute-done.3.back_ref, f32[1536,128]{1,0:T(8,128)S(1)} %own_back.1.own_ref), custom_call_target="tpu_custom_call" | custom-call | tf_op jit(solution)/shard_map/edge_back_sent/pallas_call | solution.py:271
  16.4 0.0 copy-start.6
  16.5 0.0 copy-start.5
  16.5 0.1 collective-permute-start.4
  16.6 0.4 %edge_back_kept.1 = f32[768,128]{1,0:T(8,128)S(1)} custom-call(bf16[1536,1024]{1,0:T(8,128)(2,1)S(1)} %get-tuple-element.15.matrix_ref, bf16[2,128,128]{2,1,0:T(8,128)(2,1)S(1)} %collective-permute-done.2.forth_ref, bf16[2,128,128]{2,1,0:T(8,128)(2,1)S(1)} %collective-permute-done.3.back_ref, f32[1536,128]{1,0:T(8,128)S(1)} %own_back.1.own_ref), custom_call_target="tpu_custom_call" | custom-call | tf_op jit(solution)/shard_map/edge_back_kept/pallas_call | solution.py:271
  17.0 1.0 %collective-permute-done.4 = f16[768,128]{1,0:T(8,128)(2,1)S(1)} collective-permute-done((f16[768,128]{1,0:T(8,128)(2,1)S(1)}, f16[768,128]{1,0:T(8,128)(2,1)S(1)}, u32[]{:S(2)}, u32[]{:S(2)}) %collective-permute-start.4) | collective-permute-done | bytes 196640 | tf_op jit(solution)/shard_map/ppermute | solution.py:286
  18.0 0.1 multiply_convert_fusion
  18.1 1.6 %collective-permute-start.5 = (f16[768,128]{1,0:T(8,128)(2,1)S(1)}, f16[768,128]{1,0:T(8,128)(2,1)S(1)}, u32[]{:S(2)}, u32[]{:S(2)}) collective-permute-start(f16[768,128]{1,0:T(8,128)(2,1)S(1)} %multiply_convert_fusion), channel_id=1, source_target_pairs={{0,2},{1,3},{2,0},{3,1},{4,6},{5,7},{6,4},{7,5},{8,10},{9,11},{10,... | collective-permute-start | bytes 589832 | tf_op jit(solution)/shard_map/ppermute | solution.py:291
  19.7 0.0 copy-done.6
  19.7 0.1 dynamic_slice.7
  19.7 5.4 %collective-permute-done.5 = f16[768,128]{1,0:T(8,128)(2,1)S(1)} collective-permute-done((f16[768,128]{1,0:T(8,128)(2,1)S(1)}, f16[768,128]{1,0:T(8,128)(2,1)S(1)}, u32[]{:S(2)}, u32[]{:S(2)}) %collective-permute-start.5) | collective-permute-done | bytes 196640 | tf_op jit(solution)/shard_map/ppermute | solution.py:291
  25.1 0.2 divide_convert_fusion
  25.3 0.1 collective-permute-start.6
  25.4 1.4 %collective-permute-done.6 = bf16[768,128]{1,0:T(8,128)(2,1)S(1)} collective-permute-done((bf16[768,128]{1,0:T(8,128)(2,1)S(1)}, bf16[768,128]{1,0:T(8,128)(2,1)S(1)}, u32[]{:S(2)}, u32[]{:S(2)}) %collective-permute-start.6) | collective-permute-done | bytes 196640 | tf_op jit(solution)/shard_map/ppermute | solution.py:297
  26.8 0.8 %pad_maximum_fusion = bf16[1536,128]{1,0:T(8,128)(2,1)} fusion(bf16[768,128]{1,0:T(8,128)(2,1)S(1)} %get-tuple-element.22, bf16[768,128]{1,0:T(8,128)(2,1)S(1)} %get-tuple-element.21), kind=kLoop, calls=%fused_computation | loop fusion | flops 786432 | bytes 786432 | tf_op jit(solution)/shard_map/concatenate | solution.py:300
  (8 shorter events, 0.1 us)
Async XLA Ops:
  0.0 5.8 %copy-start.2 = (s32[1,1,86]{2,1,0:T(1,128)S(1)}, s32[1,1,86]{2,1,0:T(1,128)}, u32[]{:S(2)}) copy-start(s32[1,1,86]{2,1,0:T(1,128)} %param.11) | copy-start | bytes 1036
  0.0 5.8 %copy-start.3 = (s32[1,1,86]{2,1,0:T(1,128)S(1)}, s32[1,1,86]{2,1,0:T(1,128)}, u32[]{:S(2)}) copy-start(s32[1,1,86]{2,1,0:T(1,128)} %param.12) | copy-start | bytes 1036
  0.0 5.8 %copy-start.4 = (s32[1,1,2]{2,1,0:T(1,128)S(1)}, s32[1,1,2]{2,1,0:T(1,128)}, u32[]{:S(2)}) copy-start(s32[1,1,2]{2,1,0:T(1,128)} %param.13) | copy-start | bytes 28
  0.0 5.8 %copy-start = (s32[1,1,512,128]{3,2,1,0:T(8,128)S(1)}, s32[1,1,512,128]{3,2,1,0:T(8,128)}, u32[]{:S(2)}) copy-start(s32[1,1,512,128]{3,2,1,0:T(8,128)} %param.14) | copy-start | bytes 786436
  0.0 5.8 %copy-start.1 = (bf16[1,1,512,128]{3,2,1,0:T(8,128)(2,1)S(1)}, bf16[1,1,512,128]{3,2,1,0:T(8,128)(2,1)}, u32[]{:S(2)}) copy-start(bf16[1,1,512,128]{3,2,1,0:T(8,128)(2,1)} %param.15) | copy-start | bytes 393220
  2.8 5.4 %collective-permute-start = (bf16[2,128,128]{2,1,0:T(8,128)(2,1)S(1)}, bf16[2,128,128]{2,1,0:T(8,128)(2,1)S(1)}, u32[]{:S(2)}, u32[]{:S(2)}) collective-permute-start(bf16[2,128,128]{2,1,0:T(8,128)(2,1)S(1)} %get-tuple-element.16), channel_id=1, source_target_pairs={{0,4},{1,0},{2,6},{3,2},{4,8},{5,1},{6,10},{7,3},{8,12},{9,5},{10,... | collective-permute-start | bytes 196616 | tf_op jit(solution)/shard_map/ppermute | solution.py:233
  5.8 4.3 %collective-permute-start.1 = (bf16[2,128,128]{2,1,0:T(8,128)(2,1)S(1)}, bf16[2,128,128]{2,1,0:T(8,128)(2,1)S(1)}, u32[]{:S(2)}, u32[]{:S(2)}) collective-permute-start(bf16[2,128,128]{2,1,0:T(8,128)(2,1)S(1)} %get-tuple-element.17), channel_id=1, source_target_pairs={{4,0},{0,1},{6,2},{2,3},{8,4},{1,5},{10,6},{3,7},{12,8},{5,9},{14,... | collective-permute-start | bytes 196616 | tf_op jit(solution)/shard_map/ppermute | solution.py:234
  10.2 3.5 %collective-permute-start.2 = (bf16[2,128,128]{2,1,0:T(8,128)(2,1)S(1)}, bf16[2,128,128]{2,1,0:T(8,128)(2,1)S(1)}, u32[]{:S(2)}, u32[]{:S(2)}) collective-permute-start(bf16[2,128,128]{2,1,0:T(8,128)(2,1)S(1)} %oblique_ratios.1.oblique_ref), channel_id=1, source_target_pairs={{0,4},{1,0},{2,6},{3,2},{4,8},{5,1},{6,10},{7,3},{8,12},{9,5},{10,... | collective-permute-start | bytes 196616 | tf_op jit(solution)/shard_map/ppermute | solution.py:257
  11.8 4.3 %collective-permute-start.3 = (bf16[2,128,128]{2,1,0:T(8,128)(2,1)S(1)}, bf16[2,128,128]{2,1,0:T(8,128)(2,1)S(1)}, u32[]{:S(2)}, u32[]{:S(2)}) collective-permute-start(bf16[2,128,128]{2,1,0:T(8,128)(2,1)S(1)} %oblique_ratios.1.oblique_ref), channel_id=1, source_target_pairs={{4,0},{0,1},{6,2},{2,3},{8,4},{1,5},{10,6},{3,7},{12,8},{5,9},{14,... | collective-permute-start | bytes 196616 | tf_op jit(solution)/shard_map/ppermute | solution.py:258
  16.4 3.2 %copy-start.6 = (f32[1536]{0:T(1024)S(1)}, f32[1536]{0:T(1024)}, u32[]{:S(2)}) copy-start(f32[1536]{0:T(1024)} %param.9) | copy-start | bytes 18436
  16.5 8.7 %copy-start.5 = (bf16[1536,128]{1,0:T(8,128)(2,1)S(1)}, bf16[1536,128]{1,0:T(8,128)(2,1)}, u32[]{:S(2)}) copy-start(bf16[1536,128]{1,0:T(8,128)(2,1)} %activity_hbm.1) | copy-start | bytes 1179652
  16.5 1.5 %collective-permute-start.4 = (f16[768,128]{1,0:T(8,128)(2,1)S(1)}, f16[768,128]{1,0:T(8,128)(2,1)S(1)}, u32[]{:S(2)}, u32[]{:S(2)}) collective-permute-start(f16[768,128]{1,0:T(8,128)(2,1)S(1)} %convert_element_type.22), channel_id=1, source_target_pairs={{0,1},{1,0},{2,3},{3,2},{4,5},{5,4},{6,7},{7,6},{8,9},{9,8},{10,11... | collective-permute-start | bytes 589832 | tf_op jit(solution)/shard_map/ppermute | solution.py:286
  18.1 7.0 %collective-permute-start.5 = (f16[768,128]{1,0:T(8,128)(2,1)S(1)}, f16[768,128]{1,0:T(8,128)(2,1)S(1)}, u32[]{:S(2)}, u32[]{:S(2)}) collective-permute-start(f16[768,128]{1,0:T(8,128)(2,1)S(1)} %multiply_convert_fusion), channel_id=1, source_target_pairs={{0,2},{1,3},{2,0},{3,1},{4,6},{5,7},{6,4},{7,5},{8,10},{9,11},{10,... | collective-permute-start | bytes 589832 | tf_op jit(solution)/shard_map/ppermute | solution.py:291
  25.3 1.5 %collective-permute-start.6 = (bf16[768,128]{1,0:T(8,128)(2,1)S(1)}, bf16[768,128]{1,0:T(8,128)(2,1)S(1)}, u32[]{:S(2)}, u32[]{:S(2)}) collective-permute-start(bf16[768,128]{1,0:T(8,128)(2,1)S(1)} %divide_convert_fusion), channel_id=1, source_target_pairs={{0,1},{1,0},{2,3},{3,2},{4,5},{5,4},{6,7},{7,6},{8,9},{9,8},{10,11... | collective-permute-start | bytes 589832 | tf_op jit(solution)/shard_map/ppermute | solution.py:297

commit v3 on v2

--- a/solution.py
+++ b/solution.py
@@ -26,8 +26,8 @@
     left = slab > 0
     right = slab < slabs - 1
     even = odd == 0
-    forth = jnp.logical_or(jnp.logical_and(even, left), jnp.logical_and(~even, right))
-    back = jnp.logical_or(jnp.logical_and(even, right), jnp.logical_and(~even, left))
+    forth = jnp.logical_or(jnp.logical_and(even, right), jnp.logical_and(~even, left))
+    back = jnp.logical_or(jnp.logical_and(even, left), jnp.logical_and(~even, right))
     return odd, forth, back
 
 
@@ -85,8 +85,8 @@
         image_ref[:, v * size : (v + 1) * size] = activity_ref[v * size : (v + 1) * size, :].T
     odd = lax.axis_index("angle") % 2
     outs = (
-        (forth_ref, own + width * (1 - odd)),
-        (back_ref, own + width * odd),
+        (forth_ref, own + width * odd),
+        (back_ref, own + width * (1 - odd)),
     )
     sums = [None, None]
     waited = 0
@@ -167,8 +167,8 @@
     odd, has_forth, has_back = place(slabs)
     forth = jnp.where(has_forth, forth_ref[...], jnp.zeros_like(forth_ref))
     back = jnp.where(has_back, back_ref[...], jnp.zeros_like(back_ref))
-    left = jnp.where(odd == 0, forth, back)
-    right = jnp.where(odd == 0, back, forth)
+    left = jnp.where(odd == 0, back, forth)
+    right = jnp.where(odd == 0, forth, back)
     ratios = jnp.concatenate([left, right], axis=0)
     ratios = ratios.reshape(ratios.shape[0] * size, -1)
     sums = jnp.dot(
@@ -198,7 +198,7 @@
     forth = []
     for s in range(slabs):
         for a in range(angles):
-            t = s + 1 if a % 2 == 0 else s - 1
+            t = s - 1 if a % 2 == 0 else s + 1
             here = s * angles + a
             there = t * angles + a if 0 <= t < slabs else s * angles + (a ^ 1)
             forth.append((here, there))
@@ -281,6 +281,7 @@
     mine = odd * half_rows
     image_rows = lax.dynamic_slice_in_dim(activity, mine, half_rows, 0).astype(jnp.float32)
     sens_rows = lax.dynamic_slice_in_dim(sensitivity, mine, half_rows, 0)
+    gain = image_rows / sens_rows[:, None]
     pairs = [(a, a ^ 1) for a in range(angles)]
     sent = edge_half(0, PART_SCALE, "edge_back_sent").astype(jnp.float16)
     got = lax.ppermute(sent, "angle", pairs)
@@ -293,7 +294,7 @@
     else:
         groups = [list(range(odd_one, angles, 2)) for odd_one in range(2)]
         total = lax.psum(chip, "angle", axis_index_groups=groups)
-    new_rows = (image_rows * total / sens_rows[:, None]).astype(jnp.bfloat16)
+    new_rows = (gain * total).astype(jnp.bfloat16)
     other_rows = lax.ppermute(new_rows, "angle", pairs)
     low = jnp.where(odd == 0, new_rows, other_rows)
     high = jnp.where(odd == 0, other_rows, new_rows)

time: 27.7 us -> 25.3 us (0.913)
  waiting for transfers between devices: 13.4 us -> 8.92 us
  starting transfers between devices: 6.35 us -> 8.4 us
    ppermute x1, starting transfers between devices: 0.01 us -> 2.6 us  [body(): got_back = lax.ppermute(edge_back, both, back)]
    ppermute x1, starting transfers between devices: 3.06 us -> 0.48 us  [body(): got_forth = lax.ppermute(edge_forth, both, forth)]
    ppermute x1, waiting for transfers between devices: 2.36 us -> 0.01 us  [body(): beside_back = lax.ppermute(oblique, both, back)]
    ppermute x1, starting transfers between devices: 0.01 us -> 2.08 us  [body(): beside_back = lax.ppermute(oblique, both, back)]
    ppermute x1, waiting for transfers between devices: 1.88 us -> 0.01 us  [body(): got_back = lax.ppermute(edge_back, both, back)]
    ppermute x1, starting transfers between devices: 1.59 us -> 0.36 us  [body(): beside_forth = lax.ppermute(oblique, both, forth)]
    ppermute x1, starting transfers between devices: 0.07 us -> 0.75 us  [body(): got = lax.ppermute(sent, 'angle', pairs)]
    ppermute x1, starting transfers between devices: 1.56 us -> 2.05 us  [body(): beside = lax.ppermute(chip, 'angle', [(a, a ^ 2) for a in range(angles)])]
  transfers between devices with their start and end apart: 7 -> 7, of which waited for: 6 -> 4; matrix products, arithmetic and copies ran while one was open for 0% -> 0% of each run, Pallas kernels for 12% -> 13%
where the time goes in v3:
time: 25.3 us; the launch traced here: 25.1 us
  waiting for transfers between devices  8.92 us (35%)
  starting transfers between devices  8.4 us (33%)
  Pallas kernels  6.51 us (26%)
  other arithmetic  1.09 us (4%)
    ppermute x1, waiting for transfers between devices, body(): beside = lax.ppermute(chip, 'angle', [(a, a ^ 2) for a in range(angles)])  5.14 us
    pallas_call x1, Pallas kernels, body(): pl.pallas_call(functools.partial(edge_kernel, blocks, own, lines), out_sh...  2.74 us
    ppermute x1, starting transfers between devices, body(): got_back = lax.ppermute(edge_back, both, back)  2.6 us
    pallas_call x1, Pallas kernels, body(): pl.pallas_call(functools.partial(own_kernel, blocks, own, lines), out_sha...  2.33 us
    ppermute x1, starting transfers between devices, body(): beside_back = lax.ppermute(oblique, both, back)  2.08 us
    ppermute x1, starting transfers between devices, body(): beside = lax.ppermute(chip, 'angle', [(a, a ^ 2) for a in range(angles)])  2.05 us
    ppermute x1, waiting for transfers between devices, body(): beside_forth = lax.ppermute(oblique, both, forth)  1.65 us
    ppermute x1, waiting for transfers between devices, body(): other_rows = lax.ppermute(new_rows, 'angle', pairs)  1.42 us
  transfers between devices with their start and end apart: 7, of which 4 were waited for; matrix products, arithmetic and copies ran while one was open for 0% of the time, Pallas kernels for 13%

profile of v3, /device:TPU:0, one launch (start us, length us, event | category | flops | bytes accessed | tf_op | source)
XLA Modules:
  0.0 25.1 jit_solution(2867209580962647352)
XLA Ops:
  0.0 2.7 %edge_partials.1 = (bf16[2,128,128]{2,1,0:T(8,128)(2,1)S(1)}, bf16[2,128,128]{2,1,0:T(8,128)(2,1)S(1)}, bf16[128,1536]{1,0:T(8,128)(2,1)S(1)}, bf16[86,128,128]{2,1,0:T(8,128)(2,1)S(1)}) custom-call(s32[86]{0:T(128)} %bitcast.8, s32[86]{0:T(128)} %bitcast.10, bf16[1536,128]{1,0:T(8,128)(2,1)} %activity_hbm.1, bf16[86,128,128]{2,1,0:T(8,128)(2,1)} %bitcast.13), custom_call_target="tpu_custom_call" | custom-call | tf_op jit(solution)/shard_map/edge_partials/pallas_call | solution.py:212
  2.8 0.5 %collective-permute-start = (bf16[2,128,128]{2,1,0:T(8,128)(2,1)S(1)}, bf16[2,128,128]{2,1,0:T(8,128)(2,1)S(1)}, u32[]{:S(2)}, u32[]{:S(2)}) collective-permute-start(bf16[2,128,128]{2,1,0:T(8,128)(2,1)S(1)} %get-tuple-element.16), channel_id=1, source_target_pairs={{0,1},{1,5},{2,3},{3,7},{4,0},{5,9},{6,2},{7,11},{8,4},{9,13},{10,... | collective-permute-start | bytes 196616 | tf_op jit(solution)/shard_map/ppermute | solution.py:233
  3.3 2.6 %collective-permute-start.1 = (bf16[2,128,128]{2,1,0:T(8,128)(2,1)S(1)}, bf16[2,128,128]{2,1,0:T(8,128)(2,1)S(1)}, u32[]{:S(2)}, u32[]{:S(2)}) collective-permute-start(bf16[2,128,128]{2,1,0:T(8,128)(2,1)S(1)} %get-tuple-element.17), channel_id=1, source_target_pairs={{1,0},{5,1},{3,2},{7,3},{0,4},{9,5},{2,6},{11,7},{4,8},{13,9},{6,1... | collective-permute-start | bytes 196616 | tf_op jit(solution)/shard_map/ppermute | solution.py:234
  5.9 0.0 copy-done.2
  5.9 0.0 copy-done.3
  5.9 0.0 copy-done.4
  5.9 0.0 copy-done
  5.9 0.0 copy-done.1
  5.9 2.3 %own_partials.1 = (f32[2,128,128]{2,1,0:T(8,128)S(1)}, f32[2,128,128]{2,1,0:T(8,128)S(1)}, bf16[2,128,128]{2,1,0:T(8,128)(2,1)S(1)}, bf16[1536,1024]{1,0:T(8,128)(2,1)S(1)}) custom-call(s32[86]{0:T(128)S(1)} %bitcast.9, s32[86]{0:T(128)S(1)} %bitcast.11, s32[2]{0:T(128)S(1)} %bitcast.12, bf16[128,1536]{1,0:T(8,128)(2,1)S(1)} %get-tuple-element.13.image_ref, ...), custom_call_target="tpu_custom_call" | custom-call | tf_op jit(solution)/shard_map/own_partials/pallas_call | solution.py:235
  8.2 0.0 collective-permute-done.forth_ref
  8.2 0.0 collective-permute-done.1.back_ref
  8.2 0.1 oblique_ratios.1.oblique_ref
  8.4 0.4 %collective-permute-start.2 = (bf16[2,128,128]{2,1,0:T(8,128)(2,1)S(1)}, bf16[2,128,128]{2,1,0:T(8,128)(2,1)S(1)}, u32[]{:S(2)}, u32[]{:S(2)}) collective-permute-start(bf16[2,128,128]{2,1,0:T(8,128)(2,1)S(1)} %oblique_ratios.1.oblique_ref), channel_id=1, source_target_pairs={{0,1},{1,5},{2,3},{3,7},{4,0},{5,9},{6,2},{7,11},{8,4},{9,13},{10,... | collective-permute-start | bytes 196616 | tf_op jit(solution)/shard_map/ppermute | solution.py:257
  8.7 2.1 %collective-permute-start.3 = (bf16[2,128,128]{2,1,0:T(8,128)(2,1)S(1)}, bf16[2,128,128]{2,1,0:T(8,128)(2,1)S(1)}, u32[]{:S(2)}, u32[]{:S(2)}) collective-permute-start(bf16[2,128,128]{2,1,0:T(8,128)(2,1)S(1)} %oblique_ratios.1.oblique_ref), channel_id=1, source_target_pairs={{1,0},{5,1},{3,2},{7,3},{0,4},{9,5},{2,6},{11,7},{4,8},{13,9},{6,1... | collective-permute-start | bytes 196616 | tf_op jit(solution)/shard_map/ppermute | solution.py:258
  10.8 0.6 %own_back.1.own_ref = f32[1536,128]{1,0:T(8,128)S(1)} custom-call(bf16[1536,1024]{1,0:T(8,128)(2,1)S(1)} %get-tuple-element.15.matrix_ref, bf16[2,128,128]{2,1,0:T(8,128)(2,1)S(1)} %oblique_ratios.1.oblique_ref, bf16[2,128,128]{2,1,0:T(8,128)(2,1)S(1)} %get-tuple-element.20.ratio_ref), custom_call_target="tpu_custom_call" | custom-call | tf_op jit(solution)/shard_map/own_back/pallas_call | solution.py:259
  11.4 1.6 %collective-permute-done.2.forth_ref = bf16[2,128,128]{2,1,0:T(8,128)(2,1)S(1)} collective-permute-done((bf16[2,128,128]{2,1,0:T(8,128)(2,1)S(1)}, bf16[2,128,128]{2,1,0:T(8,128)(2,1)S(1)}, u32[]{:S(2)}, u32[]{:S(2)}) %collective-permute-start.2) | collective-permute-done | bytes 65568 | tf_op jit(solution)/shard_map/ppermute | solution.py:257
  13.0 0.0 collective-permute-done.3.back_ref
  13.0 0.4 %edge_back_sent.1 = f32[768,128]{1,0:T(8,128)S(1)} custom-call(bf16[1536,1024]{1,0:T(8,128)(2,1)S(1)} %get-tuple-element.15.matrix_ref, bf16[2,128,128]{2,1,0:T(8,128)(2,1)S(1)} %collective-permute-done.2.forth_ref, bf16[2,128,128]{2,1,0:T(8,128)(2,1)S(1)} %collective-permute-done.3.back_ref, f32[1536,128]{1,0:T(8,128)S(1)} %own_back.1.own_ref), custom_call_target="tpu_custom_call" | custom-call | tf_op jit(solution)/shard_map/edge_back_sent/pallas_call | solution.py:271
  13.4 0.0 copy-start.6
  13.4 0.0 copy-start.5
  13.5 0.8 %collective-permute-start.4 = (f16[768,128]{1,0:T(8,128)(2,1)S(1)}, f16[768,128]{1,0:T(8,128)(2,1)S(1)}, u32[]{:S(2)}, u32[]{:S(2)}) collective-permute-start(f16[768,128]{1,0:T(8,128)(2,1)S(1)} %convert_element_type.22), channel_id=1, source_target_pairs={{0,1},{1,0},{2,3},{3,2},{4,5},{5,4},{6,7},{7,6},{8,9},{9,8},{10,11... | collective-permute-start | bytes 589832 | tf_op jit(solution)/shard_map/ppermute | solution.py:287
  14.2 0.4 %edge_back_kept.1 = f32[768,128]{1,0:T(8,128)S(1)} custom-call(bf16[1536,1024]{1,0:T(8,128)(2,1)S(1)} %get-tuple-element.15.matrix_ref, bf16[2,128,128]{2,1,0:T(8,128)(2,1)S(1)} %collective-permute-done.2.forth_ref, bf16[2,128,128]{2,1,0:T(8,128)(2,1)S(1)} %collective-permute-done.3.back_ref, f32[1536,128]{1,0:T(8,128)S(1)} %own_back.1.own_ref), custom_call_target="tpu_custom_call" | custom-call | tf_op jit(solution)/shard_map/edge_back_kept/pallas_call | solution.py:271
  14.6 0.7 %collective-permute-done.4 = f16[768,128]{1,0:T(8,128)(2,1)S(1)} collective-permute-done((f16[768,128]{1,0:T(8,128)(2,1)S(1)}, f16[768,128]{1,0:T(8,128)(2,1)S(1)}, u32[]{:S(2)}, u32[]{:S(2)}) %collective-permute-start.4) | collective-permute-done | bytes 196640 | tf_op jit(solution)/shard_map/ppermute | solution.py:287
  15.3 0.1 multiply_convert_fusion.1
  15.4 2.0 %collective-permute-start.5 = (f16[768,128]{1,0:T(8,128)(2,1)S(1)}, f16[768,128]{1,0:T(8,128)(2,1)S(1)}, u32[]{:S(2)}, u32[]{:S(2)}) collective-permute-start(f16[768,128]{1,0:T(8,128)(2,1)S(1)} %multiply_convert_fusion.1), channel_id=1, source_target_pairs={{0,2},{1,3},{2,0},{3,1},{4,6},{5,7},{6,4},{7,5},{8,10},{9,11},{10,... | collective-permute-start | bytes 589832 | tf_op jit(solution)/shard_map/ppermute | solution.py:292
  17.4 0.0 copy-done.6
  17.4 0.1 dynamic_slice.7
  17.5 5.1 %collective-permute-done.5 = f16[768,128]{1,0:T(8,128)(2,1)S(1)} collective-permute-done((f16[768,128]{1,0:T(8,128)(2,1)S(1)}, f16[768,128]{1,0:T(8,128)(2,1)S(1)}, u32[]{:S(2)}, u32[]{:S(2)}) %collective-permute-start.5) | collective-permute-done | bytes 196640 | tf_op jit(solution)/shard_map/ppermute | solution.py:292
  22.6 0.2 multiply_convert_fusion
  22.8 0.1 collective-permute-start.6
  22.9 1.4 %collective-permute-done.6 = bf16[768,128]{1,0:T(8,128)(2,1)S(1)} collective-permute-done((bf16[768,128]{1,0:T(8,128)(2,1)S(1)}, bf16[768,128]{1,0:T(8,128)(2,1)S(1)}, u32[]{:S(2)}, u32[]{:S(2)}) %collective-permute-start.6) | collective-permute-done | bytes 196640 | tf_op jit(solution)/shard_map/ppermute | solution.py:298
  24.4 0.8 %pad_maximum_fusion = bf16[1536,128]{1,0:T(8,128)(2,1)} fusion(bf16[768,128]{1,0:T(8,128)(2,1)S(1)} %get-tuple-element.22, bf16[768,128]{1,0:T(8,128)(2,1)S(1)} %get-tuple-element.21), kind=kLoop, calls=%fused_computation | loop fusion | flops 786432 | bytes 786432 | tf_op jit(solution)/shard_map/concatenate | solution.py:301
  (8 shorter events, 0.1 us)
Async XLA Ops:
  0.0 5.9 %copy-start.2 = (s32[1,1,86]{2,1,0:T(1,128)S(1)}, s32[1,1,86]{2,1,0:T(1,128)}, u32[]{:S(2)}) copy-start(s32[1,1,86]{2,1,0:T(1,128)} %param.11) | copy-start | bytes 1036
  0.0 5.9 %copy-start.3 = (s32[1,1,86]{2,1,0:T(1,128)S(1)}, s32[1,1,86]{2,1,0:T(1,128)}, u32[]{:S(2)}) copy-start(s32[1,1,86]{2,1,0:T(1,128)} %param.12) | copy-start | bytes 1036
  0.0 5.9 %copy-start.4 = (s32[1,1,2]{2,1,0:T(1,128)S(1)}, s32[1,1,2]{2,1,0:T(1,128)}, u32[]{:S(2)}) copy-start(s32[1,1,2]{2,1,0:T(1,128)} %param.13) | copy-start | bytes 28
  0.0 5.9 %copy-start = (s32[1,1,512,128]{3,2,1,0:T(8,128)S(1)}, s32[1,1,512,128]{3,2,1,0:T(8,128)}, u32[]{:S(2)}) copy-start(s32[1,1,512,128]{3,2,1,0:T(8,128)} %param.14) | copy-start | bytes 786436
  0.0 5.9 %copy-start.1 = (bf16[1,1,512,128]{3,2,1,0:T(8,128)(2,1)S(1)}, bf16[1,1,512,128]{3,2,1,0:T(8,128)(2,1)}, u32[]{:S(2)}) copy-start(bf16[1,1,512,128]{3,2,1,0:T(8,128)(2,1)} %param.15) | copy-start | bytes 393220
  2.8 5.5 %collective-permute-start = (bf16[2,128,128]{2,1,0:T(8,128)(2,1)S(1)}, bf16[2,128,128]{2,1,0:T(8,128)(2,1)S(1)}, u32[]{:S(2)}, u32[]{:S(2)}) collective-permute-start(bf16[2,128,128]{2,1,0:T(8,128)(2,1)S(1)} %get-tuple-element.16), channel_id=1, source_target_pairs={{0,1},{1,5},{2,3},{3,7},{4,0},{5,9},{6,2},{7,11},{8,4},{9,13},{10,... | collective-permute-start | bytes 196616 | tf_op jit(solution)/shard_map/ppermute | solution.py:233
  3.3 5.0 %collective-permute-start.1 = (bf16[2,128,128]{2,1,0:T(8,128)(2,1)S(1)}, bf16[2,128,128]{2,1,0:T(8,128)(2,1)S(1)}, u32[]{:S(2)}, u32[]{:S(2)}) collective-permute-start(bf16[2,128,128]{2,1,0:T(8,128)(2,1)S(1)} %get-tuple-element.17), channel_id=1, source_target_pairs={{1,0},{5,1},{3,2},{7,3},{0,4},{9,5},{2,6},{11,7},{4,8},{13,9},{6,1... | collective-permute-start | bytes 196616 | tf_op jit(solution)/shard_map/ppermute | solution.py:234
  8.4 4.7 %collective-permute-start.2 = (bf16[2,128,128]{2,1,0:T(8,128)(2,1)S(1)}, bf16[2,128,128]{2,1,0:T(8,128)(2,1)S(1)}, u32[]{:S(2)}, u32[]{:S(2)}) collective-permute-start(bf16[2,128,128]{2,1,0:T(8,128)(2,1)S(1)} %oblique_ratios.1.oblique_ref), channel_id=1, source_target_pairs={{0,1},{1,5},{2,3},{3,7},{4,0},{5,9},{6,2},{7,11},{8,4},{9,13},{10,... | collective-permute-start | bytes 196616 | tf_op jit(solution)/shard_map/ppermute | solution.py:257
  8.7 4.3 %collective-permute-start.3 = (bf16[2,128,128]{2,1,0:T(8,128)(2,1)S(1)}, bf16[2,128,128]{2,1,0:T(8,128)(2,1)S(1)}, u32[]{:S(2)}, u32[]{:S(2)}) collective-permute-start(bf16[2,128,128]{2,1,0:T(8,128)(2,1)S(1)} %oblique_ratios.1.oblique_ref), channel_id=1, source_target_pairs={{1,0},{5,1},{3,2},{7,3},{0,4},{9,5},{2,6},{11,7},{4,8},{13,9},{6,1... | collective-permute-start | bytes 196616 | tf_op jit(solution)/shard_map/ppermute | solution.py:258
  13.4 4.0 %copy-start.6 = (f32[1536]{0:T(1024)S(1)}, f32[1536]{0:T(1024)}, u32[]{:S(2)}) copy-start(f32[1536]{0:T(1024)} %param.9) | copy-start | bytes 18436
  13.4 9.2 %copy-start.5 = (bf16[1536,128]{1,0:T(8,128)(2,1)S(1)}, bf16[1536,128]{1,0:T(8,128)(2,1)}, u32[]{:S(2)}) copy-start(bf16[1536,128]{1,0:T(8,128)(2,1)} %activity_hbm.1) | copy-start | bytes 1179652
  13.5 1.8 %collective-permute-start.4 = (f16[768,128]{1,0:T(8,128)(2,1)S(1)}, f16[768,128]{1,0:T(8,128)(2,1)S(1)}, u32[]{:S(2)}, u32[]{:S(2)}) collective-permute-start(f16[768,128]{1,0:T(8,128)(2,1)S(1)} %convert_element_type.22), channel_id=1, source_target_pairs={{0,1},{1,0},{2,3},{3,2},{4,5},{5,4},{6,7},{7,6},{8,9},{9,8},{10,11... | collective-permute-start | bytes 589832 | tf_op jit(solution)/shard_map/ppermute | solution.py:287
  15.4 7.3 %collective-permute-start.5 = (f16[768,128]{1,0:T(8,128)(2,1)S(1)}, f16[768,128]{1,0:T(8,128)(2,1)S(1)}, u32[]{:S(2)}, u32[]{:S(2)}) collective-permute-start(f16[768,128]{1,0:T(8,128)(2,1)S(1)} %multiply_convert_fusion.1), channel_id=1, source_target_pairs={{0,2},{1,3},{2,0},{3,1},{4,6},{5,7},{6,4},{7,5},{8,10},{9,11},{10,... | collective-permute-start | bytes 589832 | tf_op jit(solution)/shard_map/ppermute | solution.py:292
  22.8 1.5 %collective-permute-start.6 = (bf16[768,128]{1,0:T(8,128)(2,1)S(1)}, bf16[768,128]{1,0:T(8,128)(2,1)S(1)}, u32[]{:S(2)}, u32[]{:S(2)}) collective-permute-start(bf16[768,128]{1,0:T(8,128)(2,1)S(1)} %multiply_convert_fusion), channel_id=1, source_target_pairs={{0,1},{1,0},{2,3},{3,2},{4,5},{5,4},{6,7},{7,6},{8,9},{9,8},{10,11... | collective-permute-start | bytes 589832 | tf_op jit(solution)/shard_map/ppermute | solution.py:298

commit v4 on v3

--- a/solution.py
+++ b/solution.py
@@ -13,7 +13,7 @@
 PART_SCALE = 256.0
 CHIP_SCALE = 128.0
 GROUP = 4
-PIECE = 8
+PIECE = 32
 
 
 def params(mebibytes=16):
@@ -112,7 +112,6 @@
 ):
     size = tiles_ref.shape[-1]
     width = (lines - own) // 2
-    half = blocks // 2
     index_tiles(voxel_ref, line_ref, slot_ref, blocks, lines)
     for j in range(width):
         order_ref[j] = rows_ref[j]
@@ -133,9 +132,9 @@
                 measured_ref[c] = measured
             else:
                 ratio_ref[start - width + c] = (measured / base).astype(ratio_ref.dtype)
-    away = (1 - lax.axis_index("angle") % 2) * half
+    away = (1 - lax.axis_index("angle") % 2) * (blocks // 2)
     for v in range(blocks):
-        voxel = away + v if v < half else half - away + v - half
+        voxel = lax.rem(away + v, blocks)
         for c in range(lines):
             line = order_ref[c] if c < own else c
             matrix_ref[v * size : (v + 1) * size, c * size : (c + 1) * size] = tile_of(
@@ -159,6 +158,17 @@
     out_ref[...] = jnp.dot(
         matrix_ref[:, : own * size], ratios, preferred_element_type=jnp.float32
     )
+
+
+def gain_kernel(size, activity_ref, sensitivity_ref, gain_ref):
+    count = gain_ref.shape[0] // size
+    first = lax.axis_index("angle") % 2 * count
+    for n in range(count):
+        at = pl.multiple_of((first + n) * size, size)
+        values = activity_ref[pl.ds(at, size)].astype(jnp.float32)
+        sens = sensitivity_ref[pl.ds(first + n, 1)]
+        gain = values / jnp.broadcast_to(sens, (size, size)).T
+        gain_ref[n * size : (n + 1) * size] = gain * (1.0 / CHIP_SCALE)
 
 
 def edge_back_kernel(slabs, own, start, scale, matrix_ref, forth_ref, back_ref, own_ref, out_ref):
@@ -175,6 +185,15 @@
         matrix_ref[start : start + rows, own * size :], ratios, preferred_element_type=jnp.float32
     )
     out_ref[...] = (sums + own_ref[start : start + rows]) * scale
+
+
+def write_rows_kernel(turn, rows_ref, *refs):
+    out_hbm, sem = refs[-2:]
+    count = rows_ref.shape[0]
+    at = pl.multiple_of((lax.axis_index("angle") + turn) % 2 * count, count)
+    copy = pltpu.make_async_copy(rows_ref, out_hbm.at[pl.ds(at, count)], sem)
+    copy.start()
+    copy.wait()
 
 
 def body(
@@ -256,6 +275,7 @@
     )(got_forth, got_back, base, taken)
     beside_forth = lax.ppermute(oblique, both, forth)
     beside_back = lax.ppermute(oblique, both, back)
+    half_rows = half * size
     own_back = pl.pallas_call(
         functools.partial(own_back_kernel, own),
         out_shape=array(jnp.float32, blocks * size, frames),
@@ -264,10 +284,16 @@
         compiler_params=params(),
         name="own_back",
     )(matrix, oblique, ratio)
-
-    half_rows = half * size
-
-    def edge_half(start, scale, name):
+    gain = pl.pallas_call(
+        functools.partial(gain_kernel, size),
+        out_shape=array(jnp.float32, half_rows, frames),
+        in_specs=[VMEM] * 2,
+        out_specs=VMEM,
+        compiler_params=params(),
+        name="gain",
+    )(activity, sensitivity.reshape(blocks, size))
+
+    def edge_rows(start, scale, name):
         return pl.pallas_call(
             functools.partial(edge_back_kernel, slabs, own, start, scale),
             out_shape=array(jnp.float32, half_rows, frames),
@@ -277,28 +303,38 @@
             name=name,
         )(matrix, beside_forth, beside_back, own_back)
 
-    odd = lax.axis_index("angle") % 2
-    mine = odd * half_rows
-    image_rows = lax.dynamic_slice_in_dim(activity, mine, half_rows, 0).astype(jnp.float32)
-    sens_rows = lax.dynamic_slice_in_dim(sensitivity, mine, half_rows, 0)
-    gain = image_rows / sens_rows[:, None]
+    def wide(values):
+        return values.astype(jnp.float32)
+
     pairs = [(a, a ^ 1) for a in range(angles)]
-    sent = edge_half(0, PART_SCALE, "edge_back_sent").astype(jnp.float16)
-    got = lax.ppermute(sent, "angle", pairs)
-    kept = edge_half(half_rows, 1.0, "edge_back_kept")
-    chip = kept + got.astype(jnp.float32) * (1.0 / PART_SCALE)
+    away = edge_rows(0, PART_SCALE, "edge_back_sent").astype(jnp.float16)
+    got = lax.ppermute(away, "angle", pairs)
+    home = edge_rows(half_rows, 1.0, "edge_back_kept")
+    chip = (home + wide(got) * (1.0 / PART_SCALE)) * CHIP_SCALE
     if angles == 4:
-        chip = (chip * CHIP_SCALE).astype(jnp.float16)
-        beside = lax.ppermute(chip, "angle", [(a, a ^ 2) for a in range(angles)])
-        total = (chip.astype(jnp.float32) + beside.astype(jnp.float32)) * (1.0 / CHIP_SCALE)
+        chip = lax.optimization_barrier(chip.astype(jnp.float16))
+        across = lax.ppermute(chip, "angle", [(a, a ^ 2) for a in range(angles)])
+        total = wide(chip) + wide(across)
     else:
         groups = [list(range(odd_one, angles, 2)) for odd_one in range(2)]
         total = lax.psum(chip, "angle", axis_index_groups=groups)
-    new_rows = (gain * total).astype(jnp.bfloat16)
-    other_rows = lax.ppermute(new_rows, "angle", pairs)
-    low = jnp.where(odd == 0, new_rows, other_rows)
-    high = jnp.where(odd == 0, other_rows, new_rows)
-    return jnp.concatenate([low, high], axis=0)
+    rows_home = lax.optimization_barrier((gain * total).astype(jnp.bfloat16))
+    rows_away = lax.ppermute(rows_home, "angle", pairs)
+
+    def write_rows(turn, name, *inputs):
+        return pl.pallas_call(
+            functools.partial(write_rows_kernel, turn),
+            out_shape=array(jnp.bfloat16, blocks * size, frames),
+            in_specs=[VMEM, HBM][: len(inputs)],
+            out_specs=HBM,
+            scratch_shapes=[pltpu.SemaphoreType.DMA],
+            input_output_aliases={1: 0} if len(inputs) > 1 else {},
+            compiler_params=params(),
+            name=name,
+        )(*inputs)
+
+    updated = write_rows(0, "write_home", rows_home)
+    return write_rows(1, "write_away", rows_away, updated)
 
 
 def solution(mesh):

time: 25.3 us -> 24.8 us (0.980)
  Pallas kernels: 6.51 us -> 7.84 us
  other arithmetic: 1.09 us -> 0.2 us
  waiting for transfers between devices: 8.92 us -> 8.12 us
    pallas_call x2 -> x5, Pallas kernels: 0.75 us -> 2.3 us  [the longest x2 1.38 us: write_rows(): pl.pallas_call(functools.partial(write_rows_kernel, turn), out_shape=arra...]
    ppermute x3, waiting for transfers between devices: 7.26 us -> 6.47 us  [the longest x1 5.06 us: body(): across = lax.ppermute(chip, 'angle', [(a, a ^ 2) for a in range(angles)])]
    concatenate x1 -> x0, other arithmetic: 0.77 us -> none  [body(): return jnp.concatenate([low, high], axis=0)]
  transfers between devices with their start and end apart: 7 -> 7, of which waited for: 4 -> 4; matrix products, arithmetic and copies ran while one was open for 0% -> 0% of each run, Pallas kernels for 13% -> 17%
where the time goes in v4:
time: 24.8 us; the launch traced here: 24.7 us
  starting transfers between devices  8.35 us (34%)
  waiting for transfers between devices  8.12 us (33%)
  Pallas kernels  7.84 us (32%)
    ppermute x1, waiting for transfers between devices, body(): across = lax.ppermute(chip, 'angle', [(a, a ^ 2) for a in range(angles)])  5.06 us
    ppermute x1, starting transfers between devices, body(): got_back = lax.ppermute(edge_back, both, back)  2.6 us
    pallas_call x1, Pallas kernels, body(): pl.pallas_call(functools.partial(edge_kernel, blocks, own, lines), out_sh...  2.5 us
    pallas_call x1, Pallas kernels, body(): pl.pallas_call(functools.partial(own_kernel, blocks, own, lines), out_sha...  2.35 us
    ppermute x1, starting transfers between devices, body(): beside_back = lax.ppermute(oblique, both, back)  2.07 us
    ppermute x1, starting transfers between devices, body(): across = lax.ppermute(chip, 'angle', [(a, a ^ 2) for a in range(angles)])  2.02 us
    ppermute x1, waiting for transfers between devices, body(): beside_forth = lax.ppermute(oblique, both, forth)  1.64 us
    pallas_call x2, Pallas kernels, write_rows(): pl.pallas_call(functools.partial(write_rows_kernel, turn), out_shape=arra...  1.38 us
  transfers between devices with their start and end apart: 7, of which 4 were waited for; matrix products, arithmetic and copies ran while one was open for 0% of the time, Pallas kernels for 17%

profile of v4, /device:TPU:0, one launch (start us, length us, event | category | flops | bytes accessed | tf_op | source)
XLA Modules:
  0.0 24.7 jit_solution(16431655409693673690)
XLA Ops:
  0.0 2.5 %edge_partials.1 = (bf16[2,128,128]{2,1,0:T(8,128)(2,1)S(1)}, bf16[2,128,128]{2,1,0:T(8,128)(2,1)S(1)}, bf16[128,1536]{1,0:T(8,128)(2,1)S(1)}, bf16[86,128,128]{2,1,0:T(8,128)(2,1)S(1)}) custom-call(s32[86]{0:T(128)} %bitcast.10, s32[86]{0:T(128)} %bitcast.12, bf16[1536,128]{1,0:T(8,128)(2,1)} %activity_hbm.1, bf16[86,128,128]{2,1,0:T(8,128)(2,1)} %bitcast.15), custom_call_target="tpu_custom_call" | custom-call | tf_op jit(solution)/shard_map/edge_partials/pallas_call | solution.py:231
  2.5 0.5 %collective-permute-start = (bf16[2,128,128]{2,1,0:T(8,128)(2,1)S(1)}, bf16[2,128,128]{2,1,0:T(8,128)(2,1)S(1)}, u32[]{:S(2)}, u32[]{:S(2)}) collective-permute-start(bf16[2,128,128]{2,1,0:T(8,128)(2,1)S(1)} %get-tuple-element.16), channel_id=1, source_target_pairs={{0,1},{1,5},{2,3},{3,7},{4,0},{5,9},{6,2},{7,11},{8,4},{9,13},{10,... | collective-permute-start | bytes 196616 | tf_op jit(solution)/shard_map/ppermute | solution.py:252
  3.0 2.6 %collective-permute-start.1 = (bf16[2,128,128]{2,1,0:T(8,128)(2,1)S(1)}, bf16[2,128,128]{2,1,0:T(8,128)(2,1)S(1)}, u32[]{:S(2)}, u32[]{:S(2)}) collective-permute-start(bf16[2,128,128]{2,1,0:T(8,128)(2,1)S(1)} %get-tuple-element.17), channel_id=1, source_target_pairs={{1,0},{5,1},{3,2},{7,3},{0,4},{9,5},{2,6},{11,7},{4,8},{13,9},{6,1... | collective-permute-start | bytes 196616 | tf_op jit(solution)/shard_map/ppermute | solution.py:253
  5.6 0.0 copy-done.4
  5.6 0.0 copy-done.5
  5.6 0.0 copy-done.6
  5.6 0.0 copy-done.1
  5.6 2.3 %own_partials.1 = (f32[2,128,128]{2,1,0:T(8,128)S(1)}, f32[2,128,128]{2,1,0:T(8,128)S(1)}, bf16[2,128,128]{2,1,0:T(8,128)(2,1)S(1)}, bf16[1536,1024]{1,0:T(8,128)(2,1)S(1)}) custom-call(s32[86]{0:T(128)S(1)} %bitcast.11, s32[86]{0:T(128)S(1)} %bitcast.13, s32[2]{0:T(128)S(1)} %bitcast.14, bf16[128,1536]{1,0:T(8,128)(2,1)S(1)} %get-tuple-element.13.image_ref, ...), custom_call_target="tpu_custom_call" | custom-call | tf_op jit(solution)/shard_map/own_partials/pallas_call | solution.py:254
  8.0 0.0 collective-permute-done.forth_ref
  8.0 0.0 collective-permute-done.1.back_ref
  8.0 0.1 oblique_ratios.1.oblique_ref
  8.1 0.3 %collective-permute-start.2 = (bf16[2,128,128]{2,1,0:T(8,128)(2,1)S(1)}, bf16[2,128,128]{2,1,0:T(8,128)(2,1)S(1)}, u32[]{:S(2)}, u32[]{:S(2)}) collective-permute-start(bf16[2,128,128]{2,1,0:T(8,128)(2,1)S(1)} %oblique_ratios.1.oblique_ref), channel_id=1, source_target_pairs={{0,1},{1,5},{2,3},{3,7},{4,0},{5,9},{6,2},{7,11},{8,4},{9,13},{10,... | collective-permute-start | bytes 196616 | tf_op jit(solution)/shard_map/ppermute | solution.py:276
  8.5 2.1 %collective-permute-start.3 = (bf16[2,128,128]{2,1,0:T(8,128)(2,1)S(1)}, bf16[2,128,128]{2,1,0:T(8,128)(2,1)S(1)}, u32[]{:S(2)}, u32[]{:S(2)}) collective-permute-start(bf16[2,128,128]{2,1,0:T(8,128)(2,1)S(1)} %oblique_ratios.1.oblique_ref), channel_id=1, source_target_pairs={{1,0},{5,1},{3,2},{7,3},{0,4},{9,5},{2,6},{11,7},{4,8},{13,9},{6,1... | collective-permute-start | bytes 196616 | tf_op jit(solution)/shard_map/ppermute | solution.py:277
  10.6 0.6 %own_back.1.own_ref = f32[1536,128]{1,0:T(8,128)S(1)} custom-call(bf16[1536,1024]{1,0:T(8,128)(2,1)S(1)} %get-tuple-element.15.matrix_ref, bf16[2,128,128]{2,1,0:T(8,128)(2,1)S(1)} %oblique_ratios.1.oblique_ref, bf16[2,128,128]{2,1,0:T(8,128)(2,1)S(1)} %get-tuple-element.20.ratio_ref), custom_call_target="tpu_custom_call" | custom-call | tf_op jit(solution)/shard_map/own_back/pallas_call | solution.py:279
  11.1 1.6 %collective-permute-done.2.forth_ref = bf16[2,128,128]{2,1,0:T(8,128)(2,1)S(1)} collective-permute-done((bf16[2,128,128]{2,1,0:T(8,128)(2,1)S(1)}, bf16[2,128,128]{2,1,0:T(8,128)(2,1)S(1)}, u32[]{:S(2)}, u32[]{:S(2)}) %collective-permute-start.2) | collective-permute-done | bytes 65568 | tf_op jit(solution)/shard_map/ppermute | solution.py:276
  12.8 0.0 collective-permute-done.3.back_ref
  12.8 0.4 %edge_back_sent.1 = f32[768,128]{1,0:T(8,128)S(1)} custom-call(bf16[1536,1024]{1,0:T(8,128)(2,1)S(1)} %get-tuple-element.15.matrix_ref, bf16[2,128,128]{2,1,0:T(8,128)(2,1)S(1)} %collective-permute-done.2.forth_ref, bf16[2,128,128]{2,1,0:T(8,128)(2,1)S(1)} %collective-permute-done.3.back_ref, f32[1536,128]{1,0:T(8,128)S(1)} %own_back.1.own_ref), custom_call_target="tpu_custom_call" | custom-call | tf_op jit(solution)/shard_map/edge_back_sent/pallas_call | solution.py:297
  13.2 0.0 copy-start
  13.2 0.0 copy-start.3
  13.2 0.8 %collective-permute-start.4 = (f16[768,128]{1,0:T(8,128)(2,1)S(1)}, f16[768,128]{1,0:T(8,128)(2,1)S(1)}, u32[]{:S(2)}, u32[]{:S(2)}) collective-permute-start(f16[768,128]{1,0:T(8,128)(2,1)S(1)} %convert_element_type.18), channel_id=1, source_target_pairs={{0,1},{1,0},{2,3},{3,2},{4,5},{5,4},{6,7},{7,6},{8,9},{9,8},{10,11... | collective-permute-start | bytes 589832 | tf_op jit(solution)/shard_map/ppermute | solution.py:311
  14.0 0.4 %edge_back_kept.1 = f32[768,128]{1,0:T(8,128)S(1)} custom-call(bf16[1536,1024]{1,0:T(8,128)(2,1)S(1)} %get-tuple-element.15.matrix_ref, bf16[2,128,128]{2,1,0:T(8,128)(2,1)S(1)} %collective-permute-done.2.forth_ref, bf16[2,128,128]{2,1,0:T(8,128)(2,1)S(1)} %collective-permute-done.3.back_ref, f32[1536,128]{1,0:T(8,128)S(1)} %own_back.1.own_ref), custom_call_target="tpu_custom_call" | custom-call | tf_op jit(solution)/shard_map/edge_back_kept/pallas_call | solution.py:297
  14.4 0.7 %collective-permute-done.4 = f16[768,128]{1,0:T(8,128)(2,1)S(1)} collective-permute-done((f16[768,128]{1,0:T(8,128)(2,1)S(1)}, f16[768,128]{1,0:T(8,128)(2,1)S(1)}, u32[]{:S(2)}, u32[]{:S(2)}) %collective-permute-start.4) | collective-permute-done | bytes 196640 | tf_op jit(solution)/shard_map/ppermute | solution.py:311
  15.0 0.1 multiply_convert_fusion.1
  15.1 2.0 %collective-permute-start.5 = (f16[768,128]{1,0:T(8,128)(2,1)S(1)}, f16[768,128]{1,0:T(8,128)(2,1)S(1)}, u32[]{:S(2)}, u32[]{:S(2)}) collective-permute-start(f16[768,128]{1,0:T(8,128)(2,1)S(1)} %multiply_convert_fusion.1), channel_id=1, source_target_pairs={{0,2},{1,3},{2,0},{3,1},{4,6},{5,7},{6,4},{7,5},{8,10},{9,11},{10,... | collective-permute-start | bytes 589832 | tf_op jit(solution)/shard_map/ppermute | solution.py:316
  17.2 0.0 copy-done.3
  17.2 0.2 gain.1
  17.3 5.1 %collective-permute-done.5 = f16[768,128]{1,0:T(8,128)(2,1)S(1)} collective-permute-done((f16[768,128]{1,0:T(8,128)(2,1)S(1)}, f16[768,128]{1,0:T(8,128)(2,1)S(1)}, u32[]{:S(2)}, u32[]{:S(2)}) %collective-permute-start.5) | collective-permute-done | bytes 196640 | tf_op jit(solution)/shard_map/ppermute | solution.py:316
  22.4 0.1 multiply_convert_fusion.rows_ref
  22.5 0.1 collective-permute-start.6
  22.6 0.7 %write_home.1.refs_0_ = bf16[1536,128]{1,0:T(8,128)(2,1)} custom-call(bf16[768,128]{1,0:T(8,128)(2,1)S(1)} %multiply_convert_fusion.rows_ref), custom_call_target="tpu_custom_call" | custom-call | tf_op jit(solution)/shard_map/write_home/pallas_call | solution.py:325
  23.3 0.7 %collective-permute-done.6.rows_ref = bf16[768,128]{1,0:T(8,128)(2,1)S(1)} collective-permute-done((bf16[768,128]{1,0:T(8,128)(2,1)S(1)}, bf16[768,128]{1,0:T(8,128)(2,1)S(1)}, u32[]{:S(2)}, u32[]{:S(2)}) %collective-permute-start.6) | collective-permute-done | bytes 196640 | tf_op jit(solution)/shard_map/ppermute | solution.py:322
  24.0 0.7 %write_away.1 = bf16[1536,128]{1,0:T(8,128)(2,1)} custom-call(bf16[768,128]{1,0:T(8,128)(2,1)S(1)} %collective-permute-done.6.rows_ref, bf16[1536,128]{1,0:T(8,128)(2,1)} %write_home.1.refs_0_), custom_call_target="tpu_custom_call", output_to_operand_aliasing={{}: (1, {})} | custom-call | tf_op jit(solution)/shard_map/write_away/pallas_call | solution.py:325
  (8 shorter events, 0.0 us)
Async XLA Ops:
  0.0 5.6 %copy-start.4 = (s32[1,1,86]{2,1,0:T(1,128)S(1)}, s32[1,1,86]{2,1,0:T(1,128)}, u32[]{:S(2)}) copy-start(s32[1,1,86]{2,1,0:T(1,128)} %param.11) | copy-start | bytes 1036
  0.0 5.6 %copy-start.5 = (s32[1,1,86]{2,1,0:T(1,128)S(1)}, s32[1,1,86]{2,1,0:T(1,128)}, u32[]{:S(2)}) copy-start(s32[1,1,86]{2,1,0:T(1,128)} %param.12) | copy-start | bytes 1036
  0.0 5.6 %copy-start.6 = (s32[1,1,2]{2,1,0:T(1,128)S(1)}, s32[1,1,2]{2,1,0:T(1,128)}, u32[]{:S(2)}) copy-start(s32[1,1,2]{2,1,0:T(1,128)} %param.13) | copy-start | bytes 28
  0.0 5.6 %copy-start.1 = (s32[1,1,512,128]{3,2,1,0:T(8,128)S(1)}, s32[1,1,512,128]{3,2,1,0:T(8,128)}, u32[]{:S(2)}) copy-start(s32[1,1,512,128]{3,2,1,0:T(8,128)} %param.14) | copy-start | bytes 786436
  0.0 5.6 %copy-start.2 = (bf16[1,1,512,128]{3,2,1,0:T(8,128)(2,1)S(1)}, bf16[1,1,512,128]{3,2,1,0:T(8,128)(2,1)}, u32[]{:S(2)}) copy-start(bf16[1,1,512,128]{3,2,1,0:T(8,128)(2,1)} %param.15) | copy-start | bytes 393220
  2.5 5.5 %collective-permute-start = (bf16[2,128,128]{2,1,0:T(8,128)(2,1)S(1)}, bf16[2,128,128]{2,1,0:T(8,128)(2,1)S(1)}, u32[]{:S(2)}, u32[]{:S(2)}) collective-permute-start(bf16[2,128,128]{2,1,0:T(8,128)(2,1)S(1)} %get-tuple-element.16), channel_id=1, source_target_pairs={{0,1},{1,5},{2,3},{3,7},{4,0},{5,9},{6,2},{7,11},{8,4},{9,13},{10,... | collective-permute-start | bytes 196616 | tf_op jit(solution)/shard_map/ppermute | solution.py:252
  3.0 5.0 %collective-permute-start.1 = (bf16[2,128,128]{2,1,0:T(8,128)(2,1)S(1)}, bf16[2,128,128]{2,1,0:T(8,128)(2,1)S(1)}, u32[]{:S(2)}, u32[]{:S(2)}) collective-permute-start(bf16[2,128,128]{2,1,0:T(8,128)(2,1)S(1)} %get-tuple-element.17), channel_id=1, source_target_pairs={{1,0},{5,1},{3,2},{7,3},{0,4},{9,5},{2,6},{11,7},{4,8},{13,9},{6,1... | collective-permute-start | bytes 196616 | tf_op jit(solution)/shard_map/ppermute | solution.py:253
  8.1 4.6 %collective-permute-start.2 = (bf16[2,128,128]{2,1,0:T(8,128)(2,1)S(1)}, bf16[2,128,128]{2,1,0:T(8,128)(2,1)S(1)}, u32[]{:S(2)}, u32[]{:S(2)}) collective-permute-start(bf16[2,128,128]{2,1,0:T(8,128)(2,1)S(1)} %oblique_ratios.1.oblique_ref), channel_id=1, source_target_pairs={{0,1},{1,5},{2,3},{3,7},{4,0},{5,9},{6,2},{7,11},{8,4},{9,13},{10,... | collective-permute-start | bytes 196616 | tf_op jit(solution)/shard_map/ppermute | solution.py:276
  8.5 4.3 %collective-permute-start.3 = (bf16[2,128,128]{2,1,0:T(8,128)(2,1)S(1)}, bf16[2,128,128]{2,1,0:T(8,128)(2,1)S(1)}, u32[]{:S(2)}, u32[]{:S(2)}) collective-permute-start(bf16[2,128,128]{2,1,0:T(8,128)(2,1)S(1)} %oblique_ratios.1.oblique_ref), channel_id=1, source_target_pairs={{1,0},{5,1},{3,2},{7,3},{0,4},{9,5},{2,6},{11,7},{4,8},{13,9},{6,1... | collective-permute-start | bytes 196616 | tf_op jit(solution)/shard_map/ppermute | solution.py:277
  13.2 4.0 %copy-start = (bf16[1536,128]{1,0:T(8,128)(2,1)S(1)}, bf16[1536,128]{1,0:T(8,128)(2,1)}, u32[]{:S(2)}) copy-start(bf16[1536,128]{1,0:T(8,128)(2,1)} %activity_hbm.1) | copy-start | bytes 1179652
  13.2 4.0 %copy-start.3 = (f32[1536]{0:T(1024)S(1)}, f32[1536]{0:T(1024)}, u32[]{:S(2)}) copy-start(f32[1536]{0:T(1024)} %param.9) | copy-start | bytes 18436
  13.2 1.8 %collective-permute-start.4 = (f16[768,128]{1,0:T(8,128)(2,1)S(1)}, f16[768,128]{1,0:T(8,128)(2,1)S(1)}, u32[]{:S(2)}, u32[]{:S(2)}) collective-permute-start(f16[768,128]{1,0:T(8,128)(2,1)S(1)} %convert_element_type.18), channel_id=1, source_target_pairs={{0,1},{1,0},{2,3},{3,2},{4,5},{5,4},{6,7},{7,6},{8,9},{9,8},{10,11... | collective-permute-start | bytes 589832 | tf_op jit(solution)/shard_map/ppermute | solution.py:311
  15.1 7.3 %collective-permute-start.5 = (f16[768,128]{1,0:T(8,128)(2,1)S(1)}, f16[768,128]{1,0:T(8,128)(2,1)S(1)}, u32[]{:S(2)}, u32[]{:S(2)}) collective-permute-start(f16[768,128]{1,0:T(8,128)(2,1)S(1)} %multiply_convert_fusion.1), channel_id=1, source_target_pairs={{0,2},{1,3},{2,0},{3,1},{4,6},{5,7},{6,4},{7,5},{8,10},{9,11},{10,... | collective-permute-start | bytes 589832 | tf_op jit(solution)/shard_map/ppermute | solution.py:316
  22.5 1.5 %collective-permute-start.6 = (bf16[768,128]{1,0:T(8,128)(2,1)S(1)}, bf16[768,128]{1,0:T(8,128)(2,1)S(1)}, u32[]{:S(2)}, u32[]{:S(2)}) collective-permute-start(bf16[768,128]{1,0:T(8,128)(2,1)S(1)} %multiply_convert_fusion.rows_ref), channel_id=1, source_target_pairs={{0,1},{1,0},{2,3},{3,2},{4,5},{5,4},{6,7},{7,6},{8,9},{9,8},{10,11... | collective-permute-start | bytes 589832 | tf_op jit(solution)/shard_map/ppermute | solution.py:322

commit v5 on v4

--- a/solution.py
+++ b/solution.py
@@ -75,8 +75,10 @@
         pieces.append(
             pltpu.make_async_copy(tiles_hbm.at[span], tiles_ref.at[span], tile_sem.at[n])
         )
-    for copy in first + pieces:
+    for copy in first:
         copy.start()
+    for copy in pieces:
+        copy.start(priority=1)
     first[0].wait()
     first[1].wait()
     index_tiles(voxel_ref, line_ref, slot_ref, blocks, lines)
@@ -187,13 +189,20 @@
     out_ref[...] = (sums + own_ref[start : start + rows]) * scale
 
 
-def write_rows_kernel(turn, rows_ref, *refs):
+def write_rows_kernel(half_rows, places, *refs):
     out_hbm, sem = refs[-2:]
-    count = rows_ref.shape[0]
-    at = pl.multiple_of((lax.axis_index("angle") + turn) % 2 * count, count)
-    copy = pltpu.make_async_copy(rows_ref, out_hbm.at[pl.ds(at, count)], sem)
-    copy.start()
-    copy.wait()
+    odd = lax.axis_index("angle") % 2
+    copies = []
+    for n, (turn, start) in enumerate(places):
+        count = refs[n].shape[0]
+        at = pl.multiple_of((odd + turn) % 2 * half_rows + start, 128)
+        copies.append(
+            pltpu.make_async_copy(refs[n], out_hbm.at[pl.ds(at, count)], sem.at[n])
+        )
+    for copy in copies:
+        copy.start()
+    for copy in copies:
+        copy.wait()
 
 
 def body(
@@ -293,10 +302,10 @@
         name="gain",
     )(activity, sensitivity.reshape(blocks, size))
 
-    def edge_rows(start, scale, name):
+    def edge_rows(start, count, scale, name):
         return pl.pallas_call(
             functools.partial(edge_back_kernel, slabs, own, start, scale),
-            out_shape=array(jnp.float32, half_rows, frames),
+            out_shape=array(jnp.float32, count, frames),
             in_specs=[VMEM] * 4,
             out_specs=VMEM,
             compiler_params=params(),
@@ -306,35 +315,48 @@
     def wide(values):
         return values.astype(jnp.float32)
 
-    pairs = [(a, a ^ 1) for a in range(angles)]
-    away = edge_rows(0, PART_SCALE, "edge_back_sent").astype(jnp.float16)
-    got = lax.ppermute(away, "angle", pairs)
-    home = edge_rows(half_rows, 1.0, "edge_back_kept")
-    chip = (home + wide(got) * (1.0 / PART_SCALE)) * CHIP_SCALE
-    if angles == 4:
-        chip = lax.optimization_barrier(chip.astype(jnp.float16))
-        across = lax.ppermute(chip, "angle", [(a, a ^ 2) for a in range(angles)])
-        total = wide(chip) + wide(across)
-    else:
-        groups = [list(range(odd_one, angles, 2)) for odd_one in range(2)]
-        total = lax.psum(chip, "angle", axis_index_groups=groups)
-    rows_home = lax.optimization_barrier((gain * total).astype(jnp.bfloat16))
-    rows_away = lax.ppermute(rows_home, "angle", pairs)
-
-    def write_rows(turn, name, *inputs):
+    def write_rows(image_now, name, *parts):
+        values = [part[0] for part in parts]
+        places = [part[1:] for part in parts]
+        before = [] if image_now is None else [image_now]
         return pl.pallas_call(
-            functools.partial(write_rows_kernel, turn),
+            functools.partial(write_rows_kernel, half_rows, places),
             out_shape=array(jnp.bfloat16, blocks * size, frames),
-            in_specs=[VMEM, HBM][: len(inputs)],
+            in_specs=[VMEM] * len(values) + [HBM] * len(before),
             out_specs=HBM,
-            scratch_shapes=[pltpu.SemaphoreType.DMA],
-            input_output_aliases={1: 0} if len(inputs) > 1 else {},
+            scratch_shapes=[pltpu.SemaphoreType.DMA((len(values),))],
+            input_output_aliases={len(values): 0} if before else {},
             compiler_params=params(),
             name=name,
-        )(*inputs)
-
-    updated = write_rows(0, "write_home", rows_home)
-    return write_rows(1, "write_away", rows_away, updated)
+        )(*values, *before)
+
+    pairs = [(a, a ^ 1) for a in range(angles)]
+    cuts = [0, half_rows // 3, half_rows]
+    away = edge_rows(0, half_rows, PART_SCALE, "edge_back_sent")
+    got = lax.ppermute(away.astype(jnp.float16), "angle", pairs)
+    home = edge_rows(half_rows, half_rows, 1.0, "edge_back_kept")
+    updated = None
+    for n, (at, end) in enumerate(zip(cuts[:-1], cuts[1:])):
+        span = slice(at, end)
+        chip = (home[span] + wide(got[span]) * (1.0 / PART_SCALE)) * CHIP_SCALE
+        if angles == 4:
+            chip = lax.optimization_barrier(chip.astype(jnp.float16))
+            across = lax.ppermute(chip, "angle", [(a, a ^ 2) for a in range(angles)])
+            if updated is not None:
+                across, updated = lax.optimization_barrier((across, updated))
+            total = wide(chip) + wide(across)
+        else:
+            groups = [list(range(odd_one, angles, 2)) for odd_one in range(2)]
+            total = lax.psum(chip, "angle", axis_index_groups=groups)
+        rows_home = (gain[span] * total).astype(jnp.bfloat16)
+        rows_home = lax.optimization_barrier(rows_home)
+        rows_away = lax.ppermute(rows_home, "angle", pairs)
+        if end < half_rows:
+            updated = write_rows(updated, f"write_{n}", (rows_home, 0, at), (rows_away, 1, at))
+        else:
+            updated = write_rows(updated, "write_home", (rows_home, 0, at))
+            updated = write_rows(updated, "write_away", (rows_away, 1, at))
+    return updated
 
 
 def solution(mesh):

time: 24.8 us -> 24.6 us (level)
  waiting for transfers between devices: 8.12 us -> 7.18 us
  Pallas kernels: 7.84 us -> 8.26 us
    ppermute x1 -> x2, waiting for transfers between devices: 5.06 us -> 3.17 us  [body(): across = lax.ppermute(chip, 'angle', [(a, a ^ 2) for a in range(angles)])]
    ppermute x1 -> x2, waiting for transfers between devices: 0.72 us -> 1.88 us  [body(): rows_away = lax.ppermute(rows_home, 'angle', pairs)]
    pallas_call x2 -> x3, Pallas kernels: 1.38 us -> 2.01 us  [write_rows(): pl.pallas_call(functools.partial(write_rows_kernel, half_rows, places), o...]
    ppermute x1 -> x2, starting transfers between devices: 2.02 us -> 2.17 us  [body(): across = lax.ppermute(chip, 'angle', [(a, a ^ 2) for a in range(angles)])]
  transfers between devices with their start and end apart: 7 -> 9, of which waited for: 4 -> 6; matrix products, arithmetic and copies ran while one was open for 0% -> 0% of each run, Pallas kernels for 17% -> 20%
where the time goes in v5:
time: 24.6 us; the launch traced here: 24.4 us
  starting transfers between devices  8.58 us (35%)
  Pallas kernels  8.26 us (34%)
  waiting for transfers between devices  7.18 us (29%)
    ppermute x2, waiting for transfers between devices, body(): across = lax.ppermute(chip, 'angle', [(a, a ^ 2) for a in range(angles)])  3.17 us
    ppermute x1, starting transfers between devices, body(): got_back = lax.ppermute(edge_back, both, back)  2.6 us
    pallas_call x1, Pallas kernels, body(): pl.pallas_call(functools.partial(own_kernel, blocks, own, lines), out_sha...  2.34 us
    pallas_call x1, Pallas kernels, body(): pl.pallas_call(functools.partial(edge_kernel, blocks, own, lines), out_sh...  2.28 us
    ppermute x2, starting transfers between devices, body(): across = lax.ppermute(chip, 'angle', [(a, a ^ 2) for a in range(angles)])  2.17 us
    ppermute x1, starting transfers between devices, body(): beside_back = lax.ppermute(oblique, both, back)  2.08 us
    pallas_call x3, Pallas kernels, write_rows(): pl.pallas_call(functools.partial(write_rows_kernel, half_rows, places), o...  2.01 us
    ppermute x2, waiting for transfers between devices, body(): rows_away = lax.ppermute(rows_home, 'angle', pairs)  1.88 us
  transfers between devices with their start and end apart: 9, of which 6 were waited for; matrix products, arithmetic and copies ran while one was open for 0% of the time, Pallas kernels for 20%

profile of v5, /device:TPU:0, one launch (start us, length us, event | category | flops | bytes accessed | tf_op | source)
XLA Modules:
  0.0 24.4 jit_solution(12132893534610591171)
XLA Ops:
  0.0 2.3 %edge_partials.1 = (bf16[2,128,128]{2,1,0:T(8,128)(2,1)S(1)}, bf16[2,128,128]{2,1,0:T(8,128)(2,1)S(1)}, bf16[128,1536]{1,0:T(8,128)(2,1)S(1)}, bf16[86,128,128]{2,1,0:T(8,128)(2,1)S(1)}) custom-call(s32[86]{0:T(128)} %bitcast.10, s32[86]{0:T(128)} %bitcast.12, bf16[1536,128]{1,0:T(8,128)(2,1)} %activity_hbm.1, bf16[86,128,128]{2,1,0:T(8,128)(2,1)} %bitcast.15), custom_call_target="tpu_custom_call" | custom-call | tf_op jit(solution)/shard_map/edge_partials/pallas_call | solution.py:240
  2.3 0.5 %collective-permute-start = (bf16[2,128,128]{2,1,0:T(8,128)(2,1)S(1)}, bf16[2,128,128]{2,1,0:T(8,128)(2,1)S(1)}, u32[]{:S(2)}, u32[]{:S(2)}) collective-permute-start(bf16[2,128,128]{2,1,0:T(8,128)(2,1)S(1)} %get-tuple-element.18), channel_id=1, source_target_pairs={{0,1},{1,5},{2,3},{3,7},{4,0},{5,9},{6,2},{7,11},{8,4},{9,13},{10,... | collective-permute-start | bytes 196616 | tf_op jit(solution)/shard_map/ppermute | solution.py:261
  2.8 2.6 %collective-permute-start.1 = (bf16[2,128,128]{2,1,0:T(8,128)(2,1)S(1)}, bf16[2,128,128]{2,1,0:T(8,128)(2,1)S(1)}, u32[]{:S(2)}, u32[]{:S(2)}) collective-permute-start(bf16[2,128,128]{2,1,0:T(8,128)(2,1)S(1)} %get-tuple-element.19), channel_id=1, source_target_pairs={{1,0},{5,1},{3,2},{7,3},{0,4},{9,5},{2,6},{11,7},{4,8},{13,9},{6,1... | collective-permute-start | bytes 196616 | tf_op jit(solution)/shard_map/ppermute | solution.py:262
  5.4 2.3 %own_partials.1 = (f32[2,128,128]{2,1,0:T(8,128)S(1)}, f32[2,128,128]{2,1,0:T(8,128)S(1)}, bf16[2,128,128]{2,1,0:T(8,128)(2,1)S(1)}, bf16[1536,1024]{1,0:T(8,128)(2,1)S(1)}) custom-call(s32[86]{0:T(128)S(1)} %bitcast.11, s32[86]{0:T(128)S(1)} %bitcast.13, s32[2]{0:T(128)S(1)} %bitcast.14, bf16[128,1536]{1,0:T(8,128)(2,1)S(1)} %get-tuple-element.15.image_ref, ...), custom_call_target="tpu_custom_call" | custom-call | tf_op jit(solution)/shard_map/own_partials/pallas_call | solution.py:263
  7.8 0.0 collective-permute-done.forth_ref
  7.8 0.0 collective-permute-done.1.back_ref
  7.8 0.1 oblique_ratios.1.oblique_ref
  7.9 0.3 %collective-permute-start.2 = (bf16[2,128,128]{2,1,0:T(8,128)(2,1)S(1)}, bf16[2,128,128]{2,1,0:T(8,128)(2,1)S(1)}, u32[]{:S(2)}, u32[]{:S(2)}) collective-permute-start(bf16[2,128,128]{2,1,0:T(8,128)(2,1)S(1)} %oblique_ratios.1.oblique_ref), channel_id=1, source_target_pairs={{0,1},{1,5},{2,3},{3,7},{4,0},{5,9},{6,2},{7,11},{8,4},{9,13},{10,... | collective-permute-start | bytes 196616 | tf_op jit(solution)/shard_map/ppermute | solution.py:285
  8.3 2.1 %collective-permute-start.3 = (bf16[2,128,128]{2,1,0:T(8,128)(2,1)S(1)}, bf16[2,128,128]{2,1,0:T(8,128)(2,1)S(1)}, u32[]{:S(2)}, u32[]{:S(2)}) collective-permute-start(bf16[2,128,128]{2,1,0:T(8,128)(2,1)S(1)} %oblique_ratios.1.oblique_ref), channel_id=1, source_target_pairs={{1,0},{5,1},{3,2},{7,3},{0,4},{9,5},{2,6},{11,7},{4,8},{13,9},{6,1... | collective-permute-start | bytes 196616 | tf_op jit(solution)/shard_map/ppermute | solution.py:286
  10.3 0.6 %own_back.1.own_ref = f32[1536,128]{1,0:T(8,128)S(1)} custom-call(bf16[1536,1024]{1,0:T(8,128)(2,1)S(1)} %get-tuple-element.17.matrix_ref, bf16[2,128,128]{2,1,0:T(8,128)(2,1)S(1)} %oblique_ratios.1.oblique_ref, bf16[2,128,128]{2,1,0:T(8,128)(2,1)S(1)} %get-tuple-element.22.ratio_ref), custom_call_target="tpu_custom_call" | custom-call | tf_op jit(solution)/shard_map/own_back/pallas_call | solution.py:288
  10.9 0.0 copy-start
  10.9 0.0 copy-start.3
  10.9 1.6 %collective-permute-done.2.forth_ref = bf16[2,128,128]{2,1,0:T(8,128)(2,1)S(1)} collective-permute-done((bf16[2,128,128]{2,1,0:T(8,128)(2,1)S(1)}, bf16[2,128,128]{2,1,0:T(8,128)(2,1)S(1)}, u32[]{:S(2)}, u32[]{:S(2)}) %collective-permute-start.2) | collective-permute-done | bytes 65568 | tf_op jit(solution)/shard_map/ppermute | solution.py:285
  12.6 0.0 collective-permute-done.3.back_ref
  12.6 0.4 %edge_back_sent.1 = f32[768,128]{1,0:T(8,128)S(1)} custom-call(bf16[1536,1024]{1,0:T(8,128)(2,1)S(1)} %get-tuple-element.17.matrix_ref, bf16[2,128,128]{2,1,0:T(8,128)(2,1)S(1)} %collective-permute-done.2.forth_ref, bf16[2,128,128]{2,1,0:T(8,128)(2,1)S(1)} %collective-permute-done.3.back_ref, f32[1536,128]{1,0:T(8,128)S(1)} %own_back.1.own_ref), custom_call_target="tpu_custom_call" | custom-call | tf_op jit(solution)/shard_map/edge_back_sent/pallas_call | solution.py:306
  13.0 0.8 %collective-permute-start.4 = (f16[768,128]{1,0:T(8,128)(2,1)S(1)}, f16[768,128]{1,0:T(8,128)(2,1)S(1)}, u32[]{:S(2)}, u32[]{:S(2)}) collective-permute-start(f16[768,128]{1,0:T(8,128)(2,1)S(1)} %convert_element_type.33), channel_id=1, source_target_pairs={{0,1},{1,0},{2,3},{3,2},{4,5},{5,4},{6,7},{7,6},{8,9},{9,8},{10,11... | collective-permute-start | bytes 589832 | tf_op jit(solution)/shard_map/ppermute | solution.py:336
  13.8 0.2 gain.1
  13.9 0.4 %edge_back_kept.1 = f32[768,128]{1,0:T(8,128)S(1)} custom-call(bf16[1536,1024]{1,0:T(8,128)(2,1)S(1)} %get-tuple-element.17.matrix_ref, bf16[2,128,128]{2,1,0:T(8,128)(2,1)S(1)} %collective-permute-done.2.forth_ref, bf16[2,128,128]{2,1,0:T(8,128)(2,1)S(1)} %collective-permute-done.3.back_ref, f32[1536,128]{1,0:T(8,128)S(1)} %own_back.1.own_ref), custom_call_target="tpu_custom_call" | custom-call | tf_op jit(solution)/shard_map/edge_back_kept/pallas_call | solution.py:306
  14.3 0.5 %collective-permute-done.4 = f16[768,128]{1,0:T(8,128)(2,1)S(1)} collective-permute-done((f16[768,128]{1,0:T(8,128)(2,1)S(1)}, f16[768,128]{1,0:T(8,128)(2,1)S(1)}, u32[]{:S(2)}, u32[]{:S(2)}) %collective-permute-start.4) | collective-permute-done | bytes 196640 | tf_op jit(solution)/shard_map/ppermute | solution.py:336
  14.9 2.0 %collective-permute-start.6 = (f16[256,128]{1,0:T(8,128)(2,1)S(1)}, f16[256,128]{1,0:T(8,128)(2,1)S(1)}, u32[]{:S(2)}, u32[]{:S(2)}) collective-permute-start(f16[256,128]{1,0:T(8,128)(2,1)S(1)} %fusion.4), channel_id=1, source_target_pairs={{0,2},{1,3},{2,0},{3,1},{4,6},{5,7},{6,4},{7,5},{8,10},{9,11},{10,... | collective-permute-start | bytes 196616 | tf_op jit(solution)/shard_map/ppermute | solution.py:344
  16.9 0.1 fusion.1
  16.9 0.1 collective-permute-start.5
  17.1 2.2 %collective-permute-done.6 = f16[256,128]{1,0:T(8,128)(2,1)S(1)} collective-permute-done((f16[256,128]{1,0:T(8,128)(2,1)S(1)}, f16[256,128]{1,0:T(8,128)(2,1)S(1)}, u32[]{:S(2)}, u32[]{:S(2)}) %collective-permute-start.6) | collective-permute-done | bytes 65568 | tf_op jit(solution)/shard_map/ppermute | solution.py:344
  19.4 0.1 collective-permute-start.7
  19.4 1.2 %collective-permute-done.7.refs_1_ = bf16[256,128]{1,0:T(8,128)(2,1)S(1)} collective-permute-done((bf16[256,128]{1,0:T(8,128)(2,1)S(1)}, bf16[256,128]{1,0:T(8,128)(2,1)S(1)}, u32[]{:S(2)}, u32[]{:S(2)}) %collective-permute-start.7) | collective-permute-done | bytes 65568 | tf_op jit(solution)/shard_map/ppermute | solution.py:353
  20.7 0.7 %write_0.1.refs_1_ = bf16[1536,128]{1,0:T(8,128)(2,1)} custom-call(bf16[256,128]{1,0:T(8,128)(2,1)S(1)} %fusion.5.refs_0_, bf16[256,128]{1,0:T(8,128)(2,1)S(1)} %collective-permute-done.7.refs_1_), custom_call_target="tpu_custom_call" | custom-call | tf_op jit(solution)/shard_map/write_0/pallas_call | solution.py:322
  21.4 0.9 %collective-permute-done.5 = f16[512,128]{1,0:T(8,128)(2,1)S(1)} collective-permute-done((f16[512,128]{1,0:T(8,128)(2,1)S(1)}, f16[512,128]{1,0:T(8,128)(2,1)S(1)}, u32[]{:S(2)}, u32[]{:S(2)}) %collective-permute-start.5) | collective-permute-done | bytes 131104 | tf_op jit(solution)/shard_map/ppermute | solution.py:344
  22.3 0.1 fusion.2.refs_0_
  22.3 0.1 collective-permute-start.8
  22.4 0.7 %write_home.1.refs_1_ = bf16[1536,128]{1,0:T(8,128)(2,1)} custom-call(bf16[512,128]{1,0:T(8,128)(2,1)S(1)} %fusion.2.refs_0_, bf16[1536,128]{1,0:T(8,128)(2,1)} %write_0.1.refs_1_), custom_call_target="tpu_custom_call", output_to_operand_aliasing={{}: (1, {})} | custom-call | tf_op jit(solution)/shard_map/write_home/pallas_call | solution.py:322
  23.1 0.6 %collective-permute-done.8.refs_0_ = bf16[512,128]{1,0:T(8,128)(2,1)S(1)} collective-permute-done((bf16[512,128]{1,0:T(8,128)(2,1)S(1)}, bf16[512,128]{1,0:T(8,128)(2,1)S(1)}, u32[]{:S(2)}, u32[]{:S(2)}) %collective-permute-start.8) | collective-permute-done | bytes 131104 | tf_op jit(solution)/shard_map/ppermute | solution.py:353
  23.8 0.7 %write_away.1 = bf16[1536,128]{1,0:T(8,128)(2,1)} custom-call(bf16[512,128]{1,0:T(8,128)(2,1)S(1)} %collective-permute-done.8.refs_0_, bf16[1536,128]{1,0:T(8,128)(2,1)} %write_home.1.refs_1_), custom_call_target="tpu_custom_call", output_to_operand_aliasing={{}: (1, {})} | custom-call | tf_op jit(solution)/shard_map/write_away/pallas_call | solution.py:322
  (15 shorter events, 0.1 us)
Async XLA Ops:
  0.0 5.4 %copy-start.4 = (s32[1,1,86]{2,1,0:T(1,128)S(1)}, s32[1,1,86]{2,1,0:T(1,128)}, u32[]{:S(2)}) copy-start(s32[1,1,86]{2,1,0:T(1,128)} %param.11) | copy-start | bytes 1036
  0.0 5.4 %copy-start.5 = (s32[1,1,86]{2,1,0:T(1,128)S(1)}, s32[1,1,86]{2,1,0:T(1,128)}, u32[]{:S(2)}) copy-start(s32[1,1,86]{2,1,0:T(1,128)} %param.12) | copy-start | bytes 1036
  0.0 5.4 %copy-start.6 = (s32[1,1,2]{2,1,0:T(1,128)S(1)}, s32[1,1,2]{2,1,0:T(1,128)}, u32[]{:S(2)}) copy-start(s32[1,1,2]{2,1,0:T(1,128)} %param.13) | copy-start | bytes 28
  0.0 5.4 %copy-start.1 = (s32[1,1,512,128]{3,2,1,0:T(8,128)S(1)}, s32[1,1,512,128]{3,2,1,0:T(8,128)}, u32[]{:S(2)}) copy-start(s32[1,1,512,128]{3,2,1,0:T(8,128)} %param.14) | copy-start | bytes 786436
  0.0 5.4 %copy-start.2 = (bf16[1,1,512,128]{3,2,1,0:T(8,128)(2,1)S(1)}, bf16[1,1,512,128]{3,2,1,0:T(8,128)(2,1)}, u32[]{:S(2)}) copy-start(bf16[1,1,512,128]{3,2,1,0:T(8,128)(2,1)} %param.15) | copy-start | bytes 393220
  2.3 5.5 %collective-permute-start = (bf16[2,128,128]{2,1,0:T(8,128)(2,1)S(1)}, bf16[2,128,128]{2,1,0:T(8,128)(2,1)S(1)}, u32[]{:S(2)}, u32[]{:S(2)}) collective-permute-start(bf16[2,128,128]{2,1,0:T(8,128)(2,1)S(1)} %get-tuple-element.18), channel_id=1, source_target_pairs={{0,1},{1,5},{2,3},{3,7},{4,0},{5,9},{6,2},{7,11},{8,4},{9,13},{10,... | collective-permute-start | bytes 196616 | tf_op jit(solution)/shard_map/ppermute | solution.py:261
  2.8 5.0 %collective-permute-start.1 = (bf16[2,128,128]{2,1,0:T(8,128)(2,1)S(1)}, bf16[2,128,128]{2,1,0:T(8,128)(2,1)S(1)}, u32[]{:S(2)}, u32[]{:S(2)}) collective-permute-start(bf16[2,128,128]{2,1,0:T(8,128)(2,1)S(1)} %get-tuple-element.19), channel_id=1, source_target_pairs={{1,0},{5,1},{3,2},{7,3},{0,4},{9,5},{2,6},{11,7},{4,8},{13,9},{6,1... | collective-permute-start | bytes 196616 | tf_op jit(solution)/shard_map/ppermute | solution.py:262
  7.9 4.6 %collective-permute-start.2 = (bf16[2,128,128]{2,1,0:T(8,128)(2,1)S(1)}, bf16[2,128,128]{2,1,0:T(8,128)(2,1)S(1)}, u32[]{:S(2)}, u32[]{:S(2)}) collective-permute-start(bf16[2,128,128]{2,1,0:T(8,128)(2,1)S(1)} %oblique_ratios.1.oblique_ref), channel_id=1, source_target_pairs={{0,1},{1,5},{2,3},{3,7},{4,0},{5,9},{6,2},{7,11},{8,4},{9,13},{10,... | collective-permute-start | bytes 196616 | tf_op jit(solution)/shard_map/ppermute | solution.py:285
  8.3 4.3 %collective-permute-start.3 = (bf16[2,128,128]{2,1,0:T(8,128)(2,1)S(1)}, bf16[2,128,128]{2,1,0:T(8,128)(2,1)S(1)}, u32[]{:S(2)}, u32[]{:S(2)}) collective-permute-start(bf16[2,128,128]{2,1,0:T(8,128)(2,1)S(1)} %oblique_ratios.1.oblique_ref), channel_id=1, source_target_pairs={{1,0},{5,1},{3,2},{7,3},{0,4},{9,5},{2,6},{11,7},{4,8},{13,9},{6,1... | collective-permute-start | bytes 196616 | tf_op jit(solution)/shard_map/ppermute | solution.py:286
  10.9 2.8 %copy-start = (bf16[1536,128]{1,0:T(8,128)(2,1)S(1)}, bf16[1536,128]{1,0:T(8,128)(2,1)}, u32[]{:S(2)}) copy-start(bf16[1536,128]{1,0:T(8,128)(2,1)} %activity_hbm.1) | copy-start | bytes 1179652
  10.9 2.8 %copy-start.3 = (f32[1536]{0:T(1024)S(1)}, f32[1536]{0:T(1024)}, u32[]{:S(2)}) copy-start(f32[1536]{0:T(1024)} %param.9) | copy-start | bytes 18436
  13.0 1.8 %collective-permute-start.4 = (f16[768,128]{1,0:T(8,128)(2,1)S(1)}, f16[768,128]{1,0:T(8,128)(2,1)S(1)}, u32[]{:S(2)}, u32[]{:S(2)}) collective-permute-start(f16[768,128]{1,0:T(8,128)(2,1)S(1)} %convert_element_type.33), channel_id=1, source_target_pairs={{0,1},{1,0},{2,3},{3,2},{4,5},{5,4},{6,7},{7,6},{8,9},{9,8},{10,11... | collective-permute-start | bytes 589832 | tf_op jit(solution)/shard_map/ppermute | solution.py:336
  14.9 4.5 %collective-permute-start.6 = (f16[256,128]{1,0:T(8,128)(2,1)S(1)}, f16[256,128]{1,0:T(8,128)(2,1)S(1)}, u32[]{:S(2)}, u32[]{:S(2)}) collective-permute-start(f16[256,128]{1,0:T(8,128)(2,1)S(1)} %fusion.4), channel_id=1, source_target_pairs={{0,2},{1,3},{2,0},{3,1},{4,6},{5,7},{6,4},{7,5},{8,10},{9,11},{10,... | collective-permute-start | bytes 196616 | tf_op jit(solution)/shard_map/ppermute | solution.py:344
  16.9 5.3 %collective-permute-start.5 = (f16[512,128]{1,0:T(8,128)(2,1)S(1)}, f16[512,128]{1,0:T(8,128)(2,1)S(1)}, u32[]{:S(2)}, u32[]{:S(2)}) collective-permute-start(f16[512,128]{1,0:T(8,128)(2,1)S(1)} %fusion.1), channel_id=1, source_target_pairs={{0,2},{1,3},{2,0},{3,1},{4,6},{5,7},{6,4},{7,5},{8,10},{9,11},{10,... | collective-permute-start | bytes 393224 | tf_op jit(solution)/shard_map/ppermute | solution.py:344
  19.4 1.3 %collective-permute-start.7 = (bf16[256,128]{1,0:T(8,128)(2,1)S(1)}, bf16[256,128]{1,0:T(8,128)(2,1)S(1)}, u32[]{:S(2)}, u32[]{:S(2)}) collective-permute-start(bf16[256,128]{1,0:T(8,128)(2,1)S(1)} %fusion.5.refs_0_), channel_id=1, source_target_pairs={{0,1},{1,0},{2,3},{3,2},{4,5},{5,4},{6,7},{7,6},{8,9},{9,8},{10,11... | collective-permute-start | bytes 196616 | tf_op jit(solution)/shard_map/ppermute | solution.py:353
  22.3 1.4 %collective-permute-start.8 = (bf16[512,128]{1,0:T(8,128)(2,1)S(1)}, bf16[512,128]{1,0:T(8,128)(2,1)S(1)}, u32[]{:S(2)}, u32[]{:S(2)}) collective-permute-start(bf16[512,128]{1,0:T(8,128)(2,1)S(1)} %fusion.2.refs_0_), channel_id=1, source_target_pairs={{0,1},{1,0},{2,3},{3,2},{4,5},{5,4},{6,7},{7,6},{8,9},{9,8},{10,11... | collective-permute-start | bytes 393224 | tf_op jit(solution)/shard_map/ppermute | solution.py:353

commit v6 on v5

--- a/solution.py
+++ b/solution.py
@@ -14,6 +14,7 @@
 CHIP_SCALE = 128.0
 GROUP = 4
 PIECE = 32
+FIRST_PART = 11
 
 
 def params(mebibytes=16):
@@ -110,7 +111,8 @@
 
 def own_kernel(
     blocks, own, lines, voxel_ref, line_ref, rows_ref, image_ref, tiles_ref, counts_ref,
-    background_ref, base_ref, measured_ref, ratio_ref, matrix_ref, slot_ref, order_ref,
+    background_ref, activity_ref, sensitivity_ref, base_ref, measured_ref, ratio_ref, matrix_ref,
+    gain_ref, slot_ref, order_ref,
 ):
     size = tiles_ref.shape[-1]
     width = (lines - own) // 2
@@ -142,6 +144,7 @@
             matrix_ref[v * size : (v + 1) * size, c * size : (c + 1) * size] = tile_of(
                 tiles_ref, slot_ref, voxel, line, lines
             )
+    fill_gain(size, activity_ref, sensitivity_ref, gain_ref)
 
 
 def oblique_kernel(slabs, forth_ref, back_ref, base_ref, measured_ref, out_ref):
@@ -162,7 +165,7 @@
     )
 
 
-def gain_kernel(size, activity_ref, sensitivity_ref, gain_ref):
+def fill_gain(size, activity_ref, sensitivity_ref, gain_ref):
     count = gain_ref.shape[0] // size
     first = lax.axis_index("angle") % 2 * count
     for n in range(count):
@@ -173,7 +176,7 @@
         gain_ref[n * size : (n + 1) * size] = gain * (1.0 / CHIP_SCALE)
 
 
-def edge_back_kernel(slabs, own, start, scale, matrix_ref, forth_ref, back_ref, own_ref, out_ref):
+def edge_back_kernel(slabs, own, start, scale, matrix_ref, back_ref, forth_ref, own_ref, out_ref):
     size = forth_ref.shape[1]
     rows = out_ref.shape[0]
     odd, has_forth, has_back = place(slabs)
@@ -195,7 +198,7 @@
     copies = []
     for n, (turn, start) in enumerate(places):
         count = refs[n].shape[0]
-        at = pl.multiple_of((odd + turn) % 2 * half_rows + start, 128)
+        at = pl.multiple_of((odd + turn) % 2 * half_rows + start, 32)
         copies.append(
             pltpu.make_async_copy(refs[n], out_hbm.at[pl.ds(at, count)], sem.at[n])
         )
@@ -260,20 +263,25 @@
     )(*[pltpu.with_memory_space_constraint(a, pltpu.HBM) for a in (voxel, line, activity, tiles)])
     got_forth = lax.ppermute(edge_forth, both, forth)
     got_back = lax.ppermute(edge_back, both, back)
-    base, taken, ratio, matrix = pl.pallas_call(
+    half_rows = half * size
+    base, taken, ratio, matrix, gain = pl.pallas_call(
         functools.partial(own_kernel, blocks, own, lines),
         out_shape=(
             array(jnp.float32, width, size, frames),
             array(jnp.float32, width, size, frames),
             array(jnp.bfloat16, own - width, size, frames),
             array(jnp.bfloat16, blocks * size, lines * size),
+            array(jnp.float32, half_rows, frames),
         ),
-        in_specs=[SMEM] * 3 + [VMEM] * 4,
-        out_specs=(VMEM,) * 4,
+        in_specs=[SMEM] * 3 + [VMEM] * 6,
+        out_specs=(VMEM,) * 5,
         scratch_shapes=[slots, pltpu.SMEM((own + 1,), jnp.int32)],
         compiler_params=params(),
         name="own_partials",
-    )(voxel, line, rows, image, held, measured, additive)
+    )(
+        voxel, line, rows, image, held, measured, additive, activity,
+        sensitivity.reshape(blocks, size),
+    )
     oblique = pl.pallas_call(
         functools.partial(oblique_kernel, slabs),
         out_shape=array(jnp.bfloat16, width, size, frames),
@@ -284,7 +292,6 @@
     )(got_forth, got_back, base, taken)
     beside_forth = lax.ppermute(oblique, both, forth)
     beside_back = lax.ppermute(oblique, both, back)
-    half_rows = half * size
     own_back = pl.pallas_call(
         functools.partial(own_back_kernel, own),
         out_shape=array(jnp.float32, blocks * size, frames),
@@ -293,16 +300,8 @@
         compiler_params=params(),
         name="own_back",
     )(matrix, oblique, ratio)
-    gain = pl.pallas_call(
-        functools.partial(gain_kernel, size),
-        out_shape=array(jnp.float32, half_rows, frames),
-        in_specs=[VMEM] * 2,
-        out_specs=VMEM,
-        compiler_params=params(),
-        name="gain",
-    )(activity, sensitivity.reshape(blocks, size))
-
-    def edge_rows(start, count, scale, name):
+
+    def edge_rows(start, count, scale, name, after=None):
         return pl.pallas_call(
             functools.partial(edge_back_kernel, slabs, own, start, scale),
             out_shape=array(jnp.float32, count, frames),
@@ -310,7 +309,7 @@
             out_specs=VMEM,
             compiler_params=params(),
             name=name,
-        )(matrix, beside_forth, beside_back, own_back)
+        )(matrix, beside_back if after is None else after, beside_forth, own_back)
 
     def wide(values):
         return values.astype(jnp.float32)
@@ -331,14 +330,19 @@
         )(*values, *before)
 
     pairs = [(a, a ^ 1) for a in range(angles)]
-    cuts = [0, half_rows // 3, half_rows]
-    away = edge_rows(0, half_rows, PART_SCALE, "edge_back_sent")
-    got = lax.ppermute(away.astype(jnp.float16), "angle", pairs)
-    home = edge_rows(half_rows, half_rows, 1.0, "edge_back_kept")
+    cuts = [0, FIRST_PART * half_rows // 24, half_rows]
+    cuts = [0, FIRST_PART * half_rows // 24, half_rows]
+    spans = [slice(at, end) for at, end in zip(cuts[:-1], cuts[1:])]
+    got = []
+    for n, span in enumerate(spans):
+        away = edge_rows(span.start, span.stop - span.start, PART_SCALE, f"edge_back_sent_{n}")
+        got.append(lax.ppermute(away.astype(jnp.float16), "angle", pairs))
     updated = None
     for n, (at, end) in enumerate(zip(cuts[:-1], cuts[1:])):
-        span = slice(at, end)
-        chip = (home[span] + wide(got[span]) * (1.0 / PART_SCALE)) * CHIP_SCALE
+        span = spans[n]
+        after, got[n] = lax.optimization_barrier((beside_back, got[n])) if n else (None, got[n])
+        home = edge_rows(half_rows + at, end - at, 1.0, f"edge_back_kept_{n}", after)
+        chip = (home + wide(got[n]) * (1.0 / PART_SCALE)) * CHIP_SCALE
         if angles == 4:
             chip = lax.optimization_barrier(chip.astype(jnp.float16))
             across = lax.ppermute(chip, "angle", [(a, a ^ 2) for a in range(angles)])

time: 24.6 us -> 24.1 us (0.980)
  waiting for transfers between devices: 7.18 us -> 6.22 us
  starting transfers between devices: 8.58 us -> 9.03 us
    ppermute x2, waiting for transfers between devices: 3.17 us -> 2.29 us  [body(): across = lax.ppermute(chip, 'angle', [(a, a ^ 2) for a in range(angles)])]
    ppermute x2, starting transfers between devices: 2.17 us -> 2.51 us  [body(): across = lax.ppermute(chip, 'angle', [(a, a ^ 2) for a in range(angles)])]
    pallas_call x2 -> x4, Pallas kernels: 0.76 us -> 1.08 us  [edge_rows(): pl.pallas_call(functools.partial(edge_back_kernel, slabs, own, start, sca...]
    ppermute x1 -> x2, waiting for transfers between devices: 0.5 us -> 0.27 us  [body(): got.append(lax.ppermute(away.astype(jnp.float16), 'angle', pairs))]
    ppermute x1 -> x2, starting transfers between devices: 0.76 us -> 0.85 us  [body(): got.append(lax.ppermute(away.astype(jnp.float16), 'angle', pairs))]
  transfers between devices with their start and end apart: 9 -> 10, of which waited for: 6 -> 7; matrix products, arithmetic and copies ran while one was open for 0% -> 1% of each run, Pallas kernels for 20% -> 21%
where the time goes in v6:
time: 24.1 us; the launch traced here: 23.9 us
  starting transfers between devices  9.03 us (37%)
  Pallas kernels  8.25 us (34%)
  waiting for transfers between devices  6.22 us (26%)
    ppermute x1, starting transfers between devices, body(): got_back = lax.ppermute(edge_back, both, back)  2.6 us
    ppermute x2, starting transfers between devices, body(): across = lax.ppermute(chip, 'angle', [(a, a ^ 2) for a in range(angles)])  2.51 us
    ppermute x2, waiting for transfers between devices, body(): across = lax.ppermute(chip, 'angle', [(a, a ^ 2) for a in range(angles)])  2.29 us
    pallas_call x1, Pallas kernels, body(): pl.pallas_call(functools.partial(edge_kernel, blocks, own, lines), out_sh...  2.28 us
    pallas_call x1, Pallas kernels, body(): pl.pallas_call(functools.partial(own_kernel, blocks, own, lines), out_sha...  2.2 us
    ppermute x1, starting transfers between devices, body(): beside_back = lax.ppermute(oblique, both, back)  2.08 us
    pallas_call x3, Pallas kernels, write_rows(): pl.pallas_call(functools.partial(write_rows_kernel, half_rows, places), o...  2.01 us
    ppermute x2, waiting for transfers between devices, body(): rows_away = lax.ppermute(rows_home, 'angle', pairs)  1.89 us
  transfers between devices with their start and end apart: 10, of which 7 were waited for; matrix products, arithmetic and copies ran while one was open for 1% of the time, Pallas kernels for 21%

profile of v6, /device:TPU:0, one launch (start us, length us, event | category | flops | bytes accessed | tf_op | source)
XLA Modules:
  0.0 23.9 jit_solution(10332257873963452422)
XLA Ops:
  0.0 2.3 %edge_partials.1 = (bf16[2,128,128]{2,1,0:T(8,128)(2,1)S(1)}, bf16[2,128,128]{2,1,0:T(8,128)(2,1)S(1)}, bf16[128,1536]{1,0:T(8,128)(2,1)S(1)}, bf16[86,128,128]{2,1,0:T(8,128)(2,1)S(1)}) custom-call(s32[86]{0:T(128)} %bitcast.10, s32[86]{0:T(128)} %bitcast.12, bf16[1536,128]{1,0:T(8,128)(2,1)} %activity_ref.1, bf16[86,128,128]{2,1,0:T(8,128)(2,1)} %bitcast.15), custom_call_target="tpu_custom_call" | custom-call | tf_op jit(solution)/shard_map/edge_partials/pallas_call | solution.py:243
  2.3 0.5 %collective-permute-start = (bf16[2,128,128]{2,1,0:T(8,128)(2,1)S(1)}, bf16[2,128,128]{2,1,0:T(8,128)(2,1)S(1)}, u32[]{:S(2)}, u32[]{:S(2)}) collective-permute-start(bf16[2,128,128]{2,1,0:T(8,128)(2,1)S(1)} %get-tuple-element.22), channel_id=1, source_target_pairs={{0,1},{1,5},{2,3},{3,7},{4,0},{5,9},{6,2},{7,11},{8,4},{9,13},{10,... | collective-permute-start | bytes 196616 | tf_op jit(solution)/shard_map/ppermute | solution.py:264
  2.8 2.6 %collective-permute-start.1 = (bf16[2,128,128]{2,1,0:T(8,128)(2,1)S(1)}, bf16[2,128,128]{2,1,0:T(8,128)(2,1)S(1)}, u32[]{:S(2)}, u32[]{:S(2)}) collective-permute-start(bf16[2,128,128]{2,1,0:T(8,128)(2,1)S(1)} %get-tuple-element.23), channel_id=1, source_target_pairs={{1,0},{5,1},{3,2},{7,3},{0,4},{9,5},{2,6},{11,7},{4,8},{13,9},{6,1... | collective-permute-start | bytes 196616 | tf_op jit(solution)/shard_map/ppermute | solution.py:265
  5.4 0.0 copy-done.2
  5.5 2.2 %own_partials.1 = (f32[2,128,128]{2,1,0:T(8,128)S(1)}, f32[2,128,128]{2,1,0:T(8,128)S(1)}, bf16[2,128,128]{2,1,0:T(8,128)(2,1)S(1)}, bf16[1536,1024]{1,0:T(8,128)(2,1)S(1)}, f32[768,128]{1,0:T(8,128)S(1)}) custom-call(s32[86]{0:T(128)S(1)} %bitcast.11, s32[86]{0:T(128)S(1)} %bitcast.13, s32[2]{0:T(128)S(1)} %bitcast.14, ...), custom_call_target="tpu_custom_call" | custom-call | tf_op jit(solution)/shard_map/own_partials/pallas_call | solution.py:267
  7.7 0.1 collective-permute-done.forth_ref
  7.8 0.0 collective-permute-done.1.back_ref
  7.8 0.1 oblique_ratios.1.oblique_ref
  7.9 0.4 %collective-permute-start.3 = (bf16[2,128,128]{2,1,0:T(8,128)(2,1)S(1)}, bf16[2,128,128]{2,1,0:T(8,128)(2,1)S(1)}, u32[]{:S(2)}, u32[]{:S(2)}) collective-permute-start(bf16[2,128,128]{2,1,0:T(8,128)(2,1)S(1)} %oblique_ratios.1.oblique_ref), channel_id=1, source_target_pairs={{0,1},{1,5},{2,3},{3,7},{4,0},{5,9},{6,2},{7,11},{8,4},{9,13},{10,... | collective-permute-start | bytes 196616 | tf_op jit(solution)/shard_map/ppermute | solution.py:293
  8.3 2.1 %collective-permute-start.2 = (bf16[2,128,128]{2,1,0:T(8,128)(2,1)S(1)}, bf16[2,128,128]{2,1,0:T(8,128)(2,1)S(1)}, u32[]{:S(2)}, u32[]{:S(2)}) collective-permute-start(bf16[2,128,128]{2,1,0:T(8,128)(2,1)S(1)} %oblique_ratios.1.oblique_ref), channel_id=1, source_target_pairs={{1,0},{5,1},{3,2},{7,3},{0,4},{9,5},{2,6},{11,7},{4,8},{13,9},{6,1... | collective-permute-start | bytes 196616 | tf_op jit(solution)/shard_map/ppermute | solution.py:294
  10.4 0.6 %own_back.1.own_ref = f32[1536,128]{1,0:T(8,128)S(1)} custom-call(bf16[1536,1024]{1,0:T(8,128)(2,1)S(1)} %get-tuple-element.21.matrix_ref, bf16[2,128,128]{2,1,0:T(8,128)(2,1)S(1)} %oblique_ratios.1.oblique_ref, bf16[2,128,128]{2,1,0:T(8,128)(2,1)S(1)} %get-tuple-element.26.ratio_ref), custom_call_target="tpu_custom_call" | custom-call | tf_op jit(solution)/shard_map/own_back/pallas_call | solution.py:295
  10.9 1.6 %collective-permute-done.3.forth_ref = bf16[2,128,128]{2,1,0:T(8,128)(2,1)S(1)} collective-permute-done((bf16[2,128,128]{2,1,0:T(8,128)(2,1)S(1)}, bf16[2,128,128]{2,1,0:T(8,128)(2,1)S(1)}, u32[]{:S(2)}, u32[]{:S(2)}) %collective-permute-start.3) | collective-permute-done | bytes 65568 | tf_op jit(solution)/shard_map/ppermute | solution.py:293
  12.6 0.0 collective-permute-done.2.back_ref
  12.6 0.3 %edge_back_sent_0.1 = f32[352,128]{1,0:T(8,128)S(1)} custom-call(bf16[1536,1024]{1,0:T(8,128)(2,1)S(1)} %get-tuple-element.21.matrix_ref, bf16[2,128,128]{2,1,0:T(8,128)(2,1)S(1)} %collective-permute-done.2.back_ref, bf16[2,128,128]{2,1,0:T(8,128)(2,1)S(1)} %collective-permute-done.3.forth_ref, f32[1536,128]{1,0:T(8,128)S(1)} %own_back.1.own_ref), custom_call_target="tpu_custom_call" | custom-call | tf_op jit(solution)/shard_map/edge_back_sent_0/pallas_call | solution.py:305
  12.9 0.7 %collective-permute-start.6 = (f16[352,128]{1,0:T(8,128)(2,1)S(1)}, f16[352,128]{1,0:T(8,128)(2,1)S(1)}, u32[]{:S(2)}, u32[]{:S(2)}) collective-permute-start(f16[352,128]{1,0:T(8,128)(2,1)S(1)} %convert_element_type.40), channel_id=1, source_target_pairs={{0,1},{1,0},{2,3},{3,2},{4,5},{5,4},{6,7},{7,6},{8,9},{9,8},{10,11... | collective-permute-start | bytes 270344 | tf_op jit(solution)/shard_map/ppermute | solution.py:339
  13.6 0.3 %edge_back_sent_1.1 = f32[416,128]{1,0:T(8,128)S(1)} custom-call(bf16[1536,1024]{1,0:T(8,128)(2,1)S(1)} %get-tuple-element.21.matrix_ref, bf16[2,128,128]{2,1,0:T(8,128)(2,1)S(1)} %collective-permute-done.2.back_ref, bf16[2,128,128]{2,1,0:T(8,128)(2,1)S(1)} %collective-permute-done.3.forth_ref, f32[1536,128]{1,0:T(8,128)S(1)} %own_back.1.own_ref), custom_call_target="tpu_custom_call" | custom-call | tf_op jit(solution)/shard_map/edge_back_sent_1/pallas_call | solution.py:305
  13.9 0.1 collective-permute-start.4
  14.0 0.3 %edge_back_kept_0.1 = f32[352,128]{1,0:T(8,128)S(1)} custom-call(bf16[1536,1024]{1,0:T(8,128)(2,1)S(1)} %get-tuple-element.21.matrix_ref, bf16[2,128,128]{2,1,0:T(8,128)(2,1)S(1)} %collective-permute-done.2.back_ref, bf16[2,128,128]{2,1,0:T(8,128)(2,1)S(1)} %collective-permute-done.3.forth_ref, f32[1536,128]{1,0:T(8,128)S(1)} %own_back.1.own_ref), custom_call_target="tpu_custom_call" | custom-call | tf_op jit(solution)/shard_map/edge_back_kept_0/pallas_call | solution.py:305
  14.3 0.3 %collective-permute-done.6 = f16[352,128]{1,0:T(8,128)(2,1)S(1)} collective-permute-done((f16[352,128]{1,0:T(8,128)(2,1)S(1)}, f16[352,128]{1,0:T(8,128)(2,1)S(1)}, u32[]{:S(2)}, u32[]{:S(2)}) %collective-permute-start.6) | collective-permute-done | bytes 90144 | tf_op jit(solution)/shard_map/ppermute | solution.py:339
  14.6 2.0 %collective-permute-start.7 = (f16[352,128]{1,0:T(8,128)(2,1)S(1)}, f16[352,128]{1,0:T(8,128)(2,1)S(1)}, u32[]{:S(2)}, u32[]{:S(2)}) collective-permute-start(f16[352,128]{1,0:T(8,128)(2,1)S(1)} %multiply_convert_fusion.3), channel_id=1, source_target_pairs={{0,2},{1,3},{2,0},{3,1},{4,6},{5,7},{6,4},{7,5},{8,10},{9,11},{10,... | collective-permute-start | bytes 270344 | tf_op jit(solution)/shard_map/ppermute | solution.py:348
  16.6 0.0 collective-permute-done.4
  16.6 0.3 %edge_back_kept_1.1 = f32[416,128]{1,0:T(8,128)S(1)} custom-call(bf16[1536,1024]{1,0:T(8,128)(2,1)S(1)} %get-tuple-element.21.matrix_ref, bf16[2,128,128]{2,1,0:T(8,128)(2,1)S(1)} %collective-permute-done.2.back_ref, bf16[2,128,128]{2,1,0:T(8,128)(2,1)S(1)} %collective-permute-done.3.forth_ref, f32[1536,128]{1,0:T(8,128)S(1)} %own_back.1.own_ref), custom_call_target="tpu_custom_call" | custom-call | tf_op jit(solution)/shard_map/edge_back_kept_1/pallas_call | solution.py:305
  17.0 0.5 %collective-permute-start.5 = (f16[416,128]{1,0:T(8,128)(2,1)S(1)}, f16[416,128]{1,0:T(8,128)(2,1)S(1)}, u32[]{:S(2)}, u32[]{:S(2)}) collective-permute-start(f16[416,128]{1,0:T(8,128)(2,1)S(1)} %multiply_convert_fusion.1), channel_id=1, source_target_pairs={{0,2},{1,3},{2,0},{3,1},{4,6},{5,7},{6,4},{7,5},{8,10},{9,11},{10,... | collective-permute-start | bytes 319496 | tf_op jit(solution)/shard_map/ppermute | solution.py:348
  17.5 2.1 %collective-permute-done.7 = f16[352,128]{1,0:T(8,128)(2,1)S(1)} collective-permute-done((f16[352,128]{1,0:T(8,128)(2,1)S(1)}, f16[352,128]{1,0:T(8,128)(2,1)S(1)}, u32[]{:S(2)}, u32[]{:S(2)}) %collective-permute-start.7) | collective-permute-done | bytes 90144 | tf_op jit(solution)/shard_map/ppermute | solution.py:348
  19.6 0.1 collective-permute-start.8
  19.7 1.3 %collective-permute-done.8.refs_1_ = bf16[352,128]{1,0:T(8,128)(2,1)S(1)} collective-permute-done((bf16[352,128]{1,0:T(8,128)(2,1)S(1)}, bf16[352,128]{1,0:T(8,128)(2,1)S(1)}, u32[]{:S(2)}, u32[]{:S(2)}) %collective-permute-start.8) | collective-permute-done | bytes 90144 | tf_op jit(solution)/shard_map/ppermute | solution.py:357
  21.0 0.7 %write_0.1.refs_1_ = bf16[1536,128]{1,0:T(8,128)(2,1)} custom-call(bf16[352,128]{1,0:T(8,128)(2,1)S(1)} %multiply_convert_fusion.2.refs_0_, bf16[352,128]{1,0:T(8,128)(2,1)S(1)} %collective-permute-done.8.refs_1_), custom_call_target="tpu_custom_call" | custom-call | tf_op jit(solution)/shard_map/write_0/pallas_call | solution.py:321
  21.7 0.2 collective-permute-done.5
  21.9 0.1 collective-permute-start.9
  22.0 0.7 %write_home.1.refs_1_ = bf16[1536,128]{1,0:T(8,128)(2,1)} custom-call(bf16[416,128]{1,0:T(8,128)(2,1)S(1)} %multiply_convert_fusion.refs_0_, bf16[1536,128]{1,0:T(8,128)(2,1)} %write_0.1.refs_1_), custom_call_target="tpu_custom_call", output_to_operand_aliasing={{}: (1, {})} | custom-call | tf_op jit(solution)/shard_map/write_home/pallas_call | solution.py:321
  22.7 0.6 %collective-permute-done.9.refs_0_ = bf16[416,128]{1,0:T(8,128)(2,1)S(1)} collective-permute-done((bf16[416,128]{1,0:T(8,128)(2,1)S(1)}, bf16[416,128]{1,0:T(8,128)(2,1)S(1)}, u32[]{:S(2)}, u32[]{:S(2)}) %collective-permute-start.9) | collective-permute-done | bytes 106528 | tf_op jit(solution)/shard_map/ppermute | solution.py:357
  23.3 0.7 %write_away.1 = bf16[1536,128]{1,0:T(8,128)(2,1)} custom-call(bf16[416,128]{1,0:T(8,128)(2,1)S(1)} %collective-permute-done.9.refs_0_, bf16[1536,128]{1,0:T(8,128)(2,1)} %write_home.1.refs_1_), custom_call_target="tpu_custom_call", output_to_operand_aliasing={{}: (1, {})} | custom-call | tf_op jit(solution)/shard_map/write_away/pallas_call | solution.py:321
  (19 shorter events, 0.2 us)
Async XLA Ops:
  0.0 5.4 %copy-start = (bf16[1536,128]{1,0:T(8,128)(2,1)S(1)}, bf16[1536,128]{1,0:T(8,128)(2,1)}, u32[]{:S(2)}) copy-start(bf16[1536,128]{1,0:T(8,128)(2,1)} %activity_ref.1) | copy-start | bytes 1179652
  0.0 5.4 %copy-start.5 = (s32[1,1,86]{2,1,0:T(1,128)S(1)}, s32[1,1,86]{2,1,0:T(1,128)}, u32[]{:S(2)}) copy-start(s32[1,1,86]{2,1,0:T(1,128)} %param.12) | copy-start | bytes 1036
  0.0 5.4 %copy-start.4 = (s32[1,1,86]{2,1,0:T(1,128)S(1)}, s32[1,1,86]{2,1,0:T(1,128)}, u32[]{:S(2)}) copy-start(s32[1,1,86]{2,1,0:T(1,128)} %param.11) | copy-start | bytes 1036
  0.0 5.4 %copy-start.2 = (bf16[1,1,512,128]{3,2,1,0:T(8,128)(2,1)S(1)}, bf16[1,1,512,128]{3,2,1,0:T(8,128)(2,1)}, u32[]{:S(2)}) copy-start(bf16[1,1,512,128]{3,2,1,0:T(8,128)(2,1)} %param.15) | copy-start | bytes 393220
  0.0 5.4 %copy-start.1 = (s32[1,1,512,128]{3,2,1,0:T(8,128)S(1)}, s32[1,1,512,128]{3,2,1,0:T(8,128)}, u32[]{:S(2)}) copy-start(s32[1,1,512,128]{3,2,1,0:T(8,128)} %param.14) | copy-start | bytes 786436
  0.0 5.4 %copy-start.6 = (s32[1,1,2]{2,1,0:T(1,128)S(1)}, s32[1,1,2]{2,1,0:T(1,128)}, u32[]{:S(2)}) copy-start(s32[1,1,2]{2,1,0:T(1,128)} %param.13) | copy-start | bytes 28
  0.0 5.4 %copy-start.3 = (f32[1536]{0:T(1024)S(1)}, f32[1536]{0:T(1024)}, u32[]{:S(2)}) copy-start(f32[1536]{0:T(1024)} %param.9) | copy-start | bytes 18436
  2.3 5.5 %collective-permute-start = (bf16[2,128,128]{2,1,0:T(8,128)(2,1)S(1)}, bf16[2,128,128]{2,1,0:T(8,128)(2,1)S(1)}, u32[]{:S(2)}, u32[]{:S(2)}) collective-permute-start(bf16[2,128,128]{2,1,0:T(8,128)(2,1)S(1)} %get-tuple-element.22), channel_id=1, source_target_pairs={{0,1},{1,5},{2,3},{3,7},{4,0},{5,9},{6,2},{7,11},{8,4},{9,13},{10,... | collective-permute-start | bytes 196616 | tf_op jit(solution)/shard_map/ppermute | solution.py:264
  2.8 5.0 %collective-permute-start.1 = (bf16[2,128,128]{2,1,0:T(8,128)(2,1)S(1)}, bf16[2,128,128]{2,1,0:T(8,128)(2,1)S(1)}, u32[]{:S(2)}, u32[]{:S(2)}) collective-permute-start(bf16[2,128,128]{2,1,0:T(8,128)(2,1)S(1)} %get-tuple-element.23), channel_id=1, source_target_pairs={{1,0},{5,1},{3,2},{7,3},{0,4},{9,5},{2,6},{11,7},{4,8},{13,9},{6,1... | collective-permute-start | bytes 196616 | tf_op jit(solution)/shard_map/ppermute | solution.py:265
  7.9 4.7 %collective-permute-start.3 = (bf16[2,128,128]{2,1,0:T(8,128)(2,1)S(1)}, bf16[2,128,128]{2,1,0:T(8,128)(2,1)S(1)}, u32[]{:S(2)}, u32[]{:S(2)}) collective-permute-start(bf16[2,128,128]{2,1,0:T(8,128)(2,1)S(1)} %oblique_ratios.1.oblique_ref), channel_id=1, source_target_pairs={{0,1},{1,5},{2,3},{3,7},{4,0},{5,9},{6,2},{7,11},{8,4},{9,13},{10,... | collective-permute-start | bytes 196616 | tf_op jit(solution)/shard_map/ppermute | solution.py:293
  8.3 4.3 %collective-permute-start.2 = (bf16[2,128,128]{2,1,0:T(8,128)(2,1)S(1)}, bf16[2,128,128]{2,1,0:T(8,128)(2,1)S(1)}, u32[]{:S(2)}, u32[]{:S(2)}) collective-permute-start(bf16[2,128,128]{2,1,0:T(8,128)(2,1)S(1)} %oblique_ratios.1.oblique_ref), channel_id=1, source_target_pairs={{1,0},{5,1},{3,2},{7,3},{0,4},{9,5},{2,6},{11,7},{4,8},{13,9},{6,1... | collective-permute-start | bytes 196616 | tf_op jit(solution)/shard_map/ppermute | solution.py:294
  12.9 1.7 %collective-permute-start.6 = (f16[352,128]{1,0:T(8,128)(2,1)S(1)}, f16[352,128]{1,0:T(8,128)(2,1)S(1)}, u32[]{:S(2)}, u32[]{:S(2)}) collective-permute-start(f16[352,128]{1,0:T(8,128)(2,1)S(1)} %convert_element_type.40), channel_id=1, source_target_pairs={{0,1},{1,0},{2,3},{3,2},{4,5},{5,4},{6,7},{7,6},{8,9},{9,8},{10,11... | collective-permute-start | bytes 270344 | tf_op jit(solution)/shard_map/ppermute | solution.py:339
  13.9 2.7 %collective-permute-start.4 = (f16[416,128]{1,0:T(8,128)(2,1)S(1)}, f16[416,128]{1,0:T(8,128)(2,1)S(1)}, u32[]{:S(2)}, u32[]{:S(2)}) collective-permute-start(f16[416,128]{1,0:T(8,128)(2,1)S(1)} %convert_element_type.36), channel_id=1, source_target_pairs={{0,1},{1,0},{2,3},{3,2},{4,5},{5,4},{6,7},{7,6},{8,9},{9,8},{10,11... | collective-permute-start | bytes 319496 | tf_op jit(solution)/shard_map/ppermute | solution.py:339
  14.6 5.0 %collective-permute-start.7 = (f16[352,128]{1,0:T(8,128)(2,1)S(1)}, f16[352,128]{1,0:T(8,128)(2,1)S(1)}, u32[]{:S(2)}, u32[]{:S(2)}) collective-permute-start(f16[352,128]{1,0:T(8,128)(2,1)S(1)} %multiply_convert_fusion.3), channel_id=1, source_target_pairs={{0,2},{1,3},{2,0},{3,1},{4,6},{5,7},{6,4},{7,5},{8,10},{9,11},{10,... | collective-permute-start | bytes 270344 | tf_op jit(solution)/shard_map/ppermute | solution.py:348
  17.0 4.9 %collective-permute-start.5 = (f16[416,128]{1,0:T(8,128)(2,1)S(1)}, f16[416,128]{1,0:T(8,128)(2,1)S(1)}, u32[]{:S(2)}, u32[]{:S(2)}) collective-permute-start(f16[416,128]{1,0:T(8,128)(2,1)S(1)} %multiply_convert_fusion.1), channel_id=1, source_target_pairs={{0,2},{1,3},{2,0},{3,1},{4,6},{5,7},{6,4},{7,5},{8,10},{9,11},{10,... | collective-permute-start | bytes 319496 | tf_op jit(solution)/shard_map/ppermute | solution.py:348
  19.6 1.4 %collective-permute-start.8 = (bf16[352,128]{1,0:T(8,128)(2,1)S(1)}, bf16[352,128]{1,0:T(8,128)(2,1)S(1)}, u32[]{:S(2)}, u32[]{:S(2)}) collective-permute-start(bf16[352,128]{1,0:T(8,128)(2,1)S(1)} %multiply_convert_fusion.2.refs_0_), channel_id=1, source_target_pairs={{0,1},{1,0},{2,3},{3,2},{4,5},{5,4},{6,7},{7,6},{8,9},{9,8},{10,11... | collective-permute-start | bytes 270344 | tf_op jit(solution)/shard_map/ppermute | solution.py:357
  21.9 1.4 %collective-permute-start.9 = (bf16[416,128]{1,0:T(8,128)(2,1)S(1)}, bf16[416,128]{1,0:T(8,128)(2,1)S(1)}, u32[]{:S(2)}, u32[]{:S(2)}) collective-permute-start(bf16[416,128]{1,0:T(8,128)(2,1)S(1)} %multiply_convert_fusion.refs_0_), channel_id=1, source_target_pairs={{0,1},{1,0},{2,3},{3,2},{4,5},{5,4},{6,7},{7,6},{8,9},{9,8},{10,11... | collective-permute-start | bytes 319496 | tf_op jit(solution)/shard_map/ppermute | solution.py:357

commit v7 on v6

--- a/solution.py
+++ b/solution.py
@@ -30,6 +30,11 @@
     forth = jnp.logical_or(jnp.logical_and(even, right), jnp.logical_and(~even, left))
     back = jnp.logical_or(jnp.logical_and(even, left), jnp.logical_and(~even, right))
     return odd, forth, back
+
+
+def home_half():
+    angle = lax.axis_index("angle")
+    return (angle + angle // 2) % 2
 
 
 def index_tiles(voxel_ref, line_ref, slot_ref, blocks, lines):
@@ -136,7 +141,7 @@
                 measured_ref[c] = measured
             else:
                 ratio_ref[start - width + c] = (measured / base).astype(ratio_ref.dtype)
-    away = (1 - lax.axis_index("angle") % 2) * (blocks // 2)
+    away = (1 - home_half()) * (blocks // 2)
     for v in range(blocks):
         voxel = lax.rem(away + v, blocks)
         for c in range(lines):
@@ -167,7 +172,7 @@
 
 def fill_gain(size, activity_ref, sensitivity_ref, gain_ref):
     count = gain_ref.shape[0] // size
-    first = lax.axis_index("angle") % 2 * count
+    first = home_half() * count
     for n in range(count):
         at = pl.multiple_of((first + n) * size, size)
         values = activity_ref[pl.ds(at, size)].astype(jnp.float32)
@@ -194,7 +199,7 @@
 
 def write_rows_kernel(half_rows, places, *refs):
     out_hbm, sem = refs[-2:]
-    odd = lax.axis_index("angle") % 2
+    odd = home_half()
     copies = []
     for n, (turn, start) in enumerate(places):
         count = refs[n].shape[0]
@@ -337,7 +342,7 @@
     for n, span in enumerate(spans):
         away = edge_rows(span.start, span.stop - span.start, PART_SCALE, f"edge_back_sent_{n}")
         got.append(lax.ppermute(away.astype(jnp.float16), "angle", pairs))
-    updated = None
+    written = []
     for n, (at, end) in enumerate(zip(cuts[:-1], cuts[1:])):
         span = spans[n]
         after, got[n] = lax.optimization_barrier((beside_back, got[n])) if n else (None, got[n])
@@ -345,22 +350,20 @@
         chip = (home + wide(got[n]) * (1.0 / PART_SCALE)) * CHIP_SCALE
         if angles == 4:
             chip = lax.optimization_barrier(chip.astype(jnp.float16))
-            across = lax.ppermute(chip, "angle", [(a, a ^ 2) for a in range(angles)])
-            if updated is not None:
-                across, updated = lax.optimization_barrier((across, updated))
+            across = lax.ppermute(chip, "angle", [(a, a ^ 3) for a in range(angles)])
+            if written:
+                across, rows_away = lax.optimization_barrier((across, rows_away))
+                written[-1] = (rows_away,) + written[-1][1:]
             total = wide(chip) + wide(across)
         else:
-            groups = [list(range(odd_one, angles, 2)) for odd_one in range(2)]
+            groups = [[a for a in range(angles) if (a + a // 2) % 2 == n] for n in range(2)]
             total = lax.psum(chip, "angle", axis_index_groups=groups)
         rows_home = (gain[span] * total).astype(jnp.bfloat16)
         rows_home = lax.optimization_barrier(rows_home)
         rows_away = lax.ppermute(rows_home, "angle", pairs)
-        if end < half_rows:
-            updated = write_rows(updated, f"write_{n}", (rows_home, 0, at), (rows_away, 1, at))
-        else:
-            updated = write_rows(updated, "write_home", (rows_home, 0, at))
-            updated = write_rows(updated, "write_away", (rows_away, 1, at))
-    return updated
+        written += [(rows_home, 0, at), (rows_away, 1, at)]
+    updated = write_rows(None, "write_first", *written[:-1])
+    return write_rows(updated, "write_last", written[-1])
 
 
 def solution(mesh):

time: 24.1 us -> 23.9 us (level)
  Pallas kernels: 8.25 us -> 7.62 us
  starting transfers between devices: 9.03 us -> 9.36 us
    ppermute x2, waiting for transfers between devices: 2.29 us -> 3.98 us  [body(): across = lax.ppermute(chip, 'angle', [(a, a ^ 3) for a in range(angles)])]
    ppermute x2, waiting for transfers between devices: 1.89 us -> 0.3 us  [body(): rows_away = lax.ppermute(rows_home, 'angle', pairs)]
    pallas_call x3 -> x2, Pallas kernels: 2.01 us -> 1.38 us  [write_rows(): pl.pallas_call(functools.partial(write_rows_kernel, half_rows, places), o...]
    ppermute x2, starting transfers between devices: 0.14 us -> 0.52 us  [body(): rows_away = lax.ppermute(rows_home, 'angle', pairs)]
  transfers between devices with their start and end apart: 10 -> 10, of which waited for: 7 -> 6; matrix products, arithmetic and copies ran while one was open for 1% -> 1% of each run, Pallas kernels for 21% -> 18%
where the time goes in v7:
time: 23.9 us; the launch traced here: 23.7 us
  starting transfers between devices  9.36 us (39%)
  Pallas kernels  7.62 us (32%)
  waiting for transfers between devices  6.32 us (26%)
    ppermute x2, waiting for transfers between devices, body(): across = lax.ppermute(chip, 'angle', [(a, a ^ 3) for a in range(angles)])  3.98 us
    ppermute x1, starting transfers between devices, body(): got_back = lax.ppermute(edge_back, both, back)  2.6 us
    ppermute x2, starting transfers between devices, body(): across = lax.ppermute(chip, 'angle', [(a, a ^ 3) for a in range(angles)])  2.46 us
    pallas_call x1, Pallas kernels, body(): pl.pallas_call(functools.partial(edge_kernel, blocks, own, lines), out_sh...  2.28 us
    pallas_call x1, Pallas kernels, body(): pl.pallas_call(functools.partial(own_kernel, blocks, own, lines), out_sha...  2.21 us
    ppermute x1, starting transfers between devices, body(): beside_back = lax.ppermute(oblique, both, back)  2.08 us
    ppermute x1, waiting for transfers between devices, body(): beside_forth = lax.ppermute(oblique, both, forth)  1.64 us
    pallas_call x2, Pallas kernels, write_rows(): pl.pallas_call(functools.partial(write_rows_kernel, half_rows, places), o...  1.38 us
  transfers between devices with their start and end apart: 10, of which 6 were waited for; matrix products, arithmetic and copies ran while one was open for 1% of the time, Pallas kernels for 18%

profile of v7, /device:TPU:0, one launch (start us, length us, event | category | flops | bytes accessed | tf_op | source)
XLA Modules:
  0.0 23.7 jit_solution(1041947219382377409)
XLA Ops:
  0.0 0.0 copy-start.6
  0.0 0.0 copy-start.3
  0.0 2.3 %edge_partials.1 = (bf16[2,128,128]{2,1,0:T(8,128)(2,1)S(1)}, bf16[2,128,128]{2,1,0:T(8,128)(2,1)S(1)}, bf16[128,1536]{1,0:T(8,128)(2,1)S(1)}, bf16[86,128,128]{2,1,0:T(8,128)(2,1)S(1)}) custom-call(s32[86]{0:T(128)} %bitcast.10, s32[86]{0:T(128)} %bitcast.12, bf16[1536,128]{1,0:T(8,128)(2,1)} %activity_ref.1, bf16[86,128,128]{2,1,0:T(8,128)(2,1)} %bitcast.15), custom_call_target="tpu_custom_call" | custom-call | tf_op jit(solution)/shard_map/edge_partials/pallas_call | solution.py:248
  2.3 0.5 %collective-permute-start = (bf16[2,128,128]{2,1,0:T(8,128)(2,1)S(1)}, bf16[2,128,128]{2,1,0:T(8,128)(2,1)S(1)}, u32[]{:S(2)}, u32[]{:S(2)}) collective-permute-start(bf16[2,128,128]{2,1,0:T(8,128)(2,1)S(1)} %get-tuple-element.22), channel_id=1, source_target_pairs={{0,1},{1,5},{2,3},{3,7},{4,0},{5,9},{6,2},{7,11},{8,4},{9,13},{10,... | collective-permute-start | bytes 196616 | tf_op jit(solution)/shard_map/ppermute | solution.py:269
  2.8 2.6 %collective-permute-start.1 = (bf16[2,128,128]{2,1,0:T(8,128)(2,1)S(1)}, bf16[2,128,128]{2,1,0:T(8,128)(2,1)S(1)}, u32[]{:S(2)}, u32[]{:S(2)}) collective-permute-start(bf16[2,128,128]{2,1,0:T(8,128)(2,1)S(1)} %get-tuple-element.23), channel_id=1, source_target_pairs={{1,0},{5,1},{3,2},{7,3},{0,4},{9,5},{2,6},{11,7},{4,8},{13,9},{6,1... | collective-permute-start | bytes 196616 | tf_op jit(solution)/shard_map/ppermute | solution.py:270
  5.5 2.2 %own_partials.1 = (f32[2,128,128]{2,1,0:T(8,128)S(1)}, f32[2,128,128]{2,1,0:T(8,128)S(1)}, bf16[2,128,128]{2,1,0:T(8,128)(2,1)S(1)}, bf16[1536,1024]{1,0:T(8,128)(2,1)S(1)}, f32[768,128]{1,0:T(8,128)S(1)}) custom-call(s32[86]{0:T(128)S(1)} %bitcast.11, s32[86]{0:T(128)S(1)} %bitcast.13, s32[2]{0:T(128)S(1)} %bitcast.14, ...), custom_call_target="tpu_custom_call" | custom-call | tf_op jit(solution)/shard_map/own_partials/pallas_call | solution.py:272
  7.7 0.1 collective-permute-done.forth_ref
  7.8 0.0 collective-permute-done.1.back_ref
  7.8 0.1 oblique_ratios.1.oblique_ref
  7.9 0.4 %collective-permute-start.3 = (bf16[2,128,128]{2,1,0:T(8,128)(2,1)S(1)}, bf16[2,128,128]{2,1,0:T(8,128)(2,1)S(1)}, u32[]{:S(2)}, u32[]{:S(2)}) collective-permute-start(bf16[2,128,128]{2,1,0:T(8,128)(2,1)S(1)} %oblique_ratios.1.oblique_ref), channel_id=1, source_target_pairs={{0,1},{1,5},{2,3},{3,7},{4,0},{5,9},{6,2},{7,11},{8,4},{9,13},{10,... | collective-permute-start | bytes 196616 | tf_op jit(solution)/shard_map/ppermute | solution.py:298
  8.3 2.1 %collective-permute-start.2 = (bf16[2,128,128]{2,1,0:T(8,128)(2,1)S(1)}, bf16[2,128,128]{2,1,0:T(8,128)(2,1)S(1)}, u32[]{:S(2)}, u32[]{:S(2)}) collective-permute-start(bf16[2,128,128]{2,1,0:T(8,128)(2,1)S(1)} %oblique_ratios.1.oblique_ref), channel_id=1, source_target_pairs={{1,0},{5,1},{3,2},{7,3},{0,4},{9,5},{2,6},{11,7},{4,8},{13,9},{6,1... | collective-permute-start | bytes 196616 | tf_op jit(solution)/shard_map/ppermute | solution.py:299
  10.4 0.6 %own_back.1.own_ref = f32[1536,128]{1,0:T(8,128)S(1)} custom-call(bf16[1536,1024]{1,0:T(8,128)(2,1)S(1)} %get-tuple-element.21.matrix_ref, bf16[2,128,128]{2,1,0:T(8,128)(2,1)S(1)} %oblique_ratios.1.oblique_ref, bf16[2,128,128]{2,1,0:T(8,128)(2,1)S(1)} %get-tuple-element.26.ratio_ref), custom_call_target="tpu_custom_call" | custom-call | tf_op jit(solution)/shard_map/own_back/pallas_call | solution.py:300
  10.9 1.6 %collective-permute-done.3.forth_ref = bf16[2,128,128]{2,1,0:T(8,128)(2,1)S(1)} collective-permute-done((bf16[2,128,128]{2,1,0:T(8,128)(2,1)S(1)}, bf16[2,128,128]{2,1,0:T(8,128)(2,1)S(1)}, u32[]{:S(2)}, u32[]{:S(2)}) %collective-permute-start.3) | collective-permute-done | bytes 65568 | tf_op jit(solution)/shard_map/ppermute | solution.py:298
  12.6 0.0 collective-permute-done.2.back_ref
  12.6 0.3 %edge_back_sent_0.1 = f32[352,128]{1,0:T(8,128)S(1)} custom-call(bf16[1536,1024]{1,0:T(8,128)(2,1)S(1)} %get-tuple-element.21.matrix_ref, bf16[2,128,128]{2,1,0:T(8,128)(2,1)S(1)} %collective-permute-done.2.back_ref, bf16[2,128,128]{2,1,0:T(8,128)(2,1)S(1)} %collective-permute-done.3.forth_ref, f32[1536,128]{1,0:T(8,128)S(1)} %own_back.1.own_ref), custom_call_target="tpu_custom_call" | custom-call | tf_op jit(solution)/shard_map/edge_back_sent_0/pallas_call | solution.py:310
  12.9 0.7 %collective-permute-start.6 = (f16[352,128]{1,0:T(8,128)(2,1)S(1)}, f16[352,128]{1,0:T(8,128)(2,1)S(1)}, u32[]{:S(2)}, u32[]{:S(2)}) collective-permute-start(f16[352,128]{1,0:T(8,128)(2,1)S(1)} %convert_element_type.40), channel_id=1, source_target_pairs={{0,1},{1,0},{2,3},{3,2},{4,5},{5,4},{6,7},{7,6},{8,9},{9,8},{10,11... | collective-permute-start | bytes 270344 | tf_op jit(solution)/shard_map/ppermute | solution.py:344
  13.6 0.3 %edge_back_sent_1.1 = f32[416,128]{1,0:T(8,128)S(1)} custom-call(bf16[1536,1024]{1,0:T(8,128)(2,1)S(1)} %get-tuple-element.21.matrix_ref, bf16[2,128,128]{2,1,0:T(8,128)(2,1)S(1)} %collective-permute-done.2.back_ref, bf16[2,128,128]{2,1,0:T(8,128)(2,1)S(1)} %collective-permute-done.3.forth_ref, f32[1536,128]{1,0:T(8,128)S(1)} %own_back.1.own_ref), custom_call_target="tpu_custom_call" | custom-call | tf_op jit(solution)/shard_map/edge_back_sent_1/pallas_call | solution.py:310
  13.9 0.1 collective-permute-start.4
  14.0 0.3 %edge_back_kept_0.1 = f32[352,128]{1,0:T(8,128)S(1)} custom-call(bf16[1536,1024]{1,0:T(8,128)(2,1)S(1)} %get-tuple-element.21.matrix_ref, bf16[2,128,128]{2,1,0:T(8,128)(2,1)S(1)} %collective-permute-done.2.back_ref, bf16[2,128,128]{2,1,0:T(8,128)(2,1)S(1)} %collective-permute-done.3.forth_ref, f32[1536,128]{1,0:T(8,128)S(1)} %own_back.1.own_ref), custom_call_target="tpu_custom_call" | custom-call | tf_op jit(solution)/shard_map/edge_back_kept_0/pallas_call | solution.py:310
  14.3 0.3 %collective-permute-done.6 = f16[352,128]{1,0:T(8,128)(2,1)S(1)} collective-permute-done((f16[352,128]{1,0:T(8,128)(2,1)S(1)}, f16[352,128]{1,0:T(8,128)(2,1)S(1)}, u32[]{:S(2)}, u32[]{:S(2)}) %collective-permute-start.6) | collective-permute-done | bytes 90144 | tf_op jit(solution)/shard_map/ppermute | solution.py:344
  14.6 1.8 %collective-permute-start.7 = (f16[352,128]{1,0:T(8,128)(2,1)S(1)}, f16[352,128]{1,0:T(8,128)(2,1)S(1)}, u32[]{:S(2)}, u32[]{:S(2)}) collective-permute-start(f16[352,128]{1,0:T(8,128)(2,1)S(1)} %multiply_convert_fusion.3), channel_id=1, source_target_pairs={{0,3},{1,2},{2,1},{3,0},{4,7},{5,6},{6,5},{7,4},{8,11},{9,10},{10,... | collective-permute-start | bytes 270344 | tf_op jit(solution)/shard_map/ppermute | solution.py:353
  16.4 0.0 collective-permute-done.4
  16.4 0.3 %edge_back_kept_1.1 = f32[416,128]{1,0:T(8,128)S(1)} custom-call(bf16[1536,1024]{1,0:T(8,128)(2,1)S(1)} %get-tuple-element.21.matrix_ref, bf16[2,128,128]{2,1,0:T(8,128)(2,1)S(1)} %collective-permute-done.2.back_ref, bf16[2,128,128]{2,1,0:T(8,128)(2,1)S(1)} %collective-permute-done.3.forth_ref, f32[1536,128]{1,0:T(8,128)S(1)} %own_back.1.own_ref), custom_call_target="tpu_custom_call" | custom-call | tf_op jit(solution)/shard_map/edge_back_kept_1/pallas_call | solution.py:310
  16.7 0.7 %collective-permute-start.5 = (f16[416,128]{1,0:T(8,128)(2,1)S(1)}, f16[416,128]{1,0:T(8,128)(2,1)S(1)}, u32[]{:S(2)}, u32[]{:S(2)}) collective-permute-start(f16[416,128]{1,0:T(8,128)(2,1)S(1)} %multiply_convert_fusion.1), channel_id=1, source_target_pairs={{0,3},{1,2},{2,1},{3,0},{4,7},{5,6},{6,5},{7,4},{8,11},{9,10},{10,... | collective-permute-start | bytes 319496 | tf_op jit(solution)/shard_map/ppermute | solution.py:353
  17.4 1.9 %collective-permute-done.7 = f16[352,128]{1,0:T(8,128)(2,1)S(1)} collective-permute-done((f16[352,128]{1,0:T(8,128)(2,1)S(1)}, f16[352,128]{1,0:T(8,128)(2,1)S(1)}, u32[]{:S(2)}, u32[]{:S(2)}) %collective-permute-start.7) | collective-permute-done | bytes 90144 | tf_op jit(solution)/shard_map/ppermute | solution.py:353
  19.4 0.2 collective-permute-start.8
  19.5 2.1 %collective-permute-done.5 = f16[416,128]{1,0:T(8,128)(2,1)S(1)} collective-permute-done((f16[416,128]{1,0:T(8,128)(2,1)S(1)}, f16[416,128]{1,0:T(8,128)(2,1)S(1)}, u32[]{:S(2)}, u32[]{:S(2)}) %collective-permute-start.5) | collective-permute-done | bytes 106528 | tf_op jit(solution)/shard_map/ppermute | solution.py:353
  21.6 0.0 collective-permute-done.8.refs_1_
  21.7 0.3 %collective-permute-start.9 = (bf16[416,128]{1,0:T(8,128)(2,1)S(1)}, bf16[416,128]{1,0:T(8,128)(2,1)S(1)}, u32[]{:S(2)}, u32[]{:S(2)}) collective-permute-start(bf16[416,128]{1,0:T(8,128)(2,1)S(1)} %multiply_convert_fusion.refs_2_), channel_id=1, source_target_pairs={{0,1},{1,0},{2,3},{3,2},{4,5},{5,4},{6,7},{7,6},{8,9},{9,8},{10,11... | collective-permute-start | bytes 319496 | tf_op jit(solution)/shard_map/ppermute | solution.py:363
  22.0 0.7 %write_first.1.refs_1_ = bf16[1536,128]{1,0:T(8,128)(2,1)} custom-call(bf16[352,128]{1,0:T(8,128)(2,1)S(1)} %multiply_convert_fusion.2.refs_0_, bf16[352,128]{1,0:T(8,128)(2,1)S(1)} %collective-permute-done.8.refs_1_, bf16[416,128]{1,0:T(8,128)(2,1)S(1)} %multiply_convert_fusion.refs_2_), custom_call_target="tpu_custom_call" | custom-call | tf_op jit(solution)/shard_map/write_first/pallas_call | solution.py:326
  22.8 0.3 %collective-permute-done.9.refs_0_ = bf16[416,128]{1,0:T(8,128)(2,1)S(1)} collective-permute-done((bf16[416,128]{1,0:T(8,128)(2,1)S(1)}, bf16[416,128]{1,0:T(8,128)(2,1)S(1)}, u32[]{:S(2)}, u32[]{:S(2)}) %collective-permute-start.9) | collective-permute-done | bytes 106528 | tf_op jit(solution)/shard_map/ppermute | solution.py:363
  23.1 0.7 %write_last.1 = bf16[1536,128]{1,0:T(8,128)(2,1)} custom-call(bf16[416,128]{1,0:T(8,128)(2,1)S(1)} %collective-permute-done.9.refs_0_, bf16[1536,128]{1,0:T(8,128)(2,1)} %write_first.1.refs_1_), custom_call_target="tpu_custom_call", output_to_operand_aliasing={{}: (1, {})} | custom-call | tf_op jit(solution)/shard_map/write_last/pallas_call | solution.py:326
  (18 shorter events, 0.2 us)
Async XLA Ops:
  0.0 5.4 %copy-start = (bf16[1536,128]{1,0:T(8,128)(2,1)S(1)}, bf16[1536,128]{1,0:T(8,128)(2,1)}, u32[]{:S(2)}) copy-start(bf16[1536,128]{1,0:T(8,128)(2,1)} %activity_ref.1) | copy-start | bytes 1179652
  0.0 5.4 %copy-start.5 = (s32[1,1,86]{2,1,0:T(1,128)S(1)}, s32[1,1,86]{2,1,0:T(1,128)}, u32[]{:S(2)}) copy-start(s32[1,1,86]{2,1,0:T(1,128)} %param.12) | copy-start | bytes 1036
  0.0 5.4 %copy-start.4 = (s32[1,1,86]{2,1,0:T(1,128)S(1)}, s32[1,1,86]{2,1,0:T(1,128)}, u32[]{:S(2)}) copy-start(s32[1,1,86]{2,1,0:T(1,128)} %param.11) | copy-start | bytes 1036
  0.0 5.4 %copy-start.2 = (bf16[1,1,512,128]{3,2,1,0:T(8,128)(2,1)S(1)}, bf16[1,1,512,128]{3,2,1,0:T(8,128)(2,1)}, u32[]{:S(2)}) copy-start(bf16[1,1,512,128]{3,2,1,0:T(8,128)(2,1)} %param.15) | copy-start | bytes 393220
  0.0 5.4 %copy-start.1 = (s32[1,1,512,128]{3,2,1,0:T(8,128)S(1)}, s32[1,1,512,128]{3,2,1,0:T(8,128)}, u32[]{:S(2)}) copy-start(s32[1,1,512,128]{3,2,1,0:T(8,128)} %param.14) | copy-start | bytes 786436
  0.0 5.4 %copy-start.6 = (s32[1,1,2]{2,1,0:T(1,128)S(1)}, s32[1,1,2]{2,1,0:T(1,128)}, u32[]{:S(2)}) copy-start(s32[1,1,2]{2,1,0:T(1,128)} %param.13) | copy-start | bytes 28
  0.0 5.4 %copy-start.3 = (f32[1536]{0:T(1024)S(1)}, f32[1536]{0:T(1024)}, u32[]{:S(2)}) copy-start(f32[1536]{0:T(1024)} %param.9) | copy-start | bytes 18436
  2.3 5.5 %collective-permute-start = (bf16[2,128,128]{2,1,0:T(8,128)(2,1)S(1)}, bf16[2,128,128]{2,1,0:T(8,128)(2,1)S(1)}, u32[]{:S(2)}, u32[]{:S(2)}) collective-permute-start(bf16[2,128,128]{2,1,0:T(8,128)(2,1)S(1)} %get-tuple-element.22), channel_id=1, source_target_pairs={{0,1},{1,5},{2,3},{3,7},{4,0},{5,9},{6,2},{7,11},{8,4},{9,13},{10,... | collective-permute-start | bytes 196616 | tf_op jit(solution)/shard_map/ppermute | solution.py:269
  2.8 5.0 %collective-permute-start.1 = (bf16[2,128,128]{2,1,0:T(8,128)(2,1)S(1)}, bf16[2,128,128]{2,1,0:T(8,128)(2,1)S(1)}, u32[]{:S(2)}, u32[]{:S(2)}) collective-permute-start(bf16[2,128,128]{2,1,0:T(8,128)(2,1)S(1)} %get-tuple-element.23), channel_id=1, source_target_pairs={{1,0},{5,1},{3,2},{7,3},{0,4},{9,5},{2,6},{11,7},{4,8},{13,9},{6,1... | collective-permute-start | bytes 196616 | tf_op jit(solution)/shard_map/ppermute | solution.py:270
  7.9 4.7 %collective-permute-start.3 = (bf16[2,128,128]{2,1,0:T(8,128)(2,1)S(1)}, bf16[2,128,128]{2,1,0:T(8,128)(2,1)S(1)}, u32[]{:S(2)}, u32[]{:S(2)}) collective-permute-start(bf16[2,128,128]{2,1,0:T(8,128)(2,1)S(1)} %oblique_ratios.1.oblique_ref), channel_id=1, source_target_pairs={{0,1},{1,5},{2,3},{3,7},{4,0},{5,9},{6,2},{7,11},{8,4},{9,13},{10,... | collective-permute-start | bytes 196616 | tf_op jit(solution)/shard_map/ppermute | solution.py:298
  8.3 4.3 %collective-permute-start.2 = (bf16[2,128,128]{2,1,0:T(8,128)(2,1)S(1)}, bf16[2,128,128]{2,1,0:T(8,128)(2,1)S(1)}, u32[]{:S(2)}, u32[]{:S(2)}) collective-permute-start(bf16[2,128,128]{2,1,0:T(8,128)(2,1)S(1)} %oblique_ratios.1.oblique_ref), channel_id=1, source_target_pairs={{1,0},{5,1},{3,2},{7,3},{0,4},{9,5},{2,6},{11,7},{4,8},{13,9},{6,1... | collective-permute-start | bytes 196616 | tf_op jit(solution)/shard_map/ppermute | solution.py:299
  12.9 1.7 %collective-permute-start.6 = (f16[352,128]{1,0:T(8,128)(2,1)S(1)}, f16[352,128]{1,0:T(8,128)(2,1)S(1)}, u32[]{:S(2)}, u32[]{:S(2)}) collective-permute-start(f16[352,128]{1,0:T(8,128)(2,1)S(1)} %convert_element_type.40), channel_id=1, source_target_pairs={{0,1},{1,0},{2,3},{3,2},{4,5},{5,4},{6,7},{7,6},{8,9},{9,8},{10,11... | collective-permute-start | bytes 270344 | tf_op jit(solution)/shard_map/ppermute | solution.py:344
  13.9 2.5 %collective-permute-start.4 = (f16[416,128]{1,0:T(8,128)(2,1)S(1)}, f16[416,128]{1,0:T(8,128)(2,1)S(1)}, u32[]{:S(2)}, u32[]{:S(2)}) collective-permute-start(f16[416,128]{1,0:T(8,128)(2,1)S(1)} %convert_element_type.36), channel_id=1, source_target_pairs={{0,1},{1,0},{2,3},{3,2},{4,5},{5,4},{6,7},{7,6},{8,9},{9,8},{10,11... | collective-permute-start | bytes 319496 | tf_op jit(solution)/shard_map/ppermute | solution.py:344
  14.6 4.7 %collective-permute-start.7 = (f16[352,128]{1,0:T(8,128)(2,1)S(1)}, f16[352,128]{1,0:T(8,128)(2,1)S(1)}, u32[]{:S(2)}, u32[]{:S(2)}) collective-permute-start(f16[352,128]{1,0:T(8,128)(2,1)S(1)} %multiply_convert_fusion.3), channel_id=1, source_target_pairs={{0,3},{1,2},{2,1},{3,0},{4,7},{5,6},{6,5},{7,4},{8,11},{9,10},{10,... | collective-permute-start | bytes 270344 | tf_op jit(solution)/shard_map/ppermute | solution.py:353
  16.7 4.9 %collective-permute-start.5 = (f16[416,128]{1,0:T(8,128)(2,1)S(1)}, f16[416,128]{1,0:T(8,128)(2,1)S(1)}, u32[]{:S(2)}, u32[]{:S(2)}) collective-permute-start(f16[416,128]{1,0:T(8,128)(2,1)S(1)} %multiply_convert_fusion.1), channel_id=1, source_target_pairs={{0,3},{1,2},{2,1},{3,0},{4,7},{5,6},{6,5},{7,4},{8,11},{9,10},{10,... | collective-permute-start | bytes 319496 | tf_op jit(solution)/shard_map/ppermute | solution.py:353
  19.4 2.3 %collective-permute-start.8 = (bf16[352,128]{1,0:T(8,128)(2,1)S(1)}, bf16[352,128]{1,0:T(8,128)(2,1)S(1)}, u32[]{:S(2)}, u32[]{:S(2)}) collective-permute-start(bf16[352,128]{1,0:T(8,128)(2,1)S(1)} %multiply_convert_fusion.2.refs_0_), channel_id=1, source_target_pairs={{0,1},{1,0},{2,3},{3,2},{4,5},{5,4},{6,7},{7,6},{8,9},{9,8},{10,11... | collective-permute-start | bytes 270344 | tf_op jit(solution)/shard_map/ppermute | solution.py:363
  21.7 1.4 %collective-permute-start.9 = (bf16[416,128]{1,0:T(8,128)(2,1)S(1)}, bf16[416,128]{1,0:T(8,128)(2,1)S(1)}, u32[]{:S(2)}, u32[]{:S(2)}) collective-permute-start(bf16[416,128]{1,0:T(8,128)(2,1)S(1)} %multiply_convert_fusion.refs_2_), channel_id=1, source_target_pairs={{0,1},{1,0},{2,3},{3,2},{4,5},{5,4},{6,7},{7,6},{8,9},{9,8},{10,11... | collective-permute-start | bytes 319496 | tf_op jit(solution)/shard_map/ppermute | solution.py:363

commit v8 on v7

--- a/solution.py
+++ b/solution.py
@@ -12,8 +12,8 @@
 HBM = pl.BlockSpec(memory_space=pltpu.HBM)
 PART_SCALE = 256.0
 CHIP_SCALE = 128.0
-GROUP = 4
-PIECE = 32
+GROUP = 2
+PIECE = 16
 FIRST_PART = 11
 
 
@@ -306,7 +306,7 @@
         name="own_back",
     )(matrix, oblique, ratio)
 
-    def edge_rows(start, count, scale, name, after=None):
+    def edge_rows(start, count, scale, name):
         return pl.pallas_call(
             functools.partial(edge_back_kernel, slabs, own, start, scale),
             out_shape=array(jnp.float32, count, frames),
@@ -314,7 +314,7 @@
             out_specs=VMEM,
             compiler_params=params(),
             name=name,
-        )(matrix, beside_back if after is None else after, beside_forth, own_back)
+        )(matrix, beside_back, beside_forth, own_back)
 
     def wide(values):
         return values.astype(jnp.float32)
@@ -342,12 +342,11 @@
     for n, span in enumerate(spans):
         away = edge_rows(span.start, span.stop - span.start, PART_SCALE, f"edge_back_sent_{n}")
         got.append(lax.ppermute(away.astype(jnp.float16), "angle", pairs))
+    home = edge_rows(half_rows, half_rows, 1.0, "edge_back_kept")
     written = []
     for n, (at, end) in enumerate(zip(cuts[:-1], cuts[1:])):
         span = spans[n]
-        after, got[n] = lax.optimization_barrier((beside_back, got[n])) if n else (None, got[n])
-        home = edge_rows(half_rows + at, end - at, 1.0, f"edge_back_kept_{n}", after)
-        chip = (home + wide(got[n]) * (1.0 / PART_SCALE)) * CHIP_SCALE
+        chip = (home[span] + wide(got[n]) * (1.0 / PART_SCALE)) * CHIP_SCALE
         if angles == 4:
             chip = lax.optimization_barrier(chip.astype(jnp.float16))
             across = lax.ppermute(chip, "angle", [(a, a ^ 3) for a in range(angles)])

time: 23.9 us -> 23.7 us (level)
    pallas_call x4 -> x3, Pallas kernels: 1.07 us -> 0.9 us  [edge_rows(): pl.pallas_call(functools.partial(edge_back_kernel, slabs, own, start, sca...]
where the time goes in v8:
time: 23.7 us; the launch traced here: 23.5 us
  starting transfers between devices  9.56 us (40%)
  Pallas kernels  7.41 us (31%)
  waiting for transfers between devices  6.16 us (26%)
    ppermute x2, waiting for transfers between devices, body(): across = lax.ppermute(chip, 'angle', [(a, a ^ 3) for a in range(angles)])  3.87 us
    ppermute x1, starting transfers between devices, body(): got_back = lax.ppermute(edge_back, both, back)  2.6 us
    ppermute x2, starting transfers between devices, body(): across = lax.ppermute(chip, 'angle', [(a, a ^ 3) for a in range(angles)])  2.49 us
    pallas_call x1, Pallas kernels, body(): pl.pallas_call(functools.partial(edge_kernel, blocks, own, lines), out_sh...  2.23 us
    pallas_call x1, Pallas kernels, body(): pl.pallas_call(functools.partial(own_kernel, blocks, own, lines), out_sha...  2.21 us
    ppermute x1, starting transfers between devices, body(): beside_back = lax.ppermute(oblique, both, back)  2.07 us
    ppermute x1, waiting for transfers between devices, body(): beside_forth = lax.ppermute(oblique, both, forth)  1.64 us
    pallas_call x2, Pallas kernels, write_rows(): pl.pallas_call(functools.partial(write_rows_kernel, half_rows, places), o...  1.38 us
  transfers between devices with their start and end apart: 10, of which 6 were waited for; matrix products, arithmetic and copies ran while one was open for 1% of the time, Pallas kernels for 18%

profile of v8, /device:TPU:0, one launch (start us, length us, event | category | flops | bytes accessed | tf_op | source)
XLA Modules:
  0.0 23.5 jit_solution(7038107087061782180)
XLA Ops:
  0.0 2.2 %edge_partials.1 = (bf16[2,128,128]{2,1,0:T(8,128)(2,1)S(1)}, bf16[2,128,128]{2,1,0:T(8,128)(2,1)S(1)}, bf16[128,1536]{1,0:T(8,128)(2,1)S(1)}, bf16[86,128,128]{2,1,0:T(8,128)(2,1)S(1)}) custom-call(s32[86]{0:T(128)} %bitcast.10, s32[86]{0:T(128)} %bitcast.12, bf16[1536,128]{1,0:T(8,128)(2,1)} %activity_ref.1, bf16[86,128,128]{2,1,0:T(8,128)(2,1)} %bitcast.15), custom_call_target="tpu_custom_call" | custom-call | tf_op jit(solution)/shard_map/edge_partials/pallas_call | solution.py:248
  2.3 0.5 %collective-permute-start = (bf16[2,128,128]{2,1,0:T(8,128)(2,1)S(1)}, bf16[2,128,128]{2,1,0:T(8,128)(2,1)S(1)}, u32[]{:S(2)}, u32[]{:S(2)}) collective-permute-start(bf16[2,128,128]{2,1,0:T(8,128)(2,1)S(1)} %get-tuple-element.20), channel_id=1, source_target_pairs={{0,1},{1,5},{2,3},{3,7},{4,0},{5,9},{6,2},{7,11},{8,4},{9,13},{10,... | collective-permute-start | bytes 196616 | tf_op jit(solution)/shard_map/ppermute | solution.py:269
  2.8 2.6 %collective-permute-start.1 = (bf16[2,128,128]{2,1,0:T(8,128)(2,1)S(1)}, bf16[2,128,128]{2,1,0:T(8,128)(2,1)S(1)}, u32[]{:S(2)}, u32[]{:S(2)}) collective-permute-start(bf16[2,128,128]{2,1,0:T(8,128)(2,1)S(1)} %get-tuple-element.21), channel_id=1, source_target_pairs={{1,0},{5,1},{3,2},{7,3},{0,4},{9,5},{2,6},{11,7},{4,8},{13,9},{6,1... | collective-permute-start | bytes 196616 | tf_op jit(solution)/shard_map/ppermute | solution.py:270
  5.4 0.0 copy-done
  5.4 0.0 copy-done.1
  5.4 2.2 %own_partials.1 = (f32[2,128,128]{2,1,0:T(8,128)S(1)}, f32[2,128,128]{2,1,0:T(8,128)S(1)}, bf16[2,128,128]{2,1,0:T(8,128)(2,1)S(1)}, bf16[1536,1024]{1,0:T(8,128)(2,1)S(1)}, f32[768,128]{1,0:T(8,128)S(1)}) custom-call(s32[86]{0:T(128)S(1)} %bitcast.11, s32[86]{0:T(128)S(1)} %bitcast.13, s32[2]{0:T(128)S(1)} %bitcast.14, ...), custom_call_target="tpu_custom_call" | custom-call | tf_op jit(solution)/shard_map/own_partials/pallas_call | solution.py:272
  7.6 0.1 collective-permute-done.forth_ref
  7.7 0.0 collective-permute-done.1.back_ref
  7.7 0.1 oblique_ratios.1.oblique_ref
  7.9 0.4 %collective-permute-start.3 = (bf16[2,128,128]{2,1,0:T(8,128)(2,1)S(1)}, bf16[2,128,128]{2,1,0:T(8,128)(2,1)S(1)}, u32[]{:S(2)}, u32[]{:S(2)}) collective-permute-start(bf16[2,128,128]{2,1,0:T(8,128)(2,1)S(1)} %oblique_ratios.1.oblique_ref), channel_id=1, source_target_pairs={{0,1},{1,5},{2,3},{3,7},{4,0},{5,9},{6,2},{7,11},{8,4},{9,13},{10,... | collective-permute-start | bytes 196616 | tf_op jit(solution)/shard_map/ppermute | solution.py:298
  8.2 2.1 %collective-permute-start.2 = (bf16[2,128,128]{2,1,0:T(8,128)(2,1)S(1)}, bf16[2,128,128]{2,1,0:T(8,128)(2,1)S(1)}, u32[]{:S(2)}, u32[]{:S(2)}) collective-permute-start(bf16[2,128,128]{2,1,0:T(8,128)(2,1)S(1)} %oblique_ratios.1.oblique_ref), channel_id=1, source_target_pairs={{1,0},{5,1},{3,2},{7,3},{0,4},{9,5},{2,6},{11,7},{4,8},{13,9},{6,1... | collective-permute-start | bytes 196616 | tf_op jit(solution)/shard_map/ppermute | solution.py:299
  10.3 0.6 %own_back.1.own_ref = f32[1536,128]{1,0:T(8,128)S(1)} custom-call(bf16[1536,1024]{1,0:T(8,128)(2,1)S(1)} %get-tuple-element.19.matrix_ref, bf16[2,128,128]{2,1,0:T(8,128)(2,1)S(1)} %oblique_ratios.1.oblique_ref, bf16[2,128,128]{2,1,0:T(8,128)(2,1)S(1)} %get-tuple-element.24.ratio_ref), custom_call_target="tpu_custom_call" | custom-call | tf_op jit(solution)/shard_map/own_back/pallas_call | solution.py:300
  10.9 1.6 %collective-permute-done.3.forth_ref = bf16[2,128,128]{2,1,0:T(8,128)(2,1)S(1)} collective-permute-done((bf16[2,128,128]{2,1,0:T(8,128)(2,1)S(1)}, bf16[2,128,128]{2,1,0:T(8,128)(2,1)S(1)}, u32[]{:S(2)}, u32[]{:S(2)}) %collective-permute-start.3) | collective-permute-done | bytes 65568 | tf_op jit(solution)/shard_map/ppermute | solution.py:298
  12.5 0.0 collective-permute-done.2.back_ref
  12.5 0.3 %edge_back_sent_0.1 = f32[352,128]{1,0:T(8,128)S(1)} custom-call(bf16[1536,1024]{1,0:T(8,128)(2,1)S(1)} %get-tuple-element.19.matrix_ref, bf16[2,128,128]{2,1,0:T(8,128)(2,1)S(1)} %collective-permute-done.2.back_ref, bf16[2,128,128]{2,1,0:T(8,128)(2,1)S(1)} %collective-permute-done.3.forth_ref, f32[1536,128]{1,0:T(8,128)S(1)} %own_back.1.own_ref), custom_call_target="tpu_custom_call" | custom-call | tf_op jit(solution)/shard_map/edge_back_sent_0/pallas_call | solution.py:310
  12.8 0.8 %collective-permute-start.6 = (f16[352,128]{1,0:T(8,128)(2,1)S(1)}, f16[352,128]{1,0:T(8,128)(2,1)S(1)}, u32[]{:S(2)}, u32[]{:S(2)}) collective-permute-start(f16[352,128]{1,0:T(8,128)(2,1)S(1)} %convert_element_type.40), channel_id=1, source_target_pairs={{0,1},{1,0},{2,3},{3,2},{4,5},{5,4},{6,7},{7,6},{8,9},{9,8},{10,11... | collective-permute-start | bytes 270344 | tf_op jit(solution)/shard_map/ppermute | solution.py:344
  13.6 0.3 %edge_back_sent_1.1 = f32[416,128]{1,0:T(8,128)S(1)} custom-call(bf16[1536,1024]{1,0:T(8,128)(2,1)S(1)} %get-tuple-element.19.matrix_ref, bf16[2,128,128]{2,1,0:T(8,128)(2,1)S(1)} %collective-permute-done.2.back_ref, bf16[2,128,128]{2,1,0:T(8,128)(2,1)S(1)} %collective-permute-done.3.forth_ref, f32[1536,128]{1,0:T(8,128)S(1)} %own_back.1.own_ref), custom_call_target="tpu_custom_call" | custom-call | tf_op jit(solution)/shard_map/edge_back_sent_1/pallas_call | solution.py:310
  13.9 0.1 collective-permute-start.4
  14.0 0.4 %edge_back_kept.1 = f32[768,128]{1,0:T(8,128)S(1)} custom-call(bf16[1536,1024]{1,0:T(8,128)(2,1)S(1)} %get-tuple-element.19.matrix_ref, bf16[2,128,128]{2,1,0:T(8,128)(2,1)S(1)} %collective-permute-done.2.back_ref, bf16[2,128,128]{2,1,0:T(8,128)(2,1)S(1)} %collective-permute-done.3.forth_ref, f32[1536,128]{1,0:T(8,128)S(1)} %own_back.1.own_ref), custom_call_target="tpu_custom_call" | custom-call | tf_op jit(solution)/shard_map/edge_back_kept/pallas_call | solution.py:310
  14.4 0.2 collective-permute-done.6
  14.6 1.8 %collective-permute-start.7 = (f16[352,128]{1,0:T(8,128)(2,1)S(1)}, f16[352,128]{1,0:T(8,128)(2,1)S(1)}, u32[]{:S(2)}, u32[]{:S(2)}) collective-permute-start(f16[352,128]{1,0:T(8,128)(2,1)S(1)} %fusion.3), channel_id=1, source_target_pairs={{0,3},{1,2},{2,1},{3,0},{4,7},{5,6},{6,5},{7,4},{8,11},{9,10},{10,... | collective-permute-start | bytes 270344 | tf_op jit(solution)/shard_map/ppermute | solution.py:352
  16.3 0.0 collective-permute-done.4
  16.3 0.1 fusion.1
  16.4 0.7 %collective-permute-start.5 = (f16[416,128]{1,0:T(8,128)(2,1)S(1)}, f16[416,128]{1,0:T(8,128)(2,1)S(1)}, u32[]{:S(2)}, u32[]{:S(2)}) collective-permute-start(f16[416,128]{1,0:T(8,128)(2,1)S(1)} %fusion.1), channel_id=1, source_target_pairs={{0,3},{1,2},{2,1},{3,0},{4,7},{5,6},{6,5},{7,4},{8,11},{9,10},{10,... | collective-permute-start | bytes 319496 | tf_op jit(solution)/shard_map/ppermute | solution.py:352
  17.1 2.2 %collective-permute-done.7 = f16[352,128]{1,0:T(8,128)(2,1)S(1)} collective-permute-done((f16[352,128]{1,0:T(8,128)(2,1)S(1)}, f16[352,128]{1,0:T(8,128)(2,1)S(1)}, u32[]{:S(2)}, u32[]{:S(2)}) %collective-permute-start.7) | collective-permute-done | bytes 90144 | tf_op jit(solution)/shard_map/ppermute | solution.py:352
  19.4 0.4 %collective-permute-start.8 = (bf16[352,128]{1,0:T(8,128)(2,1)S(1)}, bf16[352,128]{1,0:T(8,128)(2,1)S(1)}, u32[]{:S(2)}, u32[]{:S(2)}) collective-permute-start(bf16[352,128]{1,0:T(8,128)(2,1)S(1)} %multiply_convert_fusion.1.refs_0_), channel_id=1, source_target_pairs={{0,1},{1,0},{2,3},{3,2},{4,5},{5,4},{6,7},{7,6},{8,9},{9,8},{10,11... | collective-permute-start | bytes 270344 | tf_op jit(solution)/shard_map/ppermute | solution.py:362
  19.8 1.6 %collective-permute-done.5 = f16[416,128]{1,0:T(8,128)(2,1)S(1)} collective-permute-done((f16[416,128]{1,0:T(8,128)(2,1)S(1)}, f16[416,128]{1,0:T(8,128)(2,1)S(1)}, u32[]{:S(2)}, u32[]{:S(2)}) %collective-permute-start.5) | collective-permute-done | bytes 106528 | tf_op jit(solution)/shard_map/ppermute | solution.py:352
  21.4 0.0 collective-permute-done.8.refs_1_
  21.5 0.3 %collective-permute-start.9 = (bf16[416,128]{1,0:T(8,128)(2,1)S(1)}, bf16[416,128]{1,0:T(8,128)(2,1)S(1)}, u32[]{:S(2)}, u32[]{:S(2)}) collective-permute-start(bf16[416,128]{1,0:T(8,128)(2,1)S(1)} %multiply_convert_fusion.refs_2_), channel_id=1, source_target_pairs={{0,1},{1,0},{2,3},{3,2},{4,5},{5,4},{6,7},{7,6},{8,9},{9,8},{10,11... | collective-permute-start | bytes 319496 | tf_op jit(solution)/shard_map/ppermute | solution.py:362
  21.8 0.7 %write_first.1.refs_1_ = bf16[1536,128]{1,0:T(8,128)(2,1)} custom-call(bf16[352,128]{1,0:T(8,128)(2,1)S(1)} %multiply_convert_fusion.1.refs_0_, bf16[352,128]{1,0:T(8,128)(2,1)S(1)} %collective-permute-done.8.refs_1_, bf16[416,128]{1,0:T(8,128)(2,1)S(1)} %multiply_convert_fusion.refs_2_), custom_call_target="tpu_custom_call" | custom-call | tf_op jit(solution)/shard_map/write_first/pallas_call | solution.py:326
  22.5 0.4 %collective-permute-done.9.refs_0_ = bf16[416,128]{1,0:T(8,128)(2,1)S(1)} collective-permute-done((bf16[416,128]{1,0:T(8,128)(2,1)S(1)}, bf16[416,128]{1,0:T(8,128)(2,1)S(1)}, u32[]{:S(2)}, u32[]{:S(2)}) %collective-permute-start.9) | collective-permute-done | bytes 106528 | tf_op jit(solution)/shard_map/ppermute | solution.py:362
  22.9 0.7 %write_last.1 = bf16[1536,128]{1,0:T(8,128)(2,1)} custom-call(bf16[416,128]{1,0:T(8,128)(2,1)S(1)} %collective-permute-done.9.refs_0_, bf16[1536,128]{1,0:T(8,128)(2,1)} %write_first.1.refs_1_), custom_call_target="tpu_custom_call", output_to_operand_aliasing={{}: (1, {})} | custom-call | tf_op jit(solution)/shard_map/write_last/pallas_call | solution.py:326
  (17 shorter events, 0.2 us)
Async XLA Ops:
  0.0 5.4 %copy-start = (bf16[1536,128]{1,0:T(8,128)(2,1)S(1)}, bf16[1536,128]{1,0:T(8,128)(2,1)}, u32[]{:S(2)}) copy-start(bf16[1536,128]{1,0:T(8,128)(2,1)} %activity_ref.1) | copy-start | bytes 1179652
  0.0 5.4 %copy-start.5 = (s32[1,1,86]{2,1,0:T(1,128)S(1)}, s32[1,1,86]{2,1,0:T(1,128)}, u32[]{:S(2)}) copy-start(s32[1,1,86]{2,1,0:T(1,128)} %param.12) | copy-start | bytes 1036
  0.0 5.4 %copy-start.4 = (s32[1,1,86]{2,1,0:T(1,128)S(1)}, s32[1,1,86]{2,1,0:T(1,128)}, u32[]{:S(2)}) copy-start(s32[1,1,86]{2,1,0:T(1,128)} %param.11) | copy-start | bytes 1036
  0.0 5.4 %copy-start.2 = (bf16[1,1,512,128]{3,2,1,0:T(8,128)(2,1)S(1)}, bf16[1,1,512,128]{3,2,1,0:T(8,128)(2,1)}, u32[]{:S(2)}) copy-start(bf16[1,1,512,128]{3,2,1,0:T(8,128)(2,1)} %param.15) | copy-start | bytes 393220
  0.0 5.4 %copy-start.1 = (s32[1,1,512,128]{3,2,1,0:T(8,128)S(1)}, s32[1,1,512,128]{3,2,1,0:T(8,128)}, u32[]{:S(2)}) copy-start(s32[1,1,512,128]{3,2,1,0:T(8,128)} %param.14) | copy-start | bytes 786436
  0.0 5.4 %copy-start.6 = (s32[1,1,2]{2,1,0:T(1,128)S(1)}, s32[1,1,2]{2,1,0:T(1,128)}, u32[]{:S(2)}) copy-start(s32[1,1,2]{2,1,0:T(1,128)} %param.13) | copy-start | bytes 28
  0.0 5.4 %copy-start.3 = (f32[1536]{0:T(1024)S(1)}, f32[1536]{0:T(1024)}, u32[]{:S(2)}) copy-start(f32[1536]{0:T(1024)} %param.9) | copy-start | bytes 18436
  2.3 5.4 %collective-permute-start = (bf16[2,128,128]{2,1,0:T(8,128)(2,1)S(1)}, bf16[2,128,128]{2,1,0:T(8,128)(2,1)S(1)}, u32[]{:S(2)}, u32[]{:S(2)}) collective-permute-start(bf16[2,128,128]{2,1,0:T(8,128)(2,1)S(1)} %get-tuple-element.20), channel_id=1, source_target_pairs={{0,1},{1,5},{2,3},{3,7},{4,0},{5,9},{6,2},{7,11},{8,4},{9,13},{10,... | collective-permute-start | bytes 196616 | tf_op jit(solution)/shard_map/ppermute | solution.py:269
  2.8 5.0 %collective-permute-start.1 = (bf16[2,128,128]{2,1,0:T(8,128)(2,1)S(1)}, bf16[2,128,128]{2,1,0:T(8,128)(2,1)S(1)}, u32[]{:S(2)}, u32[]{:S(2)}) collective-permute-start(bf16[2,128,128]{2,1,0:T(8,128)(2,1)S(1)} %get-tuple-element.21), channel_id=1, source_target_pairs={{1,0},{5,1},{3,2},{7,3},{0,4},{9,5},{2,6},{11,7},{4,8},{13,9},{6,1... | collective-permute-start | bytes 196616 | tf_op jit(solution)/shard_map/ppermute | solution.py:270
  7.9 4.7 %collective-permute-start.3 = (bf16[2,128,128]{2,1,0:T(8,128)(2,1)S(1)}, bf16[2,128,128]{2,1,0:T(8,128)(2,1)S(1)}, u32[]{:S(2)}, u32[]{:S(2)}) collective-permute-start(bf16[2,128,128]{2,1,0:T(8,128)(2,1)S(1)} %oblique_ratios.1.oblique_ref), channel_id=1, source_target_pairs={{0,1},{1,5},{2,3},{3,7},{4,0},{5,9},{6,2},{7,11},{8,4},{9,13},{10,... | collective-permute-start | bytes 196616 | tf_op jit(solution)/shard_map/ppermute | solution.py:298
  8.2 4.3 %collective-permute-start.2 = (bf16[2,128,128]{2,1,0:T(8,128)(2,1)S(1)}, bf16[2,128,128]{2,1,0:T(8,128)(2,1)S(1)}, u32[]{:S(2)}, u32[]{:S(2)}) collective-permute-start(bf16[2,128,128]{2,1,0:T(8,128)(2,1)S(1)} %oblique_ratios.1.oblique_ref), channel_id=1, source_target_pairs={{1,0},{5,1},{3,2},{7,3},{0,4},{9,5},{2,6},{11,7},{4,8},{13,9},{6,1... | collective-permute-start | bytes 196616 | tf_op jit(solution)/shard_map/ppermute | solution.py:299
  12.8 1.7 %collective-permute-start.6 = (f16[352,128]{1,0:T(8,128)(2,1)S(1)}, f16[352,128]{1,0:T(8,128)(2,1)S(1)}, u32[]{:S(2)}, u32[]{:S(2)}) collective-permute-start(f16[352,128]{1,0:T(8,128)(2,1)S(1)} %convert_element_type.40), channel_id=1, source_target_pairs={{0,1},{1,0},{2,3},{3,2},{4,5},{5,4},{6,7},{7,6},{8,9},{9,8},{10,11... | collective-permute-start | bytes 270344 | tf_op jit(solution)/shard_map/ppermute | solution.py:344
  13.9 2.5 %collective-permute-start.4 = (f16[416,128]{1,0:T(8,128)(2,1)S(1)}, f16[416,128]{1,0:T(8,128)(2,1)S(1)}, u32[]{:S(2)}, u32[]{:S(2)}) collective-permute-start(f16[416,128]{1,0:T(8,128)(2,1)S(1)} %convert_element_type.36), channel_id=1, source_target_pairs={{0,1},{1,0},{2,3},{3,2},{4,5},{5,4},{6,7},{7,6},{8,9},{9,8},{10,11... | collective-permute-start | bytes 319496 | tf_op jit(solution)/shard_map/ppermute | solution.py:344
  14.6 4.8 %collective-permute-start.7 = (f16[352,128]{1,0:T(8,128)(2,1)S(1)}, f16[352,128]{1,0:T(8,128)(2,1)S(1)}, u32[]{:S(2)}, u32[]{:S(2)}) collective-permute-start(f16[352,128]{1,0:T(8,128)(2,1)S(1)} %fusion.3), channel_id=1, source_target_pairs={{0,3},{1,2},{2,1},{3,0},{4,7},{5,6},{6,5},{7,4},{8,11},{9,10},{10,... | collective-permute-start | bytes 270344 | tf_op jit(solution)/shard_map/ppermute | solution.py:352
  16.4 5.0 %collective-permute-start.5 = (f16[416,128]{1,0:T(8,128)(2,1)S(1)}, f16[416,128]{1,0:T(8,128)(2,1)S(1)}, u32[]{:S(2)}, u32[]{:S(2)}) collective-permute-start(f16[416,128]{1,0:T(8,128)(2,1)S(1)} %fusion.1), channel_id=1, source_target_pairs={{0,3},{1,2},{2,1},{3,0},{4,7},{5,6},{6,5},{7,4},{8,11},{9,10},{10,... | collective-permute-start | bytes 319496 | tf_op jit(solution)/shard_map/ppermute | solution.py:352
  19.4 2.0 %collective-permute-start.8 = (bf16[352,128]{1,0:T(8,128)(2,1)S(1)}, bf16[352,128]{1,0:T(8,128)(2,1)S(1)}, u32[]{:S(2)}, u32[]{:S(2)}) collective-permute-start(bf16[352,128]{1,0:T(8,128)(2,1)S(1)} %multiply_convert_fusion.1.refs_0_), channel_id=1, source_target_pairs={{0,1},{1,0},{2,3},{3,2},{4,5},{5,4},{6,7},{7,6},{8,9},{9,8},{10,11... | collective-permute-start | bytes 270344 | tf_op jit(solution)/shard_map/ppermute | solution.py:362
  21.5 1.4 %collective-permute-start.9 = (bf16[416,128]{1,0:T(8,128)(2,1)S(1)}, bf16[416,128]{1,0:T(8,128)(2,1)S(1)}, u32[]{:S(2)}, u32[]{:S(2)}) collective-permute-start(bf16[416,128]{1,0:T(8,128)(2,1)S(1)} %multiply_convert_fusion.refs_2_), channel_id=1, source_target_pairs={{0,1},{1,0},{2,3},{3,2},{4,5},{5,4},{6,7},{7,6},{8,9},{9,8},{10,11... | collective-permute-start | bytes 319496 | tf_op jit(solution)/shard_map/ppermute | solution.py:362

commit v9 on v8

--- a/solution.py
+++ b/solution.py
@@ -14,7 +14,7 @@
 CHIP_SCALE = 128.0
 GROUP = 2
 PIECE = 16
-FIRST_PART = 11
+FIRST_PART = 7
 
 
 def params(mebibytes=16):
@@ -203,7 +203,7 @@
     copies = []
     for n, (turn, start) in enumerate(places):
         count = refs[n].shape[0]
-        at = pl.multiple_of((odd + turn) % 2 * half_rows + start, 32)
+        at = pl.multiple_of((odd + turn) % 2 * half_rows + start, 16)
         copies.append(
             pltpu.make_async_copy(refs[n], out_hbm.at[pl.ds(at, count)], sem.at[n])
         )
@@ -335,8 +335,7 @@
         )(*values, *before)
 
     pairs = [(a, a ^ 1) for a in range(angles)]
-    cuts = [0, FIRST_PART * half_rows // 24, half_rows]
-    cuts = [0, FIRST_PART * half_rows // 24, half_rows]
+    cuts = [0, FIRST_PART * half_rows // 16, half_rows]
     spans = [slice(at, end) for at, end in zip(cuts[:-1], cuts[1:])]
     got = []
     for n, span in enumerate(spans):

time: 23.7 us -> 23.6 us (level)
  starting transfers between devices: 9.56 us -> 9.29 us
    ppermute x2, starting transfers between devices: 0.69 us -> 0.43 us  [body(): rows_away = lax.ppermute(rows_home, 'angle', pairs)]
    ppermute x2, waiting for transfers between devices: 3.87 us -> 4.13 us  [body(): across = lax.ppermute(chip, 'angle', [(a, a ^ 3) for a in range(angles)])]
where the time goes in v9:
time: 23.6 us; the launch traced here: 23.4 us
  starting transfers between devices  9.29 us (39%)
  Pallas kernels  7.43 us (31%)
  waiting for transfers between devices  6.33 us (27%)
    ppermute x2, waiting for transfers between devices, body(): across = lax.ppermute(chip, 'angle', [(a, a ^ 3) for a in range(angles)])  4.13 us
    ppermute x1, starting transfers between devices, body(): got_back = lax.ppermute(edge_back, both, back)  2.6 us
    ppermute x2, starting transfers between devices, body(): across = lax.ppermute(chip, 'angle', [(a, a ^ 3) for a in range(angles)])  2.5 us
    pallas_call x1, Pallas kernels, body(): pl.pallas_call(functools.partial(edge_kernel, blocks, own, lines), out_sh...  2.23 us
    pallas_call x1, Pallas kernels, body(): pl.pallas_call(functools.partial(own_kernel, blocks, own, lines), out_sha...  2.21 us
    ppermute x1, starting transfers between devices, body(): beside_back = lax.ppermute(oblique, both, back)  2.07 us
    ppermute x1, waiting for transfers between devices, body(): beside_forth = lax.ppermute(oblique, both, forth)  1.64 us
    pallas_call x2, Pallas kernels, write_rows(): pl.pallas_call(functools.partial(write_rows_kernel, half_rows, places), o...  1.38 us
  transfers between devices with their start and end apart: 10, of which 6 were waited for; matrix products, arithmetic and copies ran while one was open for 1% of the time, Pallas kernels for 18%

profile of v9, /device:TPU:0, one launch (start us, length us, event | category | flops | bytes accessed | tf_op | source)
XLA Modules:
  0.0 23.4 jit_solution(2348533284676833306)
XLA Ops:
  0.0 0.0 copy-start.6
  0.0 0.0 copy-start.3
  0.0 2.2 %edge_partials.1 = (bf16[2,128,128]{2,1,0:T(8,128)(2,1)S(1)}, bf16[2,128,128]{2,1,0:T(8,128)(2,1)S(1)}, bf16[128,1536]{1,0:T(8,128)(2,1)S(1)}, bf16[86,128,128]{2,1,0:T(8,128)(2,1)S(1)}) custom-call(s32[86]{0:T(128)} %bitcast.10, s32[86]{0:T(128)} %bitcast.12, bf16[1536,128]{1,0:T(8,128)(2,1)} %activity_ref.1, bf16[86,128,128]{2,1,0:T(8,128)(2,1)} %bitcast.15), custom_call_target="tpu_custom_call" | custom-call | tf_op jit(solution)/shard_map/edge_partials/pallas_call | solution.py:248
  2.3 0.5 %collective-permute-start = (bf16[2,128,128]{2,1,0:T(8,128)(2,1)S(1)}, bf16[2,128,128]{2,1,0:T(8,128)(2,1)S(1)}, u32[]{:S(2)}, u32[]{:S(2)}) collective-permute-start(bf16[2,128,128]{2,1,0:T(8,128)(2,1)S(1)} %get-tuple-element.20), channel_id=1, source_target_pairs={{0,1},{1,5},{2,3},{3,7},{4,0},{5,9},{6,2},{7,11},{8,4},{9,13},{10,... | collective-permute-start | bytes 196616 | tf_op jit(solution)/shard_map/ppermute | solution.py:269
  2.8 2.6 %collective-permute-start.1 = (bf16[2,128,128]{2,1,0:T(8,128)(2,1)S(1)}, bf16[2,128,128]{2,1,0:T(8,128)(2,1)S(1)}, u32[]{:S(2)}, u32[]{:S(2)}) collective-permute-start(bf16[2,128,128]{2,1,0:T(8,128)(2,1)S(1)} %get-tuple-element.21), channel_id=1, source_target_pairs={{1,0},{5,1},{3,2},{7,3},{0,4},{9,5},{2,6},{11,7},{4,8},{13,9},{6,1... | collective-permute-start | bytes 196616 | tf_op jit(solution)/shard_map/ppermute | solution.py:270
  5.4 2.2 %own_partials.1 = (f32[2,128,128]{2,1,0:T(8,128)S(1)}, f32[2,128,128]{2,1,0:T(8,128)S(1)}, bf16[2,128,128]{2,1,0:T(8,128)(2,1)S(1)}, bf16[1536,1024]{1,0:T(8,128)(2,1)S(1)}, f32[768,128]{1,0:T(8,128)S(1)}) custom-call(s32[86]{0:T(128)S(1)} %bitcast.11, s32[86]{0:T(128)S(1)} %bitcast.13, s32[2]{0:T(128)S(1)} %bitcast.14, ...), custom_call_target="tpu_custom_call" | custom-call | tf_op jit(solution)/shard_map/own_partials/pallas_call | solution.py:272
  7.6 0.1 collective-permute-done.forth_ref
  7.7 0.0 collective-permute-done.1.back_ref
  7.7 0.1 oblique_ratios.1.oblique_ref
  7.9 0.4 %collective-permute-start.3 = (bf16[2,128,128]{2,1,0:T(8,128)(2,1)S(1)}, bf16[2,128,128]{2,1,0:T(8,128)(2,1)S(1)}, u32[]{:S(2)}, u32[]{:S(2)}) collective-permute-start(bf16[2,128,128]{2,1,0:T(8,128)(2,1)S(1)} %oblique_ratios.1.oblique_ref), channel_id=1, source_target_pairs={{0,1},{1,5},{2,3},{3,7},{4,0},{5,9},{6,2},{7,11},{8,4},{9,13},{10,... | collective-permute-start | bytes 196616 | tf_op jit(solution)/shard_map/ppermute | solution.py:298
  8.2 2.1 %collective-permute-start.2 = (bf16[2,128,128]{2,1,0:T(8,128)(2,1)S(1)}, bf16[2,128,128]{2,1,0:T(8,128)(2,1)S(1)}, u32[]{:S(2)}, u32[]{:S(2)}) collective-permute-start(bf16[2,128,128]{2,1,0:T(8,128)(2,1)S(1)} %oblique_ratios.1.oblique_ref), channel_id=1, source_target_pairs={{1,0},{5,1},{3,2},{7,3},{0,4},{9,5},{2,6},{11,7},{4,8},{13,9},{6,1... | collective-permute-start | bytes 196616 | tf_op jit(solution)/shard_map/ppermute | solution.py:299
  10.3 0.6 %own_back.1.own_ref = f32[1536,128]{1,0:T(8,128)S(1)} custom-call(bf16[1536,1024]{1,0:T(8,128)(2,1)S(1)} %get-tuple-element.19.matrix_ref, bf16[2,128,128]{2,1,0:T(8,128)(2,1)S(1)} %oblique_ratios.1.oblique_ref, bf16[2,128,128]{2,1,0:T(8,128)(2,1)S(1)} %get-tuple-element.24.ratio_ref), custom_call_target="tpu_custom_call" | custom-call | tf_op jit(solution)/shard_map/own_back/pallas_call | solution.py:300
  10.9 1.6 %collective-permute-done.3.forth_ref = bf16[2,128,128]{2,1,0:T(8,128)(2,1)S(1)} collective-permute-done((bf16[2,128,128]{2,1,0:T(8,128)(2,1)S(1)}, bf16[2,128,128]{2,1,0:T(8,128)(2,1)S(1)}, u32[]{:S(2)}, u32[]{:S(2)}) %collective-permute-start.3) | collective-permute-done | bytes 65568 | tf_op jit(solution)/shard_map/ppermute | solution.py:298
  12.5 0.0 collective-permute-done.2.back_ref
  12.5 0.3 %edge_back_sent_0.1 = f32[336,128]{1,0:T(8,128)S(1)} custom-call(bf16[1536,1024]{1,0:T(8,128)(2,1)S(1)} %get-tuple-element.19.matrix_ref, bf16[2,128,128]{2,1,0:T(8,128)(2,1)S(1)} %collective-permute-done.2.back_ref, bf16[2,128,128]{2,1,0:T(8,128)(2,1)S(1)} %collective-permute-done.3.forth_ref, f32[1536,128]{1,0:T(8,128)S(1)} %own_back.1.own_ref), custom_call_target="tpu_custom_call" | custom-call | tf_op jit(solution)/shard_map/edge_back_sent_0/pallas_call | solution.py:310
  12.8 0.8 %collective-permute-start.6 = (f16[336,128]{1,0:T(8,128)(2,1)S(1)}, f16[336,128]{1,0:T(8,128)(2,1)S(1)}, u32[]{:S(2)}, u32[]{:S(2)}) collective-permute-start(f16[336,128]{1,0:T(8,128)(2,1)S(1)} %convert_element_type.40), channel_id=1, source_target_pairs={{0,1},{1,0},{2,3},{3,2},{4,5},{5,4},{6,7},{7,6},{8,9},{9,8},{10,11... | collective-permute-start | bytes 258056 | tf_op jit(solution)/shard_map/ppermute | solution.py:343
  13.6 0.3 %edge_back_sent_1.1 = f32[432,128]{1,0:T(8,128)S(1)} custom-call(bf16[1536,1024]{1,0:T(8,128)(2,1)S(1)} %get-tuple-element.19.matrix_ref, bf16[2,128,128]{2,1,0:T(8,128)(2,1)S(1)} %collective-permute-done.2.back_ref, bf16[2,128,128]{2,1,0:T(8,128)(2,1)S(1)} %collective-permute-done.3.forth_ref, f32[1536,128]{1,0:T(8,128)S(1)} %own_back.1.own_ref), custom_call_target="tpu_custom_call" | custom-call | tf_op jit(solution)/shard_map/edge_back_sent_1/pallas_call | solution.py:310
  13.9 0.1 collective-permute-start.4
  14.0 0.4 %edge_back_kept.1 = f32[768,128]{1,0:T(8,128)S(1)} custom-call(bf16[1536,1024]{1,0:T(8,128)(2,1)S(1)} %get-tuple-element.19.matrix_ref, bf16[2,128,128]{2,1,0:T(8,128)(2,1)S(1)} %collective-permute-done.2.back_ref, bf16[2,128,128]{2,1,0:T(8,128)(2,1)S(1)} %collective-permute-done.3.forth_ref, f32[1536,128]{1,0:T(8,128)S(1)} %own_back.1.own_ref), custom_call_target="tpu_custom_call" | custom-call | tf_op jit(solution)/shard_map/edge_back_kept/pallas_call | solution.py:310
  14.4 0.1 collective-permute-done.6
  14.5 1.8 %collective-permute-start.7 = (f16[336,128]{1,0:T(8,128)(2,1)S(1)}, f16[336,128]{1,0:T(8,128)(2,1)S(1)}, u32[]{:S(2)}, u32[]{:S(2)}) collective-permute-start(f16[336,128]{1,0:T(8,128)(2,1)S(1)} %fusion.3), channel_id=1, source_target_pairs={{0,3},{1,2},{2,1},{3,0},{4,7},{5,6},{6,5},{7,4},{8,11},{9,10},{10,... | collective-permute-start | bytes 258056 | tf_op jit(solution)/shard_map/ppermute | solution.py:351
  16.3 0.0 collective-permute-done.4
  16.4 0.7 %collective-permute-start.5 = (f16[432,128]{1,0:T(8,128)(2,1)S(1)}, f16[432,128]{1,0:T(8,128)(2,1)S(1)}, u32[]{:S(2)}, u32[]{:S(2)}) collective-permute-start(f16[432,128]{1,0:T(8,128)(2,1)S(1)} %fusion.1), channel_id=1, source_target_pairs={{0,3},{1,2},{2,1},{3,0},{4,7},{5,6},{6,5},{7,4},{8,11},{9,10},{10,... | collective-permute-start | bytes 331784 | tf_op jit(solution)/shard_map/ppermute | solution.py:351
  17.1 2.2 %collective-permute-done.7 = f16[336,128]{1,0:T(8,128)(2,1)S(1)} collective-permute-done((f16[336,128]{1,0:T(8,128)(2,1)S(1)}, f16[336,128]{1,0:T(8,128)(2,1)S(1)}, u32[]{:S(2)}, u32[]{:S(2)}) %collective-permute-start.7) | collective-permute-done | bytes 86048 | tf_op jit(solution)/shard_map/ppermute | solution.py:351
  19.3 0.1 collective-permute-start.8
  19.4 2.0 %collective-permute-done.5 = f16[432,128]{1,0:T(8,128)(2,1)S(1)} collective-permute-done((f16[432,128]{1,0:T(8,128)(2,1)S(1)}, f16[432,128]{1,0:T(8,128)(2,1)S(1)}, u32[]{:S(2)}, u32[]{:S(2)}) %collective-permute-start.5) | collective-permute-done | bytes 110624 | tf_op jit(solution)/shard_map/ppermute | solution.py:351
  21.3 0.0 collective-permute-done.8.refs_1_
  21.3 0.1 multiply_convert_fusion.refs_2_
  21.4 0.4 %collective-permute-start.9 = (bf16[432,128]{1,0:T(8,128)(2,1)S(1)}, bf16[432,128]{1,0:T(8,128)(2,1)S(1)}, u32[]{:S(2)}, u32[]{:S(2)}) collective-permute-start(bf16[432,128]{1,0:T(8,128)(2,1)S(1)} %multiply_convert_fusion.refs_2_), channel_id=1, source_target_pairs={{0,1},{1,0},{2,3},{3,2},{4,5},{5,4},{6,7},{7,6},{8,9},{9,8},{10,11... | collective-permute-start | bytes 331784 | tf_op jit(solution)/shard_map/ppermute | solution.py:361
  21.8 0.7 %write_first.1.refs_1_ = bf16[1536,128]{1,0:T(8,128)(2,1)} custom-call(bf16[336,128]{1,0:T(8,128)(2,1)S(1)} %multiply_convert_fusion.1.refs_0_, bf16[336,128]{1,0:T(8,128)(2,1)S(1)} %collective-permute-done.8.refs_1_, bf16[432,128]{1,0:T(8,128)(2,1)S(1)} %multiply_convert_fusion.refs_2_), custom_call_target="tpu_custom_call" | custom-call | tf_op jit(solution)/shard_map/write_first/pallas_call | solution.py:326
  22.5 0.3 %collective-permute-done.9.refs_0_ = bf16[432,128]{1,0:T(8,128)(2,1)S(1)} collective-permute-done((bf16[432,128]{1,0:T(8,128)(2,1)S(1)}, bf16[432,128]{1,0:T(8,128)(2,1)S(1)}, u32[]{:S(2)}, u32[]{:S(2)}) %collective-permute-start.9) | collective-permute-done | bytes 110624 | tf_op jit(solution)/shard_map/ppermute | solution.py:361
  22.8 0.7 %write_last.1 = bf16[1536,128]{1,0:T(8,128)(2,1)} custom-call(bf16[432,128]{1,0:T(8,128)(2,1)S(1)} %collective-permute-done.9.refs_0_, bf16[1536,128]{1,0:T(8,128)(2,1)} %write_first.1.refs_1_), custom_call_target="tpu_custom_call", output_to_operand_aliasing={{}: (1, {})} | custom-call | tf_op jit(solution)/shard_map/write_last/pallas_call | solution.py:326
  (17 shorter events, 0.2 us)
Async XLA Ops:
  0.0 5.4 %copy-start = (bf16[1536,128]{1,0:T(8,128)(2,1)S(1)}, bf16[1536,128]{1,0:T(8,128)(2,1)}, u32[]{:S(2)}) copy-start(bf16[1536,128]{1,0:T(8,128)(2,1)} %activity_ref.1) | copy-start | bytes 1179652
  0.0 5.4 %copy-start.5 = (s32[1,1,86]{2,1,0:T(1,128)S(1)}, s32[1,1,86]{2,1,0:T(1,128)}, u32[]{:S(2)}) copy-start(s32[1,1,86]{2,1,0:T(1,128)} %param.12) | copy-start | bytes 1036
  0.0 5.4 %copy-start.4 = (s32[1,1,86]{2,1,0:T(1,128)S(1)}, s32[1,1,86]{2,1,0:T(1,128)}, u32[]{:S(2)}) copy-start(s32[1,1,86]{2,1,0:T(1,128)} %param.11) | copy-start | bytes 1036
  0.0 5.4 %copy-start.2 = (bf16[1,1,512,128]{3,2,1,0:T(8,128)(2,1)S(1)}, bf16[1,1,512,128]{3,2,1,0:T(8,128)(2,1)}, u32[]{:S(2)}) copy-start(bf16[1,1,512,128]{3,2,1,0:T(8,128)(2,1)} %param.15) | copy-start | bytes 393220
  0.0 5.4 %copy-start.1 = (s32[1,1,512,128]{3,2,1,0:T(8,128)S(1)}, s32[1,1,512,128]{3,2,1,0:T(8,128)}, u32[]{:S(2)}) copy-start(s32[1,1,512,128]{3,2,1,0:T(8,128)} %param.14) | copy-start | bytes 786436
  0.0 5.4 %copy-start.6 = (s32[1,1,2]{2,1,0:T(1,128)S(1)}, s32[1,1,2]{2,1,0:T(1,128)}, u32[]{:S(2)}) copy-start(s32[1,1,2]{2,1,0:T(1,128)} %param.13) | copy-start | bytes 28
  0.0 5.4 %copy-start.3 = (f32[1536]{0:T(1024)S(1)}, f32[1536]{0:T(1024)}, u32[]{:S(2)}) copy-start(f32[1536]{0:T(1024)} %param.9) | copy-start | bytes 18436
  2.3 5.4 %collective-permute-start = (bf16[2,128,128]{2,1,0:T(8,128)(2,1)S(1)}, bf16[2,128,128]{2,1,0:T(8,128)(2,1)S(1)}, u32[]{:S(2)}, u32[]{:S(2)}) collective-permute-start(bf16[2,128,128]{2,1,0:T(8,128)(2,1)S(1)} %get-tuple-element.20), channel_id=1, source_target_pairs={{0,1},{1,5},{2,3},{3,7},{4,0},{5,9},{6,2},{7,11},{8,4},{9,13},{10,... | collective-permute-start | bytes 196616 | tf_op jit(solution)/shard_map/ppermute | solution.py:269
  2.8 5.0 %collective-permute-start.1 = (bf16[2,128,128]{2,1,0:T(8,128)(2,1)S(1)}, bf16[2,128,128]{2,1,0:T(8,128)(2,1)S(1)}, u32[]{:S(2)}, u32[]{:S(2)}) collective-permute-start(bf16[2,128,128]{2,1,0:T(8,128)(2,1)S(1)} %get-tuple-element.21), channel_id=1, source_target_pairs={{1,0},{5,1},{3,2},{7,3},{0,4},{9,5},{2,6},{11,7},{4,8},{13,9},{6,1... | collective-permute-start | bytes 196616 | tf_op jit(solution)/shard_map/ppermute | solution.py:270
  7.9 4.7 %collective-permute-start.3 = (bf16[2,128,128]{2,1,0:T(8,128)(2,1)S(1)}, bf16[2,128,128]{2,1,0:T(8,128)(2,1)S(1)}, u32[]{:S(2)}, u32[]{:S(2)}) collective-permute-start(bf16[2,128,128]{2,1,0:T(8,128)(2,1)S(1)} %oblique_ratios.1.oblique_ref), channel_id=1, source_target_pairs={{0,1},{1,5},{2,3},{3,7},{4,0},{5,9},{6,2},{7,11},{8,4},{9,13},{10,... | collective-permute-start | bytes 196616 | tf_op jit(solution)/shard_map/ppermute | solution.py:298
  8.2 4.3 %collective-permute-start.2 = (bf16[2,128,128]{2,1,0:T(8,128)(2,1)S(1)}, bf16[2,128,128]{2,1,0:T(8,128)(2,1)S(1)}, u32[]{:S(2)}, u32[]{:S(2)}) collective-permute-start(bf16[2,128,128]{2,1,0:T(8,128)(2,1)S(1)} %oblique_ratios.1.oblique_ref), channel_id=1, source_target_pairs={{1,0},{5,1},{3,2},{7,3},{0,4},{9,5},{2,6},{11,7},{4,8},{13,9},{6,1... | collective-permute-start | bytes 196616 | tf_op jit(solution)/shard_map/ppermute | solution.py:299
  12.8 1.7 %collective-permute-start.6 = (f16[336,128]{1,0:T(8,128)(2,1)S(1)}, f16[336,128]{1,0:T(8,128)(2,1)S(1)}, u32[]{:S(2)}, u32[]{:S(2)}) collective-permute-start(f16[336,128]{1,0:T(8,128)(2,1)S(1)} %convert_element_type.40), channel_id=1, source_target_pairs={{0,1},{1,0},{2,3},{3,2},{4,5},{5,4},{6,7},{7,6},{8,9},{9,8},{10,11... | collective-permute-start | bytes 258056 | tf_op jit(solution)/shard_map/ppermute | solution.py:343
  13.9 2.4 %collective-permute-start.4 = (f16[432,128]{1,0:T(8,128)(2,1)S(1)}, f16[432,128]{1,0:T(8,128)(2,1)S(1)}, u32[]{:S(2)}, u32[]{:S(2)}) collective-permute-start(f16[432,128]{1,0:T(8,128)(2,1)S(1)} %convert_element_type.36), channel_id=1, source_target_pairs={{0,1},{1,0},{2,3},{3,2},{4,5},{5,4},{6,7},{7,6},{8,9},{9,8},{10,11... | collective-permute-start | bytes 331784 | tf_op jit(solution)/shard_map/ppermute | solution.py:343
  14.5 4.7 %collective-permute-start.7 = (f16[336,128]{1,0:T(8,128)(2,1)S(1)}, f16[336,128]{1,0:T(8,128)(2,1)S(1)}, u32[]{:S(2)}, u32[]{:S(2)}) collective-permute-start(f16[336,128]{1,0:T(8,128)(2,1)S(1)} %fusion.3), channel_id=1, source_target_pairs={{0,3},{1,2},{2,1},{3,0},{4,7},{5,6},{6,5},{7,4},{8,11},{9,10},{10,... | collective-permute-start | bytes 258056 | tf_op jit(solution)/shard_map/ppermute | solution.py:351
  16.4 5.0 %collective-permute-start.5 = (f16[432,128]{1,0:T(8,128)(2,1)S(1)}, f16[432,128]{1,0:T(8,128)(2,1)S(1)}, u32[]{:S(2)}, u32[]{:S(2)}) collective-permute-start(f16[432,128]{1,0:T(8,128)(2,1)S(1)} %fusion.1), channel_id=1, source_target_pairs={{0,3},{1,2},{2,1},{3,0},{4,7},{5,6},{6,5},{7,4},{8,11},{9,10},{10,... | collective-permute-start | bytes 331784 | tf_op jit(solution)/shard_map/ppermute | solution.py:351
  19.3 2.1 %collective-permute-start.8 = (bf16[336,128]{1,0:T(8,128)(2,1)S(1)}, bf16[336,128]{1,0:T(8,128)(2,1)S(1)}, u32[]{:S(2)}, u32[]{:S(2)}) collective-permute-start(bf16[336,128]{1,0:T(8,128)(2,1)S(1)} %multiply_convert_fusion.1.refs_0_), channel_id=1, source_target_pairs={{0,1},{1,0},{2,3},{3,2},{4,5},{5,4},{6,7},{7,6},{8,9},{9,8},{10,11... | collective-permute-start | bytes 258056 | tf_op jit(solution)/shard_map/ppermute | solution.py:361
  21.4 1.4 %collective-permute-start.9 = (bf16[432,128]{1,0:T(8,128)(2,1)S(1)}, bf16[432,128]{1,0:T(8,128)(2,1)S(1)}, u32[]{:S(2)}, u32[]{:S(2)}) collective-permute-start(bf16[432,128]{1,0:T(8,128)(2,1)S(1)} %multiply_convert_fusion.refs_2_), channel_id=1, source_target_pairs={{0,1},{1,0},{2,3},{3,2},{4,5},{5,4},{6,7},{7,6},{8,9},{9,8},{10,11... | collective-permute-start | bytes 331784 | tf_op jit(solution)/shard_map/ppermute | solution.py:361

commit v10 on v9

--- a/solution.py
+++ b/solution.py
@@ -181,7 +181,7 @@
         gain_ref[n * size : (n + 1) * size] = gain * (1.0 / CHIP_SCALE)
 
 
-def edge_back_kernel(slabs, own, start, scale, matrix_ref, back_ref, forth_ref, own_ref, out_ref):
+def edge_back_kernel(slabs, own, start, matrix_ref, back_ref, forth_ref, own_ref, out_ref):
     size = forth_ref.shape[1]
     rows = out_ref.shape[0]
     odd, has_forth, has_back = place(slabs)
@@ -194,7 +194,7 @@
     sums = jnp.dot(
         matrix_ref[start : start + rows, own * size :], ratios, preferred_element_type=jnp.float32
     )
-    out_ref[...] = (sums + own_ref[start : start + rows]) * scale
+    out_ref[...] = sums + own_ref[start : start + rows]
 
 
 def write_rows_kernel(half_rows, places, *refs):
@@ -306,9 +306,9 @@
         name="own_back",
     )(matrix, oblique, ratio)
 
-    def edge_rows(start, count, scale, name):
+    def edge_rows(start, count, name):
         return pl.pallas_call(
-            functools.partial(edge_back_kernel, slabs, own, start, scale),
+            functools.partial(edge_back_kernel, slabs, own, start),
             out_shape=array(jnp.float32, count, frames),
             in_specs=[VMEM] * 4,
             out_specs=VMEM,
@@ -337,11 +337,13 @@
     pairs = [(a, a ^ 1) for a in range(angles)]
     cuts = [0, FIRST_PART * half_rows // 16, half_rows]
     spans = [slice(at, end) for at, end in zip(cuts[:-1], cuts[1:])]
-    got = []
-    for n, span in enumerate(spans):
-        away = edge_rows(span.start, span.stop - span.start, PART_SCALE, f"edge_back_sent_{n}")
-        got.append(lax.ppermute(away.astype(jnp.float16), "angle", pairs))
-    home = edge_rows(half_rows, half_rows, 1.0, "edge_back_kept")
+    first, later = spans
+    away = edge_rows(0, first.stop, "edge_back_first")
+    got = [lax.ppermute((away * PART_SCALE).astype(jnp.float16), "angle", pairs)]
+    rest = edge_rows(first.stop, 2 * half_rows - first.stop, "edge_back_rest")
+    away = rest[: later.stop - later.start] * PART_SCALE
+    got.append(lax.ppermute(away.astype(jnp.float16), "angle", pairs))
+    home = rest[later.stop - later.start :]
     written = []
     for n, (at, end) in enumerate(zip(cuts[:-1], cuts[1:])):
         span = spans[n]

time: 23.6 us -> 23.6 us (level)
  starting transfers between devices: 9.29 us -> 9.53 us
    ppermute x0 -> x1, starting transfers between devices: none -> 0.75 us  [body(): lax.ppermute((away * PART_SCALE).astype(jnp.float16), 'angle', pairs)]
    ppermute x2 -> x1, starting transfers between devices: 0.83 us -> 0.1 us  [body(): got.append(lax.ppermute(away.astype(jnp.float16), 'angle', pairs))]
    ppermute x0 -> x1, waiting for transfers between devices: none -> 0.31 us  [body(): lax.ppermute((away * PART_SCALE).astype(jnp.float16), 'angle', pairs)]
    pallas_call x3 -> x2, Pallas kernels: 0.92 us -> 0.74 us  [edge_rows(): pl.pallas_call(functools.partial(edge_back_kernel, slabs, own, start), ou...]
  transfers between devices with their start and end apart: 10 -> 10, of which waited for: 6 -> 6; matrix products, arithmetic and copies ran while one was open for 1% -> 1% of each run, Pallas kernels for 18% -> 17%
where the time goes in v10:
time: 23.6 us; the launch traced here: 23.4 us
  starting transfers between devices  9.53 us (40%)
  Pallas kernels  7.24 us (31%)
  waiting for transfers between devices  6.27 us (27%)
    ppermute x2, waiting for transfers between devices, body(): across = lax.ppermute(chip, 'angle', [(a, a ^ 3) for a in range(angles)])  3.9 us
    ppermute x2, starting transfers between devices, body(): across = lax.ppermute(chip, 'angle', [(a, a ^ 3) for a in range(angles)])  2.72 us
    ppermute x1, starting transfers between devices, body(): got_back = lax.ppermute(edge_back, both, back)  2.6 us
    pallas_call x1, Pallas kernels, body(): pl.pallas_call(functools.partial(edge_kernel, blocks, own, lines), out_sh...  2.23 us
    pallas_call x1, Pallas kernels, body(): pl.pallas_call(functools.partial(own_kernel, blocks, own, lines), out_sha...  2.21 us
    ppermute x1, starting transfers between devices, body(): beside_back = lax.ppermute(oblique, both, back)  2.07 us
    ppermute x1, waiting for transfers between devices, body(): beside_forth = lax.ppermute(oblique, both, forth)  1.64 us
    pallas_call x2, Pallas kernels, write_rows(): pl.pallas_call(functools.partial(write_rows_kernel, half_rows, places), o...  1.38 us
  transfers between devices with their start and end apart: 10, of which 6 were waited for; matrix products, arithmetic and copies ran while one was open for 1% of the time, Pallas kernels for 17%

profile of v10, /device:TPU:0, one launch (start us, length us, event | category | flops | bytes accessed | tf_op | source)
XLA Modules:
  0.0 23.4 jit_solution(4006166093879756905)
XLA Ops:
  0.0 0.0 copy-start.6
  0.0 0.0 copy-start.3
  0.0 2.2 %edge_partials.1 = (bf16[2,128,128]{2,1,0:T(8,128)(2,1)S(1)}, bf16[2,128,128]{2,1,0:T(8,128)(2,1)S(1)}, bf16[128,1536]{1,0:T(8,128)(2,1)S(1)}, bf16[86,128,128]{2,1,0:T(8,128)(2,1)S(1)}) custom-call(s32[86]{0:T(128)} %bitcast.10, s32[86]{0:T(128)} %bitcast.12, bf16[1536,128]{1,0:T(8,128)(2,1)} %activity_ref.1, bf16[86,128,128]{2,1,0:T(8,128)(2,1)} %bitcast.15), custom_call_target="tpu_custom_call" | custom-call | tf_op jit(solution)/shard_map/edge_partials/pallas_call | solution.py:248
  2.3 0.5 %collective-permute-start = (bf16[2,128,128]{2,1,0:T(8,128)(2,1)S(1)}, bf16[2,128,128]{2,1,0:T(8,128)(2,1)S(1)}, u32[]{:S(2)}, u32[]{:S(2)}) collective-permute-start(bf16[2,128,128]{2,1,0:T(8,128)(2,1)S(1)} %get-tuple-element.20), channel_id=1, source_target_pairs={{0,1},{1,5},{2,3},{3,7},{4,0},{5,9},{6,2},{7,11},{8,4},{9,13},{10,... | collective-permute-start | bytes 196616 | tf_op jit(solution)/shard_map/ppermute | solution.py:269
  2.8 2.6 %collective-permute-start.1 = (bf16[2,128,128]{2,1,0:T(8,128)(2,1)S(1)}, bf16[2,128,128]{2,1,0:T(8,128)(2,1)S(1)}, u32[]{:S(2)}, u32[]{:S(2)}) collective-permute-start(bf16[2,128,128]{2,1,0:T(8,128)(2,1)S(1)} %get-tuple-element.21), channel_id=1, source_target_pairs={{1,0},{5,1},{3,2},{7,3},{0,4},{9,5},{2,6},{11,7},{4,8},{13,9},{6,1... | collective-permute-start | bytes 196616 | tf_op jit(solution)/shard_map/ppermute | solution.py:270
  5.4 2.2 %own_partials.1 = (f32[2,128,128]{2,1,0:T(8,128)S(1)}, f32[2,128,128]{2,1,0:T(8,128)S(1)}, bf16[2,128,128]{2,1,0:T(8,128)(2,1)S(1)}, bf16[1536,1024]{1,0:T(8,128)(2,1)S(1)}, f32[768,128]{1,0:T(8,128)S(1)}) custom-call(s32[86]{0:T(128)S(1)} %bitcast.11, s32[86]{0:T(128)S(1)} %bitcast.13, s32[2]{0:T(128)S(1)} %bitcast.14, ...), custom_call_target="tpu_custom_call" | custom-call | tf_op jit(solution)/shard_map/own_partials/pallas_call | solution.py:272
  7.6 0.1 collective-permute-done.forth_ref
  7.7 0.0 collective-permute-done.1.back_ref
  7.7 0.1 oblique_ratios.1.oblique_ref
  7.9 0.4 %collective-permute-start.3 = (bf16[2,128,128]{2,1,0:T(8,128)(2,1)S(1)}, bf16[2,128,128]{2,1,0:T(8,128)(2,1)S(1)}, u32[]{:S(2)}, u32[]{:S(2)}) collective-permute-start(bf16[2,128,128]{2,1,0:T(8,128)(2,1)S(1)} %oblique_ratios.1.oblique_ref), channel_id=1, source_target_pairs={{0,1},{1,5},{2,3},{3,7},{4,0},{5,9},{6,2},{7,11},{8,4},{9,13},{10,... | collective-permute-start | bytes 196616 | tf_op jit(solution)/shard_map/ppermute | solution.py:298
  8.2 2.1 %collective-permute-start.2 = (bf16[2,128,128]{2,1,0:T(8,128)(2,1)S(1)}, bf16[2,128,128]{2,1,0:T(8,128)(2,1)S(1)}, u32[]{:S(2)}, u32[]{:S(2)}) collective-permute-start(bf16[2,128,128]{2,1,0:T(8,128)(2,1)S(1)} %oblique_ratios.1.oblique_ref), channel_id=1, source_target_pairs={{1,0},{5,1},{3,2},{7,3},{0,4},{9,5},{2,6},{11,7},{4,8},{13,9},{6,1... | collective-permute-start | bytes 196616 | tf_op jit(solution)/shard_map/ppermute | solution.py:299
  10.3 0.6 %own_back.1.own_ref = f32[1536,128]{1,0:T(8,128)S(1)} custom-call(bf16[1536,1024]{1,0:T(8,128)(2,1)S(1)} %get-tuple-element.19.matrix_ref, bf16[2,128,128]{2,1,0:T(8,128)(2,1)S(1)} %oblique_ratios.1.oblique_ref, bf16[2,128,128]{2,1,0:T(8,128)(2,1)S(1)} %get-tuple-element.24.ratio_ref), custom_call_target="tpu_custom_call" | custom-call | tf_op jit(solution)/shard_map/own_back/pallas_call | solution.py:300
  10.9 1.6 %collective-permute-done.3.forth_ref = bf16[2,128,128]{2,1,0:T(8,128)(2,1)S(1)} collective-permute-done((bf16[2,128,128]{2,1,0:T(8,128)(2,1)S(1)}, bf16[2,128,128]{2,1,0:T(8,128)(2,1)S(1)}, u32[]{:S(2)}, u32[]{:S(2)}) %collective-permute-start.3) | collective-permute-done | bytes 65568 | tf_op jit(solution)/shard_map/ppermute | solution.py:298
  12.5 0.0 collective-permute-done.2.back_ref
  12.5 0.3 %edge_back_first.1 = f32[336,128]{1,0:T(8,128)S(1)} custom-call(bf16[1536,1024]{1,0:T(8,128)(2,1)S(1)} %get-tuple-element.19.matrix_ref, bf16[2,128,128]{2,1,0:T(8,128)(2,1)S(1)} %collective-permute-done.2.back_ref, bf16[2,128,128]{2,1,0:T(8,128)(2,1)S(1)} %collective-permute-done.3.forth_ref, f32[1536,128]{1,0:T(8,128)S(1)} %own_back.1.own_ref), custom_call_target="tpu_custom_call" | custom-call | tf_op jit(solution)/shard_map/edge_back_first/pallas_call | solution.py:310
  12.8 0.8 %collective-permute-start.6 = (f16[336,128]{1,0:T(8,128)(2,1)S(1)}, f16[336,128]{1,0:T(8,128)(2,1)S(1)}, u32[]{:S(2)}, u32[]{:S(2)}) collective-permute-start(f16[336,128]{1,0:T(8,128)(2,1)S(1)} %multiply_convert_fusion.2), channel_id=1, source_target_pairs={{0,1},{1,0},{2,3},{3,2},{4,5},{5,4},{6,7},{7,6},{8,9},{9,8},{10,11... | collective-permute-start | bytes 258056 | tf_op jit(solution)/shard_map/ppermute | solution.py:342
  13.6 0.5 %edge_back_rest.1 = f32[1200,128]{1,0:T(8,128)S(1)} custom-call(bf16[1536,1024]{1,0:T(8,128)(2,1)S(1)} %get-tuple-element.19.matrix_ref, bf16[2,128,128]{2,1,0:T(8,128)(2,1)S(1)} %collective-permute-done.2.back_ref, bf16[2,128,128]{2,1,0:T(8,128)(2,1)S(1)} %collective-permute-done.3.forth_ref, f32[1536,128]{1,0:T(8,128)S(1)} %own_back.1.own_ref), custom_call_target="tpu_custom_call" | custom-call | tf_op jit(solution)/shard_map/edge_back_rest/pallas_call | solution.py:310
  14.1 0.1 collective-permute-start.4
  14.2 0.3 %collective-permute-done.6 = f16[336,128]{1,0:T(8,128)(2,1)S(1)} collective-permute-done((f16[336,128]{1,0:T(8,128)(2,1)S(1)}, f16[336,128]{1,0:T(8,128)(2,1)S(1)}, u32[]{:S(2)}, u32[]{:S(2)}) %collective-permute-start.6) | collective-permute-done | bytes 86048 | tf_op jit(solution)/shard_map/ppermute | solution.py:342
  14.5 1.8 %collective-permute-start.7 = (f16[336,128]{1,0:T(8,128)(2,1)S(1)}, f16[336,128]{1,0:T(8,128)(2,1)S(1)}, u32[]{:S(2)}, u32[]{:S(2)}) collective-permute-start(f16[336,128]{1,0:T(8,128)(2,1)S(1)} %fusion.4), channel_id=1, source_target_pairs={{0,3},{1,2},{2,1},{3,0},{4,7},{5,6},{6,5},{7,4},{8,11},{9,10},{10,... | collective-permute-start | bytes 258056 | tf_op jit(solution)/shard_map/ppermute | solution.py:353
  16.3 0.0 collective-permute-done.4
  16.3 0.1 fusion.2
  16.4 0.9 %collective-permute-start.5 = (f16[432,128]{1,0:T(8,128)(2,1)S(1)}, f16[432,128]{1,0:T(8,128)(2,1)S(1)}, u32[]{:S(2)}, u32[]{:S(2)}) collective-permute-start(f16[432,128]{1,0:T(8,128)(2,1)S(1)} %fusion.2), channel_id=1, source_target_pairs={{0,3},{1,2},{2,1},{3,0},{4,7},{5,6},{6,5},{7,4},{8,11},{9,10},{10,... | collective-permute-start | bytes 331784 | tf_op jit(solution)/shard_map/ppermute | solution.py:353
  17.3 1.9 %collective-permute-done.7 = f16[336,128]{1,0:T(8,128)(2,1)S(1)} collective-permute-done((f16[336,128]{1,0:T(8,128)(2,1)S(1)}, f16[336,128]{1,0:T(8,128)(2,1)S(1)}, u32[]{:S(2)}, u32[]{:S(2)}) %collective-permute-start.7) | collective-permute-done | bytes 86048 | tf_op jit(solution)/shard_map/ppermute | solution.py:353
  19.3 0.1 collective-permute-start.8
  19.4 2.0 %collective-permute-done.5 = f16[432,128]{1,0:T(8,128)(2,1)S(1)} collective-permute-done((f16[432,128]{1,0:T(8,128)(2,1)S(1)}, f16[432,128]{1,0:T(8,128)(2,1)S(1)}, u32[]{:S(2)}, u32[]{:S(2)}) %collective-permute-start.5) | collective-permute-done | bytes 110624 | tf_op jit(solution)/shard_map/ppermute | solution.py:353
  21.3 0.0 collective-permute-done.8.refs_1_
  21.4 0.1 multiply_convert_fusion.refs_2_
  21.4 0.4 %collective-permute-start.9 = (bf16[432,128]{1,0:T(8,128)(2,1)S(1)}, bf16[432,128]{1,0:T(8,128)(2,1)S(1)}, u32[]{:S(2)}, u32[]{:S(2)}) collective-permute-start(bf16[432,128]{1,0:T(8,128)(2,1)S(1)} %multiply_convert_fusion.refs_2_), channel_id=1, source_target_pairs={{0,1},{1,0},{2,3},{3,2},{4,5},{5,4},{6,7},{7,6},{8,9},{9,8},{10,11... | collective-permute-start | bytes 331784 | tf_op jit(solution)/shard_map/ppermute | solution.py:363
  21.8 0.7 %write_first.1.refs_1_ = bf16[1536,128]{1,0:T(8,128)(2,1)} custom-call(bf16[336,128]{1,0:T(8,128)(2,1)S(1)} %multiply_convert_fusion.1.refs_0_, bf16[336,128]{1,0:T(8,128)(2,1)S(1)} %collective-permute-done.8.refs_1_, bf16[432,128]{1,0:T(8,128)(2,1)S(1)} %multiply_convert_fusion.refs_2_), custom_call_target="tpu_custom_call" | custom-call | tf_op jit(solution)/shard_map/write_first/pallas_call | solution.py:326
  22.5 0.3 %collective-permute-done.9.refs_0_ = bf16[432,128]{1,0:T(8,128)(2,1)S(1)} collective-permute-done((bf16[432,128]{1,0:T(8,128)(2,1)S(1)}, bf16[432,128]{1,0:T(8,128)(2,1)S(1)}, u32[]{:S(2)}, u32[]{:S(2)}) %collective-permute-start.9) | collective-permute-done | bytes 110624 | tf_op jit(solution)/shard_map/ppermute | solution.py:363
  22.8 0.7 %write_last.1 = bf16[1536,128]{1,0:T(8,128)(2,1)} custom-call(bf16[432,128]{1,0:T(8,128)(2,1)S(1)} %collective-permute-done.9.refs_0_, bf16[1536,128]{1,0:T(8,128)(2,1)} %write_first.1.refs_1_), custom_call_target="tpu_custom_call", output_to_operand_aliasing={{}: (1, {})} | custom-call | tf_op jit(solution)/shard_map/write_last/pallas_call | solution.py:326
  (16 shorter events, 0.2 us)
Async XLA Ops:
  0.0 5.4 %copy-start = (bf16[1536,128]{1,0:T(8,128)(2,1)S(1)}, bf16[1536,128]{1,0:T(8,128)(2,1)}, u32[]{:S(2)}) copy-start(bf16[1536,128]{1,0:T(8,128)(2,1)} %activity_ref.1) | copy-start | bytes 1179652
  0.0 5.4 %copy-start.5 = (s32[1,1,86]{2,1,0:T(1,128)S(1)}, s32[1,1,86]{2,1,0:T(1,128)}, u32[]{:S(2)}) copy-start(s32[1,1,86]{2,1,0:T(1,128)} %param.12) | copy-start | bytes 1036
  0.0 5.4 %copy-start.4 = (s32[1,1,86]{2,1,0:T(1,128)S(1)}, s32[1,1,86]{2,1,0:T(1,128)}, u32[]{:S(2)}) copy-start(s32[1,1,86]{2,1,0:T(1,128)} %param.11) | copy-start | bytes 1036
  0.0 5.4 %copy-start.2 = (bf16[1,1,512,128]{3,2,1,0:T(8,128)(2,1)S(1)}, bf16[1,1,512,128]{3,2,1,0:T(8,128)(2,1)}, u32[]{:S(2)}) copy-start(bf16[1,1,512,128]{3,2,1,0:T(8,128)(2,1)} %param.15) | copy-start | bytes 393220
  0.0 5.4 %copy-start.1 = (s32[1,1,512,128]{3,2,1,0:T(8,128)S(1)}, s32[1,1,512,128]{3,2,1,0:T(8,128)}, u32[]{:S(2)}) copy-start(s32[1,1,512,128]{3,2,1,0:T(8,128)} %param.14) | copy-start | bytes 786436
  0.0 5.4 %copy-start.6 = (s32[1,1,2]{2,1,0:T(1,128)S(1)}, s32[1,1,2]{2,1,0:T(1,128)}, u32[]{:S(2)}) copy-start(s32[1,1,2]{2,1,0:T(1,128)} %param.13) | copy-start | bytes 28
  0.0 5.4 %copy-start.3 = (f32[1536]{0:T(1024)S(1)}, f32[1536]{0:T(1024)}, u32[]{:S(2)}) copy-start(f32[1536]{0:T(1024)} %param.9) | copy-start | bytes 18436
  2.3 5.4 %collective-permute-start = (bf16[2,128,128]{2,1,0:T(8,128)(2,1)S(1)}, bf16[2,128,128]{2,1,0:T(8,128)(2,1)S(1)}, u32[]{:S(2)}, u32[]{:S(2)}) collective-permute-start(bf16[2,128,128]{2,1,0:T(8,128)(2,1)S(1)} %get-tuple-element.20), channel_id=1, source_target_pairs={{0,1},{1,5},{2,3},{3,7},{4,0},{5,9},{6,2},{7,11},{8,4},{9,13},{10,... | collective-permute-start | bytes 196616 | tf_op jit(solution)/shard_map/ppermute | solution.py:269
  2.8 5.0 %collective-permute-start.1 = (bf16[2,128,128]{2,1,0:T(8,128)(2,1)S(1)}, bf16[2,128,128]{2,1,0:T(8,128)(2,1)S(1)}, u32[]{:S(2)}, u32[]{:S(2)}) collective-permute-start(bf16[2,128,128]{2,1,0:T(8,128)(2,1)S(1)} %get-tuple-element.21), channel_id=1, source_target_pairs={{1,0},{5,1},{3,2},{7,3},{0,4},{9,5},{2,6},{11,7},{4,8},{13,9},{6,1... | collective-permute-start | bytes 196616 | tf_op jit(solution)/shard_map/ppermute | solution.py:270
  7.9 4.7 %collective-permute-start.3 = (bf16[2,128,128]{2,1,0:T(8,128)(2,1)S(1)}, bf16[2,128,128]{2,1,0:T(8,128)(2,1)S(1)}, u32[]{:S(2)}, u32[]{:S(2)}) collective-permute-start(bf16[2,128,128]{2,1,0:T(8,128)(2,1)S(1)} %oblique_ratios.1.oblique_ref), channel_id=1, source_target_pairs={{0,1},{1,5},{2,3},{3,7},{4,0},{5,9},{6,2},{7,11},{8,4},{9,13},{10,... | collective-permute-start | bytes 196616 | tf_op jit(solution)/shard_map/ppermute | solution.py:298
  8.2 4.3 %collective-permute-start.2 = (bf16[2,128,128]{2,1,0:T(8,128)(2,1)S(1)}, bf16[2,128,128]{2,1,0:T(8,128)(2,1)S(1)}, u32[]{:S(2)}, u32[]{:S(2)}) collective-permute-start(bf16[2,128,128]{2,1,0:T(8,128)(2,1)S(1)} %oblique_ratios.1.oblique_ref), channel_id=1, source_target_pairs={{1,0},{5,1},{3,2},{7,3},{0,4},{9,5},{2,6},{11,7},{4,8},{13,9},{6,1... | collective-permute-start | bytes 196616 | tf_op jit(solution)/shard_map/ppermute | solution.py:299
  12.8 1.7 %collective-permute-start.6 = (f16[336,128]{1,0:T(8,128)(2,1)S(1)}, f16[336,128]{1,0:T(8,128)(2,1)S(1)}, u32[]{:S(2)}, u32[]{:S(2)}) collective-permute-start(f16[336,128]{1,0:T(8,128)(2,1)S(1)} %multiply_convert_fusion.2), channel_id=1, source_target_pairs={{0,1},{1,0},{2,3},{3,2},{4,5},{5,4},{6,7},{7,6},{8,9},{9,8},{10,11... | collective-permute-start | bytes 258056 | tf_op jit(solution)/shard_map/ppermute | solution.py:342
  14.1 2.2 %collective-permute-start.4 = (f16[432,128]{1,0:T(8,128)(2,1)S(1)}, f16[432,128]{1,0:T(8,128)(2,1)S(1)}, u32[]{:S(2)}, u32[]{:S(2)}) collective-permute-start(f16[432,128]{1,0:T(8,128)(2,1)S(1)} %fusion), channel_id=1, source_target_pairs={{0,1},{1,0},{2,3},{3,2},{4,5},{5,4},{6,7},{7,6},{8,9},{9,8},{10,11... | collective-permute-start | bytes 331784 | tf_op jit(solution)/shard_map/ppermute | solution.py:345
  14.5 4.7 %collective-permute-start.7 = (f16[336,128]{1,0:T(8,128)(2,1)S(1)}, f16[336,128]{1,0:T(8,128)(2,1)S(1)}, u32[]{:S(2)}, u32[]{:S(2)}) collective-permute-start(f16[336,128]{1,0:T(8,128)(2,1)S(1)} %fusion.4), channel_id=1, source_target_pairs={{0,3},{1,2},{2,1},{3,0},{4,7},{5,6},{6,5},{7,4},{8,11},{9,10},{10,... | collective-permute-start | bytes 258056 | tf_op jit(solution)/shard_map/ppermute | solution.py:353
  16.4 5.0 %collective-permute-start.5 = (f16[432,128]{1,0:T(8,128)(2,1)S(1)}, f16[432,128]{1,0:T(8,128)(2,1)S(1)}, u32[]{:S(2)}, u32[]{:S(2)}) collective-permute-start(f16[432,128]{1,0:T(8,128)(2,1)S(1)} %fusion.2), channel_id=1, source_target_pairs={{0,3},{1,2},{2,1},{3,0},{4,7},{5,6},{6,5},{7,4},{8,11},{9,10},{10,... | collective-permute-start | bytes 331784 | tf_op jit(solution)/shard_map/ppermute | solution.py:353
  19.3 2.1 %collective-permute-start.8 = (bf16[336,128]{1,0:T(8,128)(2,1)S(1)}, bf16[336,128]{1,0:T(8,128)(2,1)S(1)}, u32[]{:S(2)}, u32[]{:S(2)}) collective-permute-start(bf16[336,128]{1,0:T(8,128)(2,1)S(1)} %multiply_convert_fusion.1.refs_0_), channel_id=1, source_target_pairs={{0,1},{1,0},{2,3},{3,2},{4,5},{5,4},{6,7},{7,6},{8,9},{9,8},{10,11... | collective-permute-start | bytes 258056 | tf_op jit(solution)/shard_map/ppermute | solution.py:363
  21.4 1.4 %collective-permute-start.9 = (bf16[432,128]{1,0:T(8,128)(2,1)S(1)}, bf16[432,128]{1,0:T(8,128)(2,1)S(1)}, u32[]{:S(2)}, u32[]{:S(2)}) collective-permute-start(bf16[432,128]{1,0:T(8,128)(2,1)S(1)} %multiply_convert_fusion.refs_2_), channel_id=1, source_target_pairs={{0,1},{1,0},{2,3},{3,2},{4,5},{5,4},{6,7},{7,6},{8,9},{9,8},{10,11... | collective-permute-start | bytes 331784 | tf_op jit(solution)/shard_map/ppermute | solution.py:363

commit v11 on v10

--- a/solution.py
+++ b/solution.py
@@ -12,8 +12,8 @@
 HBM = pl.BlockSpec(memory_space=pltpu.HBM)
 PART_SCALE = 256.0
 CHIP_SCALE = 128.0
-GROUP = 2
-PIECE = 16
+GROUP = 3
+PIECE = 24
 FIRST_PART = 7
 
 

time: 23.6 us -> 23.6 us (level)
  no operation moved by 1% of the time
where the time goes in v11:
time: 23.6 us; the launch traced here: 23.4 us
  starting transfers between devices  9.54 us (40%)
  Pallas kernels  7.24 us (31%)
  waiting for transfers between devices  6.26 us (27%)
    ppermute x2, waiting for transfers between devices, body(): across = lax.ppermute(chip, 'angle', [(a, a ^ 3) for a in range(angles)])  3.9 us
    ppermute x2, starting transfers between devices, body(): across = lax.ppermute(chip, 'angle', [(a, a ^ 3) for a in range(angles)])  2.72 us
    ppermute x1, starting transfers between devices, body(): got_back = lax.ppermute(edge_back, both, back)  2.6 us
    pallas_call x1, Pallas kernels, body(): pl.pallas_call(functools.partial(edge_kernel, blocks, own, lines), out_sh...  2.23 us
    pallas_call x1, Pallas kernels, body(): pl.pallas_call(functools.partial(own_kernel, blocks, own, lines), out_sha...  2.21 us
    ppermute x1, starting transfers between devices, body(): beside_back = lax.ppermute(oblique, both, back)  2.07 us
    ppermute x1, waiting for transfers between devices, body(): beside_forth = lax.ppermute(oblique, both, forth)  1.64 us
    pallas_call x2, Pallas kernels, write_rows(): pl.pallas_call(functools.partial(write_rows_kernel, half_rows, places), o...  1.38 us
  transfers between devices with their start and end apart: 10, of which 6 were waited for; matrix products, arithmetic and copies ran while one was open for 1% of the time, Pallas kernels for 17%

profile of v11, /device:TPU:0, one launch (start us, length us, event | category | flops | bytes accessed | tf_op | source)
XLA Modules:
  0.0 23.4 jit_solution(15667764578169374818)
XLA Ops:
  0.0 0.0 copy-start.6
  0.0 0.0 copy-start.3
  0.0 2.2 %edge_partials.1 = (bf16[2,128,128]{2,1,0:T(8,128)(2,1)S(1)}, bf16[2,128,128]{2,1,0:T(8,128)(2,1)S(1)}, bf16[128,1536]{1,0:T(8,128)(2,1)S(1)}, bf16[86,128,128]{2,1,0:T(8,128)(2,1)S(1)}) custom-call(s32[86]{0:T(128)} %bitcast.10, s32[86]{0:T(128)} %bitcast.12, bf16[1536,128]{1,0:T(8,128)(2,1)} %activity_ref.1, bf16[86,128,128]{2,1,0:T(8,128)(2,1)} %bitcast.15), custom_call_target="tpu_custom_call" | custom-call | tf_op jit(solution)/shard_map/edge_partials/pallas_call | solution.py:248
  2.3 0.5 %collective-permute-start = (bf16[2,128,128]{2,1,0:T(8,128)(2,1)S(1)}, bf16[2,128,128]{2,1,0:T(8,128)(2,1)S(1)}, u32[]{:S(2)}, u32[]{:S(2)}) collective-permute-start(bf16[2,128,128]{2,1,0:T(8,128)(2,1)S(1)} %get-tuple-element.20), channel_id=1, source_target_pairs={{0,1},{1,5},{2,3},{3,7},{4,0},{5,9},{6,2},{7,11},{8,4},{9,13},{10,... | collective-permute-start | bytes 196616 | tf_op jit(solution)/shard_map/ppermute | solution.py:269
  2.8 2.6 %collective-permute-start.1 = (bf16[2,128,128]{2,1,0:T(8,128)(2,1)S(1)}, bf16[2,128,128]{2,1,0:T(8,128)(2,1)S(1)}, u32[]{:S(2)}, u32[]{:S(2)}) collective-permute-start(bf16[2,128,128]{2,1,0:T(8,128)(2,1)S(1)} %get-tuple-element.21), channel_id=1, source_target_pairs={{1,0},{5,1},{3,2},{7,3},{0,4},{9,5},{2,6},{11,7},{4,8},{13,9},{6,1... | collective-permute-start | bytes 196616 | tf_op jit(solution)/shard_map/ppermute | solution.py:270
  5.4 2.2 %own_partials.1 = (f32[2,128,128]{2,1,0:T(8,128)S(1)}, f32[2,128,128]{2,1,0:T(8,128)S(1)}, bf16[2,128,128]{2,1,0:T(8,128)(2,1)S(1)}, bf16[1536,1024]{1,0:T(8,128)(2,1)S(1)}, f32[768,128]{1,0:T(8,128)S(1)}) custom-call(s32[86]{0:T(128)S(1)} %bitcast.11, s32[86]{0:T(128)S(1)} %bitcast.13, s32[2]{0:T(128)S(1)} %bitcast.14, ...), custom_call_target="tpu_custom_call" | custom-call | tf_op jit(solution)/shard_map/own_partials/pallas_call | solution.py:272
  7.6 0.1 collective-permute-done.forth_ref
  7.7 0.0 collective-permute-done.1.back_ref
  7.7 0.1 oblique_ratios.1.oblique_ref
  7.9 0.4 %collective-permute-start.3 = (bf16[2,128,128]{2,1,0:T(8,128)(2,1)S(1)}, bf16[2,128,128]{2,1,0:T(8,128)(2,1)S(1)}, u32[]{:S(2)}, u32[]{:S(2)}) collective-permute-start(bf16[2,128,128]{2,1,0:T(8,128)(2,1)S(1)} %oblique_ratios.1.oblique_ref), channel_id=1, source_target_pairs={{0,1},{1,5},{2,3},{3,7},{4,0},{5,9},{6,2},{7,11},{8,4},{9,13},{10,... | collective-permute-start | bytes 196616 | tf_op jit(solution)/shard_map/ppermute | solution.py:298
  8.2 2.1 %collective-permute-start.2 = (bf16[2,128,128]{2,1,0:T(8,128)(2,1)S(1)}, bf16[2,128,128]{2,1,0:T(8,128)(2,1)S(1)}, u32[]{:S(2)}, u32[]{:S(2)}) collective-permute-start(bf16[2,128,128]{2,1,0:T(8,128)(2,1)S(1)} %oblique_ratios.1.oblique_ref), channel_id=1, source_target_pairs={{1,0},{5,1},{3,2},{7,3},{0,4},{9,5},{2,6},{11,7},{4,8},{13,9},{6,1... | collective-permute-start | bytes 196616 | tf_op jit(solution)/shard_map/ppermute | solution.py:299
  10.3 0.6 %own_back.1.own_ref = f32[1536,128]{1,0:T(8,128)S(1)} custom-call(bf16[1536,1024]{1,0:T(8,128)(2,1)S(1)} %get-tuple-element.19.matrix_ref, bf16[2,128,128]{2,1,0:T(8,128)(2,1)S(1)} %oblique_ratios.1.oblique_ref, bf16[2,128,128]{2,1,0:T(8,128)(2,1)S(1)} %get-tuple-element.24.ratio_ref), custom_call_target="tpu_custom_call" | custom-call | tf_op jit(solution)/shard_map/own_back/pallas_call | solution.py:300
  10.9 1.6 %collective-permute-done.3.forth_ref = bf16[2,128,128]{2,1,0:T(8,128)(2,1)S(1)} collective-permute-done((bf16[2,128,128]{2,1,0:T(8,128)(2,1)S(1)}, bf16[2,128,128]{2,1,0:T(8,128)(2,1)S(1)}, u32[]{:S(2)}, u32[]{:S(2)}) %collective-permute-start.3) | collective-permute-done | bytes 65568 | tf_op jit(solution)/shard_map/ppermute | solution.py:298
  12.5 0.0 collective-permute-done.2.back_ref
  12.5 0.3 %edge_back_first.1 = f32[336,128]{1,0:T(8,128)S(1)} custom-call(bf16[1536,1024]{1,0:T(8,128)(2,1)S(1)} %get-tuple-element.19.matrix_ref, bf16[2,128,128]{2,1,0:T(8,128)(2,1)S(1)} %collective-permute-done.2.back_ref, bf16[2,128,128]{2,1,0:T(8,128)(2,1)S(1)} %collective-permute-done.3.forth_ref, f32[1536,128]{1,0:T(8,128)S(1)} %own_back.1.own_ref), custom_call_target="tpu_custom_call" | custom-call | tf_op jit(solution)/shard_map/edge_back_first/pallas_call | solution.py:310
  12.8 0.8 %collective-permute-start.6 = (f16[336,128]{1,0:T(8,128)(2,1)S(1)}, f16[336,128]{1,0:T(8,128)(2,1)S(1)}, u32[]{:S(2)}, u32[]{:S(2)}) collective-permute-start(f16[336,128]{1,0:T(8,128)(2,1)S(1)} %multiply_convert_fusion.2), channel_id=1, source_target_pairs={{0,1},{1,0},{2,3},{3,2},{4,5},{5,4},{6,7},{7,6},{8,9},{9,8},{10,11... | collective-permute-start | bytes 258056 | tf_op jit(solution)/shard_map/ppermute | solution.py:342
  13.6 0.5 %edge_back_rest.1 = f32[1200,128]{1,0:T(8,128)S(1)} custom-call(bf16[1536,1024]{1,0:T(8,128)(2,1)S(1)} %get-tuple-element.19.matrix_ref, bf16[2,128,128]{2,1,0:T(8,128)(2,1)S(1)} %collective-permute-done.2.back_ref, bf16[2,128,128]{2,1,0:T(8,128)(2,1)S(1)} %collective-permute-done.3.forth_ref, f32[1536,128]{1,0:T(8,128)S(1)} %own_back.1.own_ref), custom_call_target="tpu_custom_call" | custom-call | tf_op jit(solution)/shard_map/edge_back_rest/pallas_call | solution.py:310
  14.1 0.1 collective-permute-start.4
  14.2 0.3 %collective-permute-done.6 = f16[336,128]{1,0:T(8,128)(2,1)S(1)} collective-permute-done((f16[336,128]{1,0:T(8,128)(2,1)S(1)}, f16[336,128]{1,0:T(8,128)(2,1)S(1)}, u32[]{:S(2)}, u32[]{:S(2)}) %collective-permute-start.6) | collective-permute-done | bytes 86048 | tf_op jit(solution)/shard_map/ppermute | solution.py:342
  14.5 1.8 %collective-permute-start.7 = (f16[336,128]{1,0:T(8,128)(2,1)S(1)}, f16[336,128]{1,0:T(8,128)(2,1)S(1)}, u32[]{:S(2)}, u32[]{:S(2)}) collective-permute-start(f16[336,128]{1,0:T(8,128)(2,1)S(1)} %fusion.4), channel_id=1, source_target_pairs={{0,3},{1,2},{2,1},{3,0},{4,7},{5,6},{6,5},{7,4},{8,11},{9,10},{10,... | collective-permute-start | bytes 258056 | tf_op jit(solution)/shard_map/ppermute | solution.py:353
  16.3 0.0 collective-permute-done.4
  16.3 0.1 fusion.2
  16.4 0.9 %collective-permute-start.5 = (f16[432,128]{1,0:T(8,128)(2,1)S(1)}, f16[432,128]{1,0:T(8,128)(2,1)S(1)}, u32[]{:S(2)}, u32[]{:S(2)}) collective-permute-start(f16[432,128]{1,0:T(8,128)(2,1)S(1)} %fusion.2), channel_id=1, source_target_pairs={{0,3},{1,2},{2,1},{3,0},{4,7},{5,6},{6,5},{7,4},{8,11},{9,10},{10,... | collective-permute-start | bytes 331784 | tf_op jit(solution)/shard_map/ppermute | solution.py:353
  17.3 1.9 %collective-permute-done.7 = f16[336,128]{1,0:T(8,128)(2,1)S(1)} collective-permute-done((f16[336,128]{1,0:T(8,128)(2,1)S(1)}, f16[336,128]{1,0:T(8,128)(2,1)S(1)}, u32[]{:S(2)}, u32[]{:S(2)}) %collective-permute-start.7) | collective-permute-done | bytes 86048 | tf_op jit(solution)/shard_map/ppermute | solution.py:353
  19.3 0.1 collective-permute-start.8
  19.4 2.0 %collective-permute-done.5 = f16[432,128]{1,0:T(8,128)(2,1)S(1)} collective-permute-done((f16[432,128]{1,0:T(8,128)(2,1)S(1)}, f16[432,128]{1,0:T(8,128)(2,1)S(1)}, u32[]{:S(2)}, u32[]{:S(2)}) %collective-permute-start.5) | collective-permute-done | bytes 110624 | tf_op jit(solution)/shard_map/ppermute | solution.py:353
  21.3 0.0 collective-permute-done.8.refs_1_
  21.3 0.1 multiply_convert_fusion.refs_2_
  21.4 0.4 %collective-permute-start.9 = (bf16[432,128]{1,0:T(8,128)(2,1)S(1)}, bf16[432,128]{1,0:T(8,128)(2,1)S(1)}, u32[]{:S(2)}, u32[]{:S(2)}) collective-permute-start(bf16[432,128]{1,0:T(8,128)(2,1)S(1)} %multiply_convert_fusion.refs_2_), channel_id=1, source_target_pairs={{0,1},{1,0},{2,3},{3,2},{4,5},{5,4},{6,7},{7,6},{8,9},{9,8},{10,11... | collective-permute-start | bytes 331784 | tf_op jit(solution)/shard_map/ppermute | solution.py:363
  21.8 0.7 %write_first.1.refs_1_ = bf16[1536,128]{1,0:T(8,128)(2,1)} custom-call(bf16[336,128]{1,0:T(8,128)(2,1)S(1)} %multiply_convert_fusion.1.refs_0_, bf16[336,128]{1,0:T(8,128)(2,1)S(1)} %collective-permute-done.8.refs_1_, bf16[432,128]{1,0:T(8,128)(2,1)S(1)} %multiply_convert_fusion.refs_2_), custom_call_target="tpu_custom_call" | custom-call | tf_op jit(solution)/shard_map/write_first/pallas_call | solution.py:326
  22.5 0.3 %collective-permute-done.9.refs_0_ = bf16[432,128]{1,0:T(8,128)(2,1)S(1)} collective-permute-done((bf16[432,128]{1,0:T(8,128)(2,1)S(1)}, bf16[432,128]{1,0:T(8,128)(2,1)S(1)}, u32[]{:S(2)}, u32[]{:S(2)}) %collective-permute-start.9) | collective-permute-done | bytes 110624 | tf_op jit(solution)/shard_map/ppermute | solution.py:363
  22.8 0.7 %write_last.1 = bf16[1536,128]{1,0:T(8,128)(2,1)} custom-call(bf16[432,128]{1,0:T(8,128)(2,1)S(1)} %collective-permute-done.9.refs_0_, bf16[1536,128]{1,0:T(8,128)(2,1)} %write_first.1.refs_1_), custom_call_target="tpu_custom_call", output_to_operand_aliasing={{}: (1, {})} | custom-call | tf_op jit(solution)/shard_map/write_last/pallas_call | solution.py:326
  (16 shorter events, 0.2 us)
Async XLA Ops:
  0.0 5.4 %copy-start = (bf16[1536,128]{1,0:T(8,128)(2,1)S(1)}, bf16[1536,128]{1,0:T(8,128)(2,1)}, u32[]{:S(2)}) copy-start(bf16[1536,128]{1,0:T(8,128)(2,1)} %activity_ref.1) | copy-start | bytes 1179652
  0.0 5.4 %copy-start.5 = (s32[1,1,86]{2,1,0:T(1,128)S(1)}, s32[1,1,86]{2,1,0:T(1,128)}, u32[]{:S(2)}) copy-start(s32[1,1,86]{2,1,0:T(1,128)} %param.12) | copy-start | bytes 1036
  0.0 5.4 %copy-start.4 = (s32[1,1,86]{2,1,0:T(1,128)S(1)}, s32[1,1,86]{2,1,0:T(1,128)}, u32[]{:S(2)}) copy-start(s32[1,1,86]{2,1,0:T(1,128)} %param.11) | copy-start | bytes 1036
  0.0 5.4 %copy-start.2 = (bf16[1,1,512,128]{3,2,1,0:T(8,128)(2,1)S(1)}, bf16[1,1,512,128]{3,2,1,0:T(8,128)(2,1)}, u32[]{:S(2)}) copy-start(bf16[1,1,512,128]{3,2,1,0:T(8,128)(2,1)} %param.15) | copy-start | bytes 393220
  0.0 5.4 %copy-start.1 = (s32[1,1,512,128]{3,2,1,0:T(8,128)S(1)}, s32[1,1,512,128]{3,2,1,0:T(8,128)}, u32[]{:S(2)}) copy-start(s32[1,1,512,128]{3,2,1,0:T(8,128)} %param.14) | copy-start | bytes 786436
  0.0 5.4 %copy-start.6 = (s32[1,1,2]{2,1,0:T(1,128)S(1)}, s32[1,1,2]{2,1,0:T(1,128)}, u32[]{:S(2)}) copy-start(s32[1,1,2]{2,1,0:T(1,128)} %param.13) | copy-start | bytes 28
  0.0 5.4 %copy-start.3 = (f32[1536]{0:T(1024)S(1)}, f32[1536]{0:T(1024)}, u32[]{:S(2)}) copy-start(f32[1536]{0:T(1024)} %param.9) | copy-start | bytes 18436
  2.3 5.5 %collective-permute-start = (bf16[2,128,128]{2,1,0:T(8,128)(2,1)S(1)}, bf16[2,128,128]{2,1,0:T(8,128)(2,1)S(1)}, u32[]{:S(2)}, u32[]{:S(2)}) collective-permute-start(bf16[2,128,128]{2,1,0:T(8,128)(2,1)S(1)} %get-tuple-element.20), channel_id=1, source_target_pairs={{0,1},{1,5},{2,3},{3,7},{4,0},{5,9},{6,2},{7,11},{8,4},{9,13},{10,... | collective-permute-start | bytes 196616 | tf_op jit(solution)/shard_map/ppermute | solution.py:269
  2.8 5.0 %collective-permute-start.1 = (bf16[2,128,128]{2,1,0:T(8,128)(2,1)S(1)}, bf16[2,128,128]{2,1,0:T(8,128)(2,1)S(1)}, u32[]{:S(2)}, u32[]{:S(2)}) collective-permute-start(bf16[2,128,128]{2,1,0:T(8,128)(2,1)S(1)} %get-tuple-element.21), channel_id=1, source_target_pairs={{1,0},{5,1},{3,2},{7,3},{0,4},{9,5},{2,6},{11,7},{4,8},{13,9},{6,1... | collective-permute-start | bytes 196616 | tf_op jit(solution)/shard_map/ppermute | solution.py:270
  7.9 4.7 %collective-permute-start.3 = (bf16[2,128,128]{2,1,0:T(8,128)(2,1)S(1)}, bf16[2,128,128]{2,1,0:T(8,128)(2,1)S(1)}, u32[]{:S(2)}, u32[]{:S(2)}) collective-permute-start(bf16[2,128,128]{2,1,0:T(8,128)(2,1)S(1)} %oblique_ratios.1.oblique_ref), channel_id=1, source_target_pairs={{0,1},{1,5},{2,3},{3,7},{4,0},{5,9},{6,2},{7,11},{8,4},{9,13},{10,... | collective-permute-start | bytes 196616 | tf_op jit(solution)/shard_map/ppermute | solution.py:298
  8.2 4.3 %collective-permute-start.2 = (bf16[2,128,128]{2,1,0:T(8,128)(2,1)S(1)}, bf16[2,128,128]{2,1,0:T(8,128)(2,1)S(1)}, u32[]{:S(2)}, u32[]{:S(2)}) collective-permute-start(bf16[2,128,128]{2,1,0:T(8,128)(2,1)S(1)} %oblique_ratios.1.oblique_ref), channel_id=1, source_target_pairs={{1,0},{5,1},{3,2},{7,3},{0,4},{9,5},{2,6},{11,7},{4,8},{13,9},{6,1... | collective-permute-start | bytes 196616 | tf_op jit(solution)/shard_map/ppermute | solution.py:299
  12.8 1.7 %collective-permute-start.6 = (f16[336,128]{1,0:T(8,128)(2,1)S(1)}, f16[336,128]{1,0:T(8,128)(2,1)S(1)}, u32[]{:S(2)}, u32[]{:S(2)}) collective-permute-start(f16[336,128]{1,0:T(8,128)(2,1)S(1)} %multiply_convert_fusion.2), channel_id=1, source_target_pairs={{0,1},{1,0},{2,3},{3,2},{4,5},{5,4},{6,7},{7,6},{8,9},{9,8},{10,11... | collective-permute-start | bytes 258056 | tf_op jit(solution)/shard_map/ppermute | solution.py:342
  14.1 2.2 %collective-permute-start.4 = (f16[432,128]{1,0:T(8,128)(2,1)S(1)}, f16[432,128]{1,0:T(8,128)(2,1)S(1)}, u32[]{:S(2)}, u32[]{:S(2)}) collective-permute-start(f16[432,128]{1,0:T(8,128)(2,1)S(1)} %fusion), channel_id=1, source_target_pairs={{0,1},{1,0},{2,3},{3,2},{4,5},{5,4},{6,7},{7,6},{8,9},{9,8},{10,11... | collective-permute-start | bytes 331784 | tf_op jit(solution)/shard_map/ppermute | solution.py:345
  14.5 4.7 %collective-permute-start.7 = (f16[336,128]{1,0:T(8,128)(2,1)S(1)}, f16[336,128]{1,0:T(8,128)(2,1)S(1)}, u32[]{:S(2)}, u32[]{:S(2)}) collective-permute-start(f16[336,128]{1,0:T(8,128)(2,1)S(1)} %fusion.4), channel_id=1, source_target_pairs={{0,3},{1,2},{2,1},{3,0},{4,7},{5,6},{6,5},{7,4},{8,11},{9,10},{10,... | collective-permute-start | bytes 258056 | tf_op jit(solution)/shard_map/ppermute | solution.py:353
  16.4 5.0 %collective-permute-start.5 = (f16[432,128]{1,0:T(8,128)(2,1)S(1)}, f16[432,128]{1,0:T(8,128)(2,1)S(1)}, u32[]{:S(2)}, u32[]{:S(2)}) collective-permute-start(f16[432,128]{1,0:T(8,128)(2,1)S(1)} %fusion.2), channel_id=1, source_target_pairs={{0,3},{1,2},{2,1},{3,0},{4,7},{5,6},{6,5},{7,4},{8,11},{9,10},{10,... | collective-permute-start | bytes 331784 | tf_op jit(solution)/shard_map/ppermute | solution.py:353
  19.3 2.0 %collective-permute-start.8 = (bf16[336,128]{1,0:T(8,128)(2,1)S(1)}, bf16[336,128]{1,0:T(8,128)(2,1)S(1)}, u32[]{:S(2)}, u32[]{:S(2)}) collective-permute-start(bf16[336,128]{1,0:T(8,128)(2,1)S(1)} %multiply_convert_fusion.1.refs_0_), channel_id=1, source_target_pairs={{0,1},{1,0},{2,3},{3,2},{4,5},{5,4},{6,7},{7,6},{8,9},{9,8},{10,11... | collective-permute-start | bytes 258056 | tf_op jit(solution)/shard_map/ppermute | solution.py:363
  21.4 1.4 %collective-permute-start.9 = (bf16[432,128]{1,0:T(8,128)(2,1)S(1)}, bf16[432,128]{1,0:T(8,128)(2,1)S(1)}, u32[]{:S(2)}, u32[]{:S(2)}) collective-permute-start(bf16[432,128]{1,0:T(8,128)(2,1)S(1)} %multiply_convert_fusion.refs_2_), channel_id=1, source_target_pairs={{0,1},{1,0},{2,3},{3,2},{4,5},{5,4},{6,7},{7,6},{8,9},{9,8},{10,11... | collective-permute-start | bytes 331784 | tf_op jit(solution)/shard_map/ppermute | solution.py:363

commit v12 on v11

--- a/solution.py
+++ b/solution.py
@@ -92,11 +92,9 @@
     for v in range(blocks):
         image_ref[:, v * size : (v + 1) * size] = activity_ref[v * size : (v + 1) * size, :].T
     odd = lax.axis_index("angle") % 2
-    outs = (
-        (forth_ref, own + width * odd),
-        (back_ref, own + width * (1 - odd)),
-    )
-    sums = [None, None]
+    which = [own + width * odd + c for c in range(width)]
+    which += [own + width * (1 - odd) + c for c in range(width)]
+    sums = None
     waited = 0
     for low in range(0, blocks, GROUP):
         high = min(low + GROUP, blocks)
@@ -105,13 +103,11 @@
             copy.wait()
         waited = needed
         image = image_ref[:, low * size : high * size]
-        for n, (_, start) in enumerate(outs):
-            which = [start + c for c in range(width)]
-            part = project(image, tiles_ref, slot_ref, range(low, high), which, lines)
-            sums[n] = part if sums[n] is None else sums[n] + part
-    for n, (out_ref, _) in enumerate(outs):
-        for c in range(width):
-            out_ref[c] = sums[n][:, c * size : (c + 1) * size].astype(out_ref.dtype)
+        part = project(image, tiles_ref, slot_ref, range(low, high), which, lines)
+        sums = part if sums is None else sums + part
+    for c in range(width):
+        forth_ref[c] = sums[:, c * size : (c + 1) * size].astype(forth_ref.dtype)
+        back_ref[c] = sums[:, (width + c) * size : (width + c + 1) * size].astype(back_ref.dtype)
 
 
 def own_kernel(

time: 23.6 us -> 23.6 us (level)
  no operation moved by 1% of the time
where the time goes in v12:
time: 23.6 us; the launch traced here: 23.4 us
  starting transfers between devices  9.54 us (40%)
  Pallas kernels  7.24 us (31%)
  waiting for transfers between devices  6.26 us (27%)
    ppermute x2, waiting for transfers between devices, body(): across = lax.ppermute(chip, 'angle', [(a, a ^ 3) for a in range(angles)])  3.9 us
    ppermute x2, starting transfers between devices, body(): across = lax.ppermute(chip, 'angle', [(a, a ^ 3) for a in range(angles)])  2.72 us
    ppermute x1, starting transfers between devices, body(): got_back = lax.ppermute(edge_back, both, back)  2.6 us
    pallas_call x1, Pallas kernels, body(): pl.pallas_call(functools.partial(edge_kernel, blocks, own, lines), out_sh...  2.23 us
    pallas_call x1, Pallas kernels, body(): pl.pallas_call(functools.partial(own_kernel, blocks, own, lines), out_sha...  2.21 us
    ppermute x1, starting transfers between devices, body(): beside_back = lax.ppermute(oblique, both, back)  2.07 us
    ppermute x1, waiting for transfers between devices, body(): beside_forth = lax.ppermute(oblique, both, forth)  1.64 us
    pallas_call x2, Pallas kernels, write_rows(): pl.pallas_call(functools.partial(write_rows_kernel, half_rows, places), o...  1.38 us
  transfers between devices with their start and end apart: 10, of which 6 were waited for; matrix products, arithmetic and copies ran while one was open for 1% of the time, Pallas kernels for 17%

profile of v12, /device:TPU:0, one launch (start us, length us, event | category | flops | bytes accessed | tf_op | source)
XLA Modules:
  0.0 23.4 jit_solution(5879743478925868208)
XLA Ops:
  0.0 0.0 copy-start.6
  0.0 0.0 copy-start.3
  0.0 2.2 %edge_partials.1 = (bf16[2,128,128]{2,1,0:T(8,128)(2,1)S(1)}, bf16[2,128,128]{2,1,0:T(8,128)(2,1)S(1)}, bf16[128,1536]{1,0:T(8,128)(2,1)S(1)}, bf16[86,128,128]{2,1,0:T(8,128)(2,1)S(1)}) custom-call(s32[86]{0:T(128)} %bitcast.10, s32[86]{0:T(128)} %bitcast.12, bf16[1536,128]{1,0:T(8,128)(2,1)} %activity_ref.1, bf16[86,128,128]{2,1,0:T(8,128)(2,1)} %bitcast.15), custom_call_target="tpu_custom_call" | custom-call | tf_op jit(solution)/shard_map/edge_partials/pallas_call | solution.py:244
  2.3 0.5 %collective-permute-start = (bf16[2,128,128]{2,1,0:T(8,128)(2,1)S(1)}, bf16[2,128,128]{2,1,0:T(8,128)(2,1)S(1)}, u32[]{:S(2)}, u32[]{:S(2)}) collective-permute-start(bf16[2,128,128]{2,1,0:T(8,128)(2,1)S(1)} %get-tuple-element.20), channel_id=1, source_target_pairs={{0,1},{1,5},{2,3},{3,7},{4,0},{5,9},{6,2},{7,11},{8,4},{9,13},{10,... | collective-permute-start | bytes 196616 | tf_op jit(solution)/shard_map/ppermute | solution.py:265
  2.8 2.6 %collective-permute-start.1 = (bf16[2,128,128]{2,1,0:T(8,128)(2,1)S(1)}, bf16[2,128,128]{2,1,0:T(8,128)(2,1)S(1)}, u32[]{:S(2)}, u32[]{:S(2)}) collective-permute-start(bf16[2,128,128]{2,1,0:T(8,128)(2,1)S(1)} %get-tuple-element.21), channel_id=1, source_target_pairs={{1,0},{5,1},{3,2},{7,3},{0,4},{9,5},{2,6},{11,7},{4,8},{13,9},{6,1... | collective-permute-start | bytes 196616 | tf_op jit(solution)/shard_map/ppermute | solution.py:266
  5.4 2.2 %own_partials.1 = (f32[2,128,128]{2,1,0:T(8,128)S(1)}, f32[2,128,128]{2,1,0:T(8,128)S(1)}, bf16[2,128,128]{2,1,0:T(8,128)(2,1)S(1)}, bf16[1536,1024]{1,0:T(8,128)(2,1)S(1)}, f32[768,128]{1,0:T(8,128)S(1)}) custom-call(s32[86]{0:T(128)S(1)} %bitcast.11, s32[86]{0:T(128)S(1)} %bitcast.13, s32[2]{0:T(128)S(1)} %bitcast.14, ...), custom_call_target="tpu_custom_call" | custom-call | tf_op jit(solution)/shard_map/own_partials/pallas_call | solution.py:268
  7.6 0.1 collective-permute-done.forth_ref
  7.7 0.0 collective-permute-done.1.back_ref
  7.7 0.1 oblique_ratios.1.oblique_ref
  7.9 0.4 %collective-permute-start.3 = (bf16[2,128,128]{2,1,0:T(8,128)(2,1)S(1)}, bf16[2,128,128]{2,1,0:T(8,128)(2,1)S(1)}, u32[]{:S(2)}, u32[]{:S(2)}) collective-permute-start(bf16[2,128,128]{2,1,0:T(8,128)(2,1)S(1)} %oblique_ratios.1.oblique_ref), channel_id=1, source_target_pairs={{0,1},{1,5},{2,3},{3,7},{4,0},{5,9},{6,2},{7,11},{8,4},{9,13},{10,... | collective-permute-start | bytes 196616 | tf_op jit(solution)/shard_map/ppermute | solution.py:294
  8.2 2.1 %collective-permute-start.2 = (bf16[2,128,128]{2,1,0:T(8,128)(2,1)S(1)}, bf16[2,128,128]{2,1,0:T(8,128)(2,1)S(1)}, u32[]{:S(2)}, u32[]{:S(2)}) collective-permute-start(bf16[2,128,128]{2,1,0:T(8,128)(2,1)S(1)} %oblique_ratios.1.oblique_ref), channel_id=1, source_target_pairs={{1,0},{5,1},{3,2},{7,3},{0,4},{9,5},{2,6},{11,7},{4,8},{13,9},{6,1... | collective-permute-start | bytes 196616 | tf_op jit(solution)/shard_map/ppermute | solution.py:295
  10.3 0.6 %own_back.1.own_ref = f32[1536,128]{1,0:T(8,128)S(1)} custom-call(bf16[1536,1024]{1,0:T(8,128)(2,1)S(1)} %get-tuple-element.19.matrix_ref, bf16[2,128,128]{2,1,0:T(8,128)(2,1)S(1)} %oblique_ratios.1.oblique_ref, bf16[2,128,128]{2,1,0:T(8,128)(2,1)S(1)} %get-tuple-element.24.ratio_ref), custom_call_target="tpu_custom_call" | custom-call | tf_op jit(solution)/shard_map/own_back/pallas_call | solution.py:296
  10.9 1.6 %collective-permute-done.3.forth_ref = bf16[2,128,128]{2,1,0:T(8,128)(2,1)S(1)} collective-permute-done((bf16[2,128,128]{2,1,0:T(8,128)(2,1)S(1)}, bf16[2,128,128]{2,1,0:T(8,128)(2,1)S(1)}, u32[]{:S(2)}, u32[]{:S(2)}) %collective-permute-start.3) | collective-permute-done | bytes 65568 | tf_op jit(solution)/shard_map/ppermute | solution.py:294
  12.5 0.0 collective-permute-done.2.back_ref
  12.5 0.3 %edge_back_first.1 = f32[336,128]{1,0:T(8,128)S(1)} custom-call(bf16[1536,1024]{1,0:T(8,128)(2,1)S(1)} %get-tuple-element.19.matrix_ref, bf16[2,128,128]{2,1,0:T(8,128)(2,1)S(1)} %collective-permute-done.2.back_ref, bf16[2,128,128]{2,1,0:T(8,128)(2,1)S(1)} %collective-permute-done.3.forth_ref, f32[1536,128]{1,0:T(8,128)S(1)} %own_back.1.own_ref), custom_call_target="tpu_custom_call" | custom-call | tf_op jit(solution)/shard_map/edge_back_first/pallas_call | solution.py:306
  12.8 0.8 %collective-permute-start.6 = (f16[336,128]{1,0:T(8,128)(2,1)S(1)}, f16[336,128]{1,0:T(8,128)(2,1)S(1)}, u32[]{:S(2)}, u32[]{:S(2)}) collective-permute-start(f16[336,128]{1,0:T(8,128)(2,1)S(1)} %multiply_convert_fusion.2), channel_id=1, source_target_pairs={{0,1},{1,0},{2,3},{3,2},{4,5},{5,4},{6,7},{7,6},{8,9},{9,8},{10,11... | collective-permute-start | bytes 258056 | tf_op jit(solution)/shard_map/ppermute | solution.py:338
  13.6 0.5 %edge_back_rest.1 = f32[1200,128]{1,0:T(8,128)S(1)} custom-call(bf16[1536,1024]{1,0:T(8,128)(2,1)S(1)} %get-tuple-element.19.matrix_ref, bf16[2,128,128]{2,1,0:T(8,128)(2,1)S(1)} %collective-permute-done.2.back_ref, bf16[2,128,128]{2,1,0:T(8,128)(2,1)S(1)} %collective-permute-done.3.forth_ref, f32[1536,128]{1,0:T(8,128)S(1)} %own_back.1.own_ref), custom_call_target="tpu_custom_call" | custom-call | tf_op jit(solution)/shard_map/edge_back_rest/pallas_call | solution.py:306
  14.1 0.1 collective-permute-start.4
  14.2 0.3 %collective-permute-done.6 = f16[336,128]{1,0:T(8,128)(2,1)S(1)} collective-permute-done((f16[336,128]{1,0:T(8,128)(2,1)S(1)}, f16[336,128]{1,0:T(8,128)(2,1)S(1)}, u32[]{:S(2)}, u32[]{:S(2)}) %collective-permute-start.6) | collective-permute-done | bytes 86048 | tf_op jit(solution)/shard_map/ppermute | solution.py:338
  14.5 1.8 %collective-permute-start.7 = (f16[336,128]{1,0:T(8,128)(2,1)S(1)}, f16[336,128]{1,0:T(8,128)(2,1)S(1)}, u32[]{:S(2)}, u32[]{:S(2)}) collective-permute-start(f16[336,128]{1,0:T(8,128)(2,1)S(1)} %fusion.4), channel_id=1, source_target_pairs={{0,3},{1,2},{2,1},{3,0},{4,7},{5,6},{6,5},{7,4},{8,11},{9,10},{10,... | collective-permute-start | bytes 258056 | tf_op jit(solution)/shard_map/ppermute | solution.py:349
  16.3 0.0 collective-permute-done.4
  16.3 0.1 fusion.2
  16.4 0.9 %collective-permute-start.5 = (f16[432,128]{1,0:T(8,128)(2,1)S(1)}, f16[432,128]{1,0:T(8,128)(2,1)S(1)}, u32[]{:S(2)}, u32[]{:S(2)}) collective-permute-start(f16[432,128]{1,0:T(8,128)(2,1)S(1)} %fusion.2), channel_id=1, source_target_pairs={{0,3},{1,2},{2,1},{3,0},{4,7},{5,6},{6,5},{7,4},{8,11},{9,10},{10,... | collective-permute-start | bytes 331784 | tf_op jit(solution)/shard_map/ppermute | solution.py:349
  17.3 1.9 %collective-permute-done.7 = f16[336,128]{1,0:T(8,128)(2,1)S(1)} collective-permute-done((f16[336,128]{1,0:T(8,128)(2,1)S(1)}, f16[336,128]{1,0:T(8,128)(2,1)S(1)}, u32[]{:S(2)}, u32[]{:S(2)}) %collective-permute-start.7) | collective-permute-done | bytes 86048 | tf_op jit(solution)/shard_map/ppermute | solution.py:349
  19.3 0.1 collective-permute-start.8
  19.4 2.0 %collective-permute-done.5 = f16[432,128]{1,0:T(8,128)(2,1)S(1)} collective-permute-done((f16[432,128]{1,0:T(8,128)(2,1)S(1)}, f16[432,128]{1,0:T(8,128)(2,1)S(1)}, u32[]{:S(2)}, u32[]{:S(2)}) %collective-permute-start.5) | collective-permute-done | bytes 110624 | tf_op jit(solution)/shard_map/ppermute | solution.py:349
  21.3 0.0 collective-permute-done.8.refs_1_
  21.3 0.1 multiply_convert_fusion.refs_2_
  21.4 0.4 %collective-permute-start.9 = (bf16[432,128]{1,0:T(8,128)(2,1)S(1)}, bf16[432,128]{1,0:T(8,128)(2,1)S(1)}, u32[]{:S(2)}, u32[]{:S(2)}) collective-permute-start(bf16[432,128]{1,0:T(8,128)(2,1)S(1)} %multiply_convert_fusion.refs_2_), channel_id=1, source_target_pairs={{0,1},{1,0},{2,3},{3,2},{4,5},{5,4},{6,7},{7,6},{8,9},{9,8},{10,11... | collective-permute-start | bytes 331784 | tf_op jit(solution)/shard_map/ppermute | solution.py:359
  21.8 0.7 %write_first.1.refs_1_ = bf16[1536,128]{1,0:T(8,128)(2,1)} custom-call(bf16[336,128]{1,0:T(8,128)(2,1)S(1)} %multiply_convert_fusion.1.refs_0_, bf16[336,128]{1,0:T(8,128)(2,1)S(1)} %collective-permute-done.8.refs_1_, bf16[432,128]{1,0:T(8,128)(2,1)S(1)} %multiply_convert_fusion.refs_2_), custom_call_target="tpu_custom_call" | custom-call | tf_op jit(solution)/shard_map/write_first/pallas_call | solution.py:322
  22.5 0.3 %collective-permute-done.9.refs_0_ = bf16[432,128]{1,0:T(8,128)(2,1)S(1)} collective-permute-done((bf16[432,128]{1,0:T(8,128)(2,1)S(1)}, bf16[432,128]{1,0:T(8,128)(2,1)S(1)}, u32[]{:S(2)}, u32[]{:S(2)}) %collective-permute-start.9) | collective-permute-done | bytes 110624 | tf_op jit(solution)/shard_map/ppermute | solution.py:359
  22.8 0.7 %write_last.1 = bf16[1536,128]{1,0:T(8,128)(2,1)} custom-call(bf16[432,128]{1,0:T(8,128)(2,1)S(1)} %collective-permute-done.9.refs_0_, bf16[1536,128]{1,0:T(8,128)(2,1)} %write_first.1.refs_1_), custom_call_target="tpu_custom_call", output_to_operand_aliasing={{}: (1, {})} | custom-call | tf_op jit(solution)/shard_map/write_last/pallas_call | solution.py:322
  (16 shorter events, 0.2 us)
Async XLA Ops:
  0.0 5.4 %copy-start = (bf16[1536,128]{1,0:T(8,128)(2,1)S(1)}, bf16[1536,128]{1,0:T(8,128)(2,1)}, u32[]{:S(2)}) copy-start(bf16[1536,128]{1,0:T(8,128)(2,1)} %activity_ref.1) | copy-start | bytes 1179652
  0.0 5.4 %copy-start.5 = (s32[1,1,86]{2,1,0:T(1,128)S(1)}, s32[1,1,86]{2,1,0:T(1,128)}, u32[]{:S(2)}) copy-start(s32[1,1,86]{2,1,0:T(1,128)} %param.12) | copy-start | bytes 1036
  0.0 5.4 %copy-start.4 = (s32[1,1,86]{2,1,0:T(1,128)S(1)}, s32[1,1,86]{2,1,0:T(1,128)}, u32[]{:S(2)}) copy-start(s32[1,1,86]{2,1,0:T(1,128)} %param.11) | copy-start | bytes 1036
  0.0 5.4 %copy-start.2 = (bf16[1,1,512,128]{3,2,1,0:T(8,128)(2,1)S(1)}, bf16[1,1,512,128]{3,2,1,0:T(8,128)(2,1)}, u32[]{:S(2)}) copy-start(bf16[1,1,512,128]{3,2,1,0:T(8,128)(2,1)} %param.15) | copy-start | bytes 393220
  0.0 5.4 %copy-start.1 = (s32[1,1,512,128]{3,2,1,0:T(8,128)S(1)}, s32[1,1,512,128]{3,2,1,0:T(8,128)}, u32[]{:S(2)}) copy-start(s32[1,1,512,128]{3,2,1,0:T(8,128)} %param.14) | copy-start | bytes 786436
  0.0 5.4 %copy-start.6 = (s32[1,1,2]{2,1,0:T(1,128)S(1)}, s32[1,1,2]{2,1,0:T(1,128)}, u32[]{:S(2)}) copy-start(s32[1,1,2]{2,1,0:T(1,128)} %param.13) | copy-start | bytes 28
  0.0 5.4 %copy-start.3 = (f32[1536]{0:T(1024)S(1)}, f32[1536]{0:T(1024)}, u32[]{:S(2)}) copy-start(f32[1536]{0:T(1024)} %param.9) | copy-start | bytes 18436
  2.3 5.5 %collective-permute-start = (bf16[2,128,128]{2,1,0:T(8,128)(2,1)S(1)}, bf16[2,128,128]{2,1,0:T(8,128)(2,1)S(1)}, u32[]{:S(2)}, u32[]{:S(2)}) collective-permute-start(bf16[2,128,128]{2,1,0:T(8,128)(2,1)S(1)} %get-tuple-element.20), channel_id=1, source_target_pairs={{0,1},{1,5},{2,3},{3,7},{4,0},{5,9},{6,2},{7,11},{8,4},{9,13},{10,... | collective-permute-start | bytes 196616 | tf_op jit(solution)/shard_map/ppermute | solution.py:265
  2.8 5.0 %collective-permute-start.1 = (bf16[2,128,128]{2,1,0:T(8,128)(2,1)S(1)}, bf16[2,128,128]{2,1,0:T(8,128)(2,1)S(1)}, u32[]{:S(2)}, u32[]{:S(2)}) collective-permute-start(bf16[2,128,128]{2,1,0:T(8,128)(2,1)S(1)} %get-tuple-element.21), channel_id=1, source_target_pairs={{1,0},{5,1},{3,2},{7,3},{0,4},{9,5},{2,6},{11,7},{4,8},{13,9},{6,1... | collective-permute-start | bytes 196616 | tf_op jit(solution)/shard_map/ppermute | solution.py:266
  7.9 4.7 %collective-permute-start.3 = (bf16[2,128,128]{2,1,0:T(8,128)(2,1)S(1)}, bf16[2,128,128]{2,1,0:T(8,128)(2,1)S(1)}, u32[]{:S(2)}, u32[]{:S(2)}) collective-permute-start(bf16[2,128,128]{2,1,0:T(8,128)(2,1)S(1)} %oblique_ratios.1.oblique_ref), channel_id=1, source_target_pairs={{0,1},{1,5},{2,3},{3,7},{4,0},{5,9},{6,2},{7,11},{8,4},{9,13},{10,... | collective-permute-start | bytes 196616 | tf_op jit(solution)/shard_map/ppermute | solution.py:294
  8.2 4.3 %collective-permute-start.2 = (bf16[2,128,128]{2,1,0:T(8,128)(2,1)S(1)}, bf16[2,128,128]{2,1,0:T(8,128)(2,1)S(1)}, u32[]{:S(2)}, u32[]{:S(2)}) collective-permute-start(bf16[2,128,128]{2,1,0:T(8,128)(2,1)S(1)} %oblique_ratios.1.oblique_ref), channel_id=1, source_target_pairs={{1,0},{5,1},{3,2},{7,3},{0,4},{9,5},{2,6},{11,7},{4,8},{13,9},{6,1... | collective-permute-start | bytes 196616 | tf_op jit(solution)/shard_map/ppermute | solution.py:295
  12.8 1.7 %collective-permute-start.6 = (f16[336,128]{1,0:T(8,128)(2,1)S(1)}, f16[336,128]{1,0:T(8,128)(2,1)S(1)}, u32[]{:S(2)}, u32[]{:S(2)}) collective-permute-start(f16[336,128]{1,0:T(8,128)(2,1)S(1)} %multiply_convert_fusion.2), channel_id=1, source_target_pairs={{0,1},{1,0},{2,3},{3,2},{4,5},{5,4},{6,7},{7,6},{8,9},{9,8},{10,11... | collective-permute-start | bytes 258056 | tf_op jit(solution)/shard_map/ppermute | solution.py:338
  14.1 2.2 %collective-permute-start.4 = (f16[432,128]{1,0:T(8,128)(2,1)S(1)}, f16[432,128]{1,0:T(8,128)(2,1)S(1)}, u32[]{:S(2)}, u32[]{:S(2)}) collective-permute-start(f16[432,128]{1,0:T(8,128)(2,1)S(1)} %fusion), channel_id=1, source_target_pairs={{0,1},{1,0},{2,3},{3,2},{4,5},{5,4},{6,7},{7,6},{8,9},{9,8},{10,11... | collective-permute-start | bytes 331784 | tf_op jit(solution)/shard_map/ppermute | solution.py:341
  14.5 4.7 %collective-permute-start.7 = (f16[336,128]{1,0:T(8,128)(2,1)S(1)}, f16[336,128]{1,0:T(8,128)(2,1)S(1)}, u32[]{:S(2)}, u32[]{:S(2)}) collective-permute-start(f16[336,128]{1,0:T(8,128)(2,1)S(1)} %fusion.4), channel_id=1, source_target_pairs={{0,3},{1,2},{2,1},{3,0},{4,7},{5,6},{6,5},{7,4},{8,11},{9,10},{10,... | collective-permute-start | bytes 258056 | tf_op jit(solution)/shard_map/ppermute | solution.py:349
  16.4 5.0 %collective-permute-start.5 = (f16[432,128]{1,0:T(8,128)(2,1)S(1)}, f16[432,128]{1,0:T(8,128)(2,1)S(1)}, u32[]{:S(2)}, u32[]{:S(2)}) collective-permute-start(f16[432,128]{1,0:T(8,128)(2,1)S(1)} %fusion.2), channel_id=1, source_target_pairs={{0,3},{1,2},{2,1},{3,0},{4,7},{5,6},{6,5},{7,4},{8,11},{9,10},{10,... | collective-permute-start | bytes 331784 | tf_op jit(solution)/shard_map/ppermute | solution.py:349
  19.3 2.0 %collective-permute-start.8 = (bf16[336,128]{1,0:T(8,128)(2,1)S(1)}, bf16[336,128]{1,0:T(8,128)(2,1)S(1)}, u32[]{:S(2)}, u32[]{:S(2)}) collective-permute-start(bf16[336,128]{1,0:T(8,128)(2,1)S(1)} %multiply_convert_fusion.1.refs_0_), channel_id=1, source_target_pairs={{0,1},{1,0},{2,3},{3,2},{4,5},{5,4},{6,7},{7,6},{8,9},{9,8},{10,11... | collective-permute-start | bytes 258056 | tf_op jit(solution)/shard_map/ppermute | solution.py:359
  21.4 1.4 %collective-permute-start.9 = (bf16[432,128]{1,0:T(8,128)(2,1)S(1)}, bf16[432,128]{1,0:T(8,128)(2,1)S(1)}, u32[]{:S(2)}, u32[]{:S(2)}) collective-permute-start(bf16[432,128]{1,0:T(8,128)(2,1)S(1)} %multiply_convert_fusion.refs_2_), channel_id=1, source_target_pairs={{0,1},{1,0},{2,3},{3,2},{4,5},{5,4},{6,7},{7,6},{8,9},{9,8},{10,11... | collective-permute-start | bytes 331784 | tf_op jit(solution)/shard_map/ppermute | solution.py:359
